TPU v7x, 32 devices: a whole 2x2x4 slice. The times are simulated.
32 devices in a mesh: row: 4 (over y, x), col: 8 (over z, core).
Axes of the slice: x: 2, y: 2, z: 4, core: 2. Of those that a mesh axis runs over, the one named last changes fastest.
Arguments:
- preference: bfloat16 [8192, 16384], P('col', 'row'), may hold values from -6 to 6
- users: float32 [64, 16384], P(None, 'row'), may hold values from -2 to 2
- items: float32 [64, 8192], P(None, ('col', 'row')), may hold values from -2 to 2
Outputs:
- new_users: float32 [64, 16384], P(None, 'row')
- new_items: float32 [64, 8192], P(None, ('col', 'row'))
All inputs are finite; a program needn't handle non-finite values.
Results may differ from a plain program's by a relative error of at most 0.0051.
Values may be sent and summed in bfloat16 or wider, within the bound.
No kernel may reach another device: no remote copies, remote signals or barrier semaphores. Data moves between devices by JAX's collectives and lax.ppermute only.
A program may use at most 64 MiB of HBM per device.

v0:
```python
import math

import jax
import jax.numpy as jnp
from jax import lax
from jax.sharding import PartitionSpec as P

ITERS = 2


step_scale = 1.0


def from_behind(block, axis, distance):
    devices = range(lax.axis_size(axis))
    route = [((i - distance) % len(devices), i) for i in devices]
    return lax.ppermute(block, axis, route)


def residual_of(labels_block, scores):
    weights = labels_block.astype(jnp.float32)
    return (jnp.abs(weights) * jax.nn.sigmoid(scores) - jnp.maximum(weights, 0.0)).astype(
        jnp.bfloat16
    )


def body(preference, users, items):
    rows_count = lax.axis_size("row")
    cols_count = lax.axis_size("col")
    items_dev, users_dev = preference.shape
    rank_dim = users.shape[0]
    block_cols = items.shape[1]
    user_rate = step_scale / math.sqrt(items_dev * cols_count)
    item_rate = step_scale / math.sqrt(users_dev * rows_count)
    share_cols = users_dev // cols_count
    for iteration in range(ITERS):
        user_b = users.astype(jnp.bfloat16)
        item_b = items.astype(jnp.bfloat16)
        own_index = lax.axis_index("row")
        visitor = item_b
        carried = jnp.zeros((rank_dim, block_cols), jnp.float32)
        grad_user = jnp.zeros((rank_dim, users_dev), jnp.float32)
        for rotation in range(rows_count):
            anchor = (own_index - rotation) % rows_count
            labels_block = lax.dynamic_slice_in_dim(preference, anchor * block_cols, block_cols, 0)
            scores = jnp.einsum("kn,km->nm", visitor, user_b, preferred_element_type=jnp.float32)
            residual = residual_of(labels_block, scores)
            grad_user = grad_user + jnp.einsum(
                "kn,nm->km", visitor, residual, preferred_element_type=jnp.float32
            )
            carried = carried + jnp.einsum(
                "km,nm->kn", user_b, residual, preferred_element_type=jnp.float32
            )
            if rotation + 1 < rows_count:
                visitor = from_behind(visitor, "row", 1)
            carried = from_behind(carried, "row", 1)
        user_share = lax.psum_scatter(grad_user, "col", scatter_dimension=1, tiled=True)
        own_users = lax.dynamic_slice_in_dim(
            users, lax.axis_index("col") * share_cols, share_cols, 1
        )
        users = lax.all_gather(own_users - user_rate * user_share, "col", axis=1, tiled=True)
        items = items - item_rate * carried
    return (users, items)


def solution(mesh):
    return jax.shard_map(
        body,
        mesh=mesh,
        in_specs=(P("col", "row"), P(None, "row"), P(None, ("col", "row"))),
        out_specs=(P(None, "row"), P(None, ("col", "row"))),
        check_vma=False,
    )
```

profile of v0, /device:TPU:0, one launch (start us, length us, event | category | flops | bytes accessed | tf_op | source)
XLA Modules:
  0.0 182.7 jit_solution(5103849584762460562)
XLA Ops:
  7.2 0.8 convert_element_type.53
  8.1 2.9 %collective-permute-start = (bf16[64,256]{1,0:T(8,128)(2,1)S(1)}, bf16[64,256]{1,0:T(8,128)(2,1)S(1)}, u32[]{:S(2)}, u32[]{:S(2)}) collective-permute-start(bf16[64,256]{1,0:T(8,128)(2,1)S(1)} %convert_element_type.53), channel_id=1, source_target_pairs={{24,0},{0,8},{8,16},{16,24},{25,1},{1,9},{9,17},{17,25},{26,2},{2,... | collective-permute-start | bytes 98312 | tf_op jit(solution)/shard_map/ppermute | solution.py:17
  11.0 1.3 convert_element_type.54
  12.3 3.2 %fusion.33 = bf16[256,4096]{1,0:T(8,128)(2,1)S(1)} fusion(bf16[64,256]{1,0:T(8,128)(2,1)S(1)} %convert_element_type.53, bf16[64,4096]{1,0:T(8,128)(2,1)S(1)} %convert_element_type.54, bf16[1024,4096]{1,0:T(8,128)(2,1)} %param.3, s32[]{:T(128)S(6)} %select_n.49), kind=kOutput, calls=%fused_computation.49 | convolution fusion | flops 143654912 | bytes 4751364 | tf_op jit(solution)/shard_map/kn,km->nm/dot_general | solution.py:46
  15.5 1.5 fusion.55
  16.9 1.5 collective-permute-start.1
  18.5 3.2 %fusion.35 = bf16[256,4096]{1,0:T(8,128)(2,1)S(1)} fusion(bf16[64,256]{1,0:T(8,128)(2,1)S(1)} %collective-permute-done, bf16[64,4096]{1,0:T(8,128)(2,1)S(1)} %convert_element_type.54, bf16[1024,4096]{1,0:T(8,128)(2,1)} %param.3, s32[]{:T(128)S(6)} %select_n.51), kind=kOutput, calls=%fused_computation.51 | convolution fusion | flops 143654912 | bytes 4751364 | tf_op jit(solution)/shard_map/kn,km->nm/dot_general | solution.py:46
  22.2 1.5 collective-permute-start.2
  23.7 3.2 %fusion.37 = bf16[256,4096]{1,0:T(8,128)(2,1)S(1)} fusion(bf16[64,256]{1,0:T(8,128)(2,1)S(1)} %collective-permute-done.1, bf16[64,4096]{1,0:T(8,128)(2,1)S(1)} %convert_element_type.54, bf16[1024,4096]{1,0:T(8,128)(2,1)} %param.3, s32[]{:T(128)S(6)} %select_n.53), kind=kOutput, calls=%fused_computation.53 | convolution fusion | flops 143654912 | bytes 4751364 | tf_op jit(solution)/shard_map/kn,km->nm/dot_general | solution.py:46
  27.4 3.4 %fusion.39 = bf16[256,4096]{1,0:T(8,128)(2,1)S(1)} fusion(bf16[64,256]{1,0:T(8,128)(2,1)S(1)} %collective-permute-done.2, bf16[64,4096]{1,0:T(8,128)(2,1)S(1)} %convert_element_type.54, bf16[1024,4096]{1,0:T(8,128)(2,1)} %param.3, s32[]{:T(128)S(6)} %select_n.55), kind=kOutput, calls=%fused_computation.55 | convolution fusion | flops 143654912 | bytes 4751364 | tf_op jit(solution)/shard_map/kn,km->nm/dot_general | solution.py:46
  30.9 1.4 copy-done
  32.3 1.5 fusion.48
  33.8 32.6 %reduce-scatter.3.cloned.1.call-done = f32[64,512]{1,0:T(8,128)} async-done(((f32[64,4096]{1,0:T(8,128)}), f32[64,512]{1,0:T(8,128)}) %reduce-scatter.3.cloned.1.call-update) | async-done | bytes 131088 | tf_op jit(solution)/shard_map/reduce_scatter | solution.py:57
  66.3 1.6 multiply_subtract_fusion.1
  68.1 0.8 convolution_bitcast_fusion.3
  68.8 1.6 collective-permute-start.3
  70.4 3.6 %collective-permute-done.3 = f32[64,256]{1,0:T(8,128)S(1)} collective-permute-done((f32[64,256]{1,0:T(8,128)S(1)}, f32[64,256]{1,0:T(8,128)S(1)}, u32[]{:S(2)}, u32[]{:S(2)}) %collective-permute-start.3) | collective-permute-done | bytes 65568 | tf_op jit(solution)/shard_map/ppermute | solution.py:17
  74.1 2.4 %fusion.49 = f32[64,256]{1,0:T(8,128)S(1)} fusion(f32[64,256]{1,0:T(8,128)S(1)} %collective-permute-done.3, bf16[256,4096]{1,0:T(8,128)(2,1)} %copy-done.2, bf16[64,4096]{1,0:T(8,128)(2,1)S(1)} %convert_element_type.54), kind=kOutput, calls=%fused_computation.75 | convolution fusion | flops 134234112 | bytes 2752512 | tf_op jit(solution)/shard_map/km,nm->kn/dot_general | solution.py:51
  76.5 0.6 collective-permute-start.4
  77.1 0.8 convolution_bitcast_fusion.1
  77.9 3.8 %collective-permute-done.4 = f32[64,256]{1,0:T(8,128)S(1)} collective-permute-done((f32[64,256]{1,0:T(8,128)S(1)}, f32[64,256]{1,0:T(8,128)S(1)}, u32[]{:S(2)}, u32[]{:S(2)}) %collective-permute-start.4) | collective-permute-done | bytes 65568 | tf_op jit(solution)/shard_map/ppermute | solution.py:17
  81.8 0.8 convolution_bitcast_fusion
  82.6 4.4 %collective-permute-done.5 = f32[64,256]{1,0:T(8,128)S(1)} collective-permute-done((f32[64,256]{1,0:T(8,128)S(1)}, f32[64,256]{1,0:T(8,128)S(1)}, u32[]{:S(2)}, u32[]{:S(2)}) %collective-permute-start.5) | collective-permute-done | bytes 65568 | tf_op jit(solution)/shard_map/ppermute | solution.py:17
  87.0 5.2 %collective-permute-done.6 = f32[64,256]{1,0:T(8,128)S(1)} collective-permute-done((f32[64,256]{1,0:T(8,128)S(1)}, f32[64,256]{1,0:T(8,128)S(1)}, u32[]{:S(2)}, u32[]{:S(2)}) %collective-permute-start.6) | collective-permute-done | bytes 65568 | tf_op jit(solution)/shard_map/ppermute | solution.py:17
  92.3 4.8 %collective-permute-done.7 = bf16[64,256]{1,0:T(8,128)(2,1)S(1)} collective-permute-done((bf16[64,256]{1,0:T(8,128)(2,1)S(1)}, bf16[64,256]{1,0:T(8,128)(2,1)S(1)}, u32[]{:S(2)}, u32[]{:S(2)}) %collective-permute-start.7) | collective-permute-done | bytes 32800 | tf_op jit(solution)/shard_map/ppermute | solution.py:17
  97.1 4.8 %collective-permute-done.8 = bf16[64,256]{1,0:T(8,128)(2,1)S(1)} collective-permute-done((bf16[64,256]{1,0:T(8,128)(2,1)S(1)}, bf16[64,256]{1,0:T(8,128)(2,1)S(1)}, u32[]{:S(2)}, u32[]{:S(2)}) %collective-permute-start.8) | collective-permute-done | bytes 32800 | tf_op jit(solution)/shard_map/ppermute | solution.py:17
  101.9 1.4 convert_element_type.63
  103.3 3.4 %fusion.41 = bf16[256,4096]{1,0:T(8,128)(2,1)S(1)} fusion(bf16[64,256]{1,0:T(8,128)(2,1)S(1)} %fusion.50, bf16[64,4096]{1,0:T(8,128)(2,1)S(1)} %convert_element_type.63, bf16[1024,4096]{1,0:T(8,128)(2,1)} %param.3, s32[]{:T(128)S(6)} %select_n.49), kind=kOutput, calls=%fused_computation.57 | convolution fusion | flops 143654912 | bytes 4751364 | tf_op jit(solution)/shard_map/kn,km->nm/dot_general | solution.py:46
  106.7 1.6 fusion.45
  108.4 1.6 fusion.43
  110.5 0.5 convolution_add_fusion.5
  111.0 1.6 fusion.47
  112.7 0.5 convolution_add_fusion.4
  113.1 1.5 convolution_add_fusion.3
  114.7 31.1 %reduce-scatter.5.cloned.1.call-done = f32[64,512]{1,0:T(8,128)} async-done(((f32[64,4096]{1,0:T(8,128)}), f32[64,512]{1,0:T(8,128)}) %reduce-scatter.5.cloned.1.call-update) | async-done | bytes 131088 | tf_op jit(solution)/shard_map/reduce_scatter | solution.py:57
  145.8 1.6 multiply_subtract_fusion
  147.5 2.5 %fusion.52 = f32[64,256]{1,0:T(8,128)S(1)} fusion(bf16[64,4096]{1,0:T(8,128)(2,1)S(1)} %convert_element_type.63, bf16[256,4096]{1,0:T(8,128)(2,1)} %copy-done.8), kind=kOutput, calls=%fused_computation.83 | convolution fusion | flops 134217728 | bytes 2686976 | tf_op jit(solution)/shard_map/km,nm->kn/dot_general | solution.py:51
  150.0 1.5 collective-permute-start.10
  151.5 3.7 %collective-permute-done.10 = f32[64,256]{1,0:T(8,128)S(1)} collective-permute-done((f32[64,256]{1,0:T(8,128)S(1)}, f32[64,256]{1,0:T(8,128)S(1)}, u32[]{:S(2)}, u32[]{:S(2)}) %collective-permute-start.10) | collective-permute-done | bytes 65568 | tf_op jit(solution)/shard_map/ppermute | solution.py:17
  155.2 2.4 %convolution_add_fusion.6 = f32[64,256]{1,0:T(8,128)S(1)} fusion(f32[64,256]{1,0:T(8,128)S(1)} %collective-permute-done.10, bf16[64,4096]{1,0:T(8,128)(2,1)S(1)} %convert_element_type.63, bf16[256,4096]{1,0:T(8,128)(2,1)} %copy-done.7), kind=kOutput, calls=%fused_computation.76 | convolution fusion | flops 134234112 | bytes 2752512 | tf_op jit(solution)/shard_map/km,nm->kn/dot_general | solution.py:51
  157.6 0.6 collective-permute-start.11
  158.2 0.8 fusion.53
  158.9 3.9 %collective-permute-done.11 = f32[64,256]{1,0:T(8,128)S(1)} collective-permute-done((f32[64,256]{1,0:T(8,128)S(1)}, f32[64,256]{1,0:T(8,128)S(1)}, u32[]{:S(2)}, u32[]{:S(2)}) %collective-permute-start.11) | collective-permute-done | bytes 65568 | tf_op jit(solution)/shard_map/ppermute | solution.py:17
  162.9 0.8 fusion.54
  163.6 4.4 %collective-permute-done.12 = f32[64,256]{1,0:T(8,128)S(1)} collective-permute-done((f32[64,256]{1,0:T(8,128)S(1)}, f32[64,256]{1,0:T(8,128)S(1)}, u32[]{:S(2)}, u32[]{:S(2)}) %collective-permute-start.12) | collective-permute-done | bytes 65568 | tf_op jit(solution)/shard_map/ppermute | solution.py:17
  168.1 5.2 %collective-permute-done.13 = f32[64,256]{1,0:T(8,128)S(1)} collective-permute-done((f32[64,256]{1,0:T(8,128)S(1)}, f32[64,256]{1,0:T(8,128)S(1)}, u32[]{:S(2)}, u32[]{:S(2)}) %collective-permute-start.13) | collective-permute-done | bytes 65568 | tf_op jit(solution)/shard_map/ppermute | solution.py:17
  173.2 0.6 multiply_subtract_fusion.2
  173.9 2.3 %copy.6 = f32[64,4096]{1,0:T(8,128)} copy(f32[64,4096]{1,0:T(8,128)} %all-gather.5.cloned.1.call-done) | data formatting | bytes 2097152
  (55 shorter events, 2.1 us)
Async XLA Ops:
  7.2 59.2 %reduce-scatter.3.cloned.1.call-start = ((), (), s32[]{:S(2)}) async-start(), calls=%async_computation.2 | async-start | bytes 1179648 | tf_op jit(solution)/shard_map/reduce_scatter | solution.py:57
  8.1 8.9 %collective-permute-start = (bf16[64,256]{1,0:T(8,128)(2,1)S(1)}, bf16[64,256]{1,0:T(8,128)(2,1)S(1)}, u32[]{:S(2)}, u32[]{:S(2)}) collective-permute-start(bf16[64,256]{1,0:T(8,128)(2,1)S(1)} %convert_element_type.53), channel_id=1, source_target_pairs={{24,0},{0,8},{8,16},{16,24},{25,1},{1,9},{9,17},{17,25},{26,2},{2,... | collective-permute-start | bytes 98312 | tf_op jit(solution)/shard_map/ppermute | solution.py:17
  16.9 4.7 %copy-start.9 = (f32[4096,64]{0,1:T(8,128)S(1)}, f32[4096,64]{0,1:T(8,128)}, u32[]{:S(2)}) copy-start(f32[4096,64]{0,1:T(8,128)} %fusion.55) | copy-start | bytes 3145732
  16.9 5.2 %collective-permute-start.1 = (bf16[64,256]{1,0:T(8,128)(2,1)S(1)}, bf16[64,256]{1,0:T(8,128)(2,1)S(1)}, u32[]{:S(2)}, u32[]{:S(2)}) collective-permute-start(bf16[64,256]{1,0:T(8,128)(2,1)S(1)} %collective-permute-done), channel_id=1, source_target_pairs={{24,0},{0,8},{8,16},{16,24},{25,1},{1,9},{9,17},{17,25},{26,2},{2,... | collective-permute-start | bytes 98312 | tf_op jit(solution)/shard_map/ppermute | solution.py:17
  21.7 5.3 %copy-start.2 = (bf16[256,4096]{1,0:T(8,128)(2,1)}, bf16[256,4096]{1,0:T(8,128)(2,1)S(1)}, u32[]{:S(2)}) copy-start(bf16[256,4096]{1,0:T(8,128)(2,1)S(1)} %fusion.35) | copy-start | bytes 6291460
  22.2 5.3 %collective-permute-start.2 = (bf16[64,256]{1,0:T(8,128)(2,1)S(1)}, bf16[64,256]{1,0:T(8,128)(2,1)S(1)}, u32[]{:S(2)}, u32[]{:S(2)}) collective-permute-start(bf16[64,256]{1,0:T(8,128)(2,1)S(1)} %collective-permute-done.1), channel_id=1, source_target_pairs={{24,0},{0,8},{8,16},{16,24},{25,1},{1,9},{9,17},{17,25},{26,2},{2,... | collective-permute-start | bytes 98312 | tf_op jit(solution)/shard_map/ppermute | solution.py:17
  26.9 3.9 %copy-start.3 = (bf16[256,4096]{1,0:T(8,128)(2,1)}, bf16[256,4096]{1,0:T(8,128)(2,1)S(1)}, u32[]{:S(2)}) copy-start(bf16[256,4096]{1,0:T(8,128)(2,1)S(1)} %fusion.37) | copy-start | bytes 6291460
  30.9 1.4 copy-start
  33.7 68.1 %all-gather.3.cloned.1.call-start = ((), (), s32[]{:S(2)}) async-start(), calls=%async_computation.3 | async-start | bytes 1179648 | tf_op jit(solution)/shard_map/all_gather | solution.py:61
  68.0 77.8 %reduce-scatter.5.cloned.1.call-start = ((), (), s32[]{:S(2)}) async-start(), calls=%async_computation.4 | async-start | bytes 1179648 | tf_op jit(solution)/shard_map/reduce_scatter | solution.py:57
  68.1 9.1 %copy-start.4 = (bf16[256,4096]{1,0:T(8,128)(2,1)S(1)}, bf16[256,4096]{1,0:T(8,128)(2,1)}, u32[]{:S(2)}) copy-start(bf16[256,4096]{1,0:T(8,128)(2,1)} %copy-done.3) | copy-start | bytes 6291460
  68.1 13.7 %copy-start.1 = (bf16[256,4096]{1,0:T(8,128)(2,1)S(1)}, bf16[256,4096]{1,0:T(8,128)(2,1)}, u32[]{:S(2)}) copy-start(bf16[256,4096]{1,0:T(8,128)(2,1)} %copy-done) | copy-start | bytes 6291460
  68.8 23.3 %copy-start.10 = (f32[64,256]{1,0:T(8,128)S(1)}, f32[64,256]{1,0:T(8,128)}, u32[]{:S(2)}) copy-start(f32[64,256]{1,0:T(8,128)} %param.5) | copy-start | bytes 196612
  68.8 5.2 %collective-permute-start.3 = (f32[64,256]{1,0:T(8,128)S(1)}, f32[64,256]{1,0:T(8,128)S(1)}, u32[]{:S(2)}, u32[]{:S(2)}) collective-permute-start(f32[64,256]{1,0:T(8,128)S(1)} %convolution_bitcast_fusion.3), channel_id=1, source_target_pairs={{24,0},{0,8},{8,16},{16,24},{25,1},{1,9},{9,17},{17,25},{26,2},{2,... | collective-permute-start | bytes 196616 | tf_op jit(solution)/shard_map/ppermute | solution.py:17
  76.5 5.2 %collective-permute-start.4 = (f32[64,256]{1,0:T(8,128)S(1)}, f32[64,256]{1,0:T(8,128)S(1)}, u32[]{:S(2)}, u32[]{:S(2)}) collective-permute-start(f32[64,256]{1,0:T(8,128)S(1)} %fusion.49), channel_id=1, source_target_pairs={{24,0},{0,8},{8,16},{16,24},{25,1},{1,9},{9,17},{17,25},{26,2},{2,... | collective-permute-start | bytes 196616 | tf_op jit(solution)/shard_map/ppermute | solution.py:17
  81.7 5.2 %collective-permute-start.5 = (f32[64,256]{1,0:T(8,128)S(1)}, f32[64,256]{1,0:T(8,128)S(1)}, u32[]{:S(2)}, u32[]{:S(2)}) collective-permute-start(f32[64,256]{1,0:T(8,128)S(1)} %add.127), channel_id=1, source_target_pairs={{24,0},{0,8},{8,16},{16,24},{25,1},{1,9},{9,17},{17,25},{26,2},{2,... | collective-permute-start | bytes 196616 | tf_op jit(solution)/shard_map/ppermute | solution.py:17
  87.0 5.2 %collective-permute-start.6 = (f32[64,256]{1,0:T(8,128)S(1)}, f32[64,256]{1,0:T(8,128)S(1)}, u32[]{:S(2)}, u32[]{:S(2)}) collective-permute-start(f32[64,256]{1,0:T(8,128)S(1)} %add.128), channel_id=1, source_target_pairs={{24,0},{0,8},{8,16},{16,24},{25,1},{1,9},{9,17},{17,25},{26,2},{2,... | collective-permute-start | bytes 196616 | tf_op jit(solution)/shard_map/ppermute | solution.py:17
  92.2 4.9 %collective-permute-start.7 = (bf16[64,256]{1,0:T(8,128)(2,1)S(1)}, bf16[64,256]{1,0:T(8,128)(2,1)S(1)}, u32[]{:S(2)}, u32[]{:S(2)}) collective-permute-start(bf16[64,256]{1,0:T(8,128)(2,1)S(1)} %fusion.50), channel_id=1, source_target_pairs={{24,0},{0,8},{8,16},{16,24},{25,1},{1,9},{9,17},{17,25},{26,2},{2,... | collective-permute-start | bytes 98312 | tf_op jit(solution)/shard_map/ppermute | solution.py:17
  97.1 4.8 %collective-permute-start.8 = (bf16[64,256]{1,0:T(8,128)(2,1)S(1)}, bf16[64,256]{1,0:T(8,128)(2,1)S(1)}, u32[]{:S(2)}, u32[]{:S(2)}) collective-permute-start(bf16[64,256]{1,0:T(8,128)(2,1)S(1)} %collective-permute-done.7), channel_id=1, source_target_pairs={{24,0},{0,8},{8,16},{16,24},{25,1},{1,9},{9,17},{17,25},{26,2},{2,... | collective-permute-start | bytes 98312 | tf_op jit(solution)/shard_map/ppermute | solution.py:17
  101.9 9.1 %collective-permute-start.9 = (bf16[64,256]{1,0:T(8,128)(2,1)S(1)}, bf16[64,256]{1,0:T(8,128)(2,1)S(1)}, u32[]{:S(2)}, u32[]{:S(2)}) collective-permute-start(bf16[64,256]{1,0:T(8,128)(2,1)S(1)} %collective-permute-done.8), channel_id=1, source_target_pairs={{24,0},{0,8},{8,16},{16,24},{25,1},{1,9},{9,17},{17,25},{26,2},{2,... | collective-permute-start | bytes 98312 | tf_op jit(solution)/shard_map/ppermute | solution.py:17
  101.9 4.8 %slice-start = ((s8[8388608]{0:T(1024)(128)(4,1)}), s8[4194304]{0:T(1024)(128)(4,1)S(1)}, s32[]{:S(2)}) async-start(s8[8388608]{0:T(1024)(128)(4,1)} %bitcast.60), calls=%async_computation.6 | async-start | bytes 8388608
  103.3 3.4 %slice-start.1 = ((s8[8388608]{0:T(1024)(128)(4,1)}), s8[4194304]{0:T(1024)(128)(4,1)S(1)}, s32[]{:S(2)}) async-start(s8[8388608]{0:T(1024)(128)(4,1)} %bitcast.60), calls=%async_computation.7 | async-start | bytes 8388608
  106.7 3.8 %copy-start.8 = (bf16[256,4096]{1,0:T(8,128)(2,1)}, bf16[256,4096]{1,0:T(8,128)(2,1)S(1)}, u32[]{:S(2)}) copy-start(bf16[256,4096]{1,0:T(8,128)(2,1)S(1)} %fusion.41) | copy-start | bytes 6291460
  108.4 4.3 %copy-start.5 = (bf16[256,4096]{1,0:T(8,128)(2,1)}, bf16[256,4096]{1,0:T(8,128)(2,1)S(1)}, u32[]{:S(2)}) copy-start(bf16[256,4096]{1,0:T(8,128)(2,1)S(1)} %fusion.45) | copy-start | bytes 6291460
  110.0 2.7 %copy-start.7 = (bf16[256,4096]{1,0:T(8,128)(2,1)}, bf16[256,4096]{1,0:T(8,128)(2,1)S(1)}, u32[]{:S(2)}) copy-start(bf16[256,4096]{1,0:T(8,128)(2,1)S(1)} %fusion.43) | copy-start | bytes 6291460
  114.6 59.2 %all-gather.5.cloned.1.call-start = ((), (), s32[]{:S(2)}) async-start(), calls=%async_computation.5 | async-start | bytes 1179648 | tf_op jit(solution)/shard_map/all_gather | solution.py:61
  147.5 10.7 %copy-start.6 = (bf16[256,4096]{1,0:T(8,128)(2,1)S(1)}, bf16[256,4096]{1,0:T(8,128)(2,1)}, u32[]{:S(2)}) copy-start(bf16[256,4096]{1,0:T(8,128)(2,1)} %copy-done.5) | copy-start | bytes 6291460
  150.0 5.2 %collective-permute-start.10 = (f32[64,256]{1,0:T(8,128)S(1)}, f32[64,256]{1,0:T(8,128)S(1)}, u32[]{:S(2)}, u32[]{:S(2)}) collective-permute-start(f32[64,256]{1,0:T(8,128)S(1)} %fusion.52), channel_id=1, source_target_pairs={{24,0},{0,8},{8,16},{16,24},{25,1},{1,9},{9,17},{17,25},{26,2},{2,... | collective-permute-start | bytes 196616 | tf_op jit(solution)/shard_map/ppermute | solution.py:17
  157.6 5.2 %collective-permute-start.11 = (f32[64,256]{1,0:T(8,128)S(1)}, f32[64,256]{1,0:T(8,128)S(1)}, u32[]{:S(2)}, u32[]{:S(2)}) collective-permute-start(f32[64,256]{1,0:T(8,128)S(1)} %convolution_add_fusion.6), channel_id=1, source_target_pairs={{24,0},{0,8},{8,16},{16,24},{25,1},{1,9},{9,17},{17,25},{26,2},{2,... | collective-permute-start | bytes 196616 | tf_op jit(solution)/shard_map/ppermute | solution.py:17
  162.8 5.2 %collective-permute-start.12 = (f32[64,256]{1,0:T(8,128)S(1)}, f32[64,256]{1,0:T(8,128)S(1)}, u32[]{:S(2)}, u32[]{:S(2)}) collective-permute-start(f32[64,256]{1,0:T(8,128)S(1)} %add.137), channel_id=1, source_target_pairs={{24,0},{0,8},{8,16},{16,24},{25,1},{1,9},{9,17},{17,25},{26,2},{2,... | collective-permute-start | bytes 196616 | tf_op jit(solution)/shard_map/ppermute | solution.py:17
  168.0 5.2 %collective-permute-start.13 = (f32[64,256]{1,0:T(8,128)S(1)}, f32[64,256]{1,0:T(8,128)S(1)}, u32[]{:S(2)}, u32[]{:S(2)}) collective-permute-start(f32[64,256]{1,0:T(8,128)S(1)} %add.138), channel_id=1, source_target_pairs={{24,0},{0,8},{8,16},{16,24},{25,1},{1,9},{9,17},{17,25},{26,2},{2,... | collective-permute-start | bytes 196616 | tf_op jit(solution)/shard_map/ppermute | solution.py:17
Sparse Core Ops, SparseCore 0:
  33.9 32.4 reduce-scatter.2
  68.5 20.4 all-gather.2
  114.8 31.0 reduce-scatter.4
  147.9 20.5 all-gather.4
where the time goes:
time: 183 us
  waiting for transfers between devices  107 us (58%)
  matrix products  39.1 us (21%)
  between operations  14.1 us (8%)
  starting transfers between devices  10.7 us (6%)
  other arithmetic  7.53 us (4%)
  local copies, waits for them, and re-layouts  3.69 us (2%)
    reduce_scatter x2, waiting for transfers between devices, body(): lax.psum_scatter(grad_user, 'col', scatter_dimension=1, tiled=True)  63.7 us
    ppermute x14, waiting for transfers between devices, from_behind(): return lax.ppermute(block, axis, route)  43.7 us
    dot_general x8, matrix products, body(): jnp.einsum('kn,km->nm', visitor, user_b, preferred_element_type=jnp.float32)  21.2 us
    dot_general x8, matrix products, body(): jnp.einsum('km,nm->kn', user_b, residual, preferred_element_type=jnp.floa...  11.1 us
    ppermute x14, starting transfers between devices, from_behind(): return lax.ppermute(block, axis, route)  10.6 us
    dot_general x8, matrix products, body(): jnp.einsum('kn,nm->km', visitor, residual, preferred_element_type=jnp.flo...  6.82 us
    unnamed x27, local copies, waits for them, and re-layouts  3.69 us
  transfers between devices with their start and end apart: 18, of which 12 were waited for; matrix products, arithmetic and copies ran while one was open for 19% of the time, Pallas kernels for 0%

commit v1 on v0

v1 whole, which is shorter than its diff:
```python
import functools
import math

import jax
import jax.numpy as jnp
from jax import lax
from jax.experimental import pallas as pl
from jax.experimental.pallas import tpu as pltpu
from jax.sharding import PartitionSpec as P

ITERS = 2
CORES = 2
TILE_USERS = 1024
TILE_ITEMS = 512

f32, bf16 = jnp.float32, jnp.bfloat16


def swap(block, axis, distance):
    return lax.ppermute(block, axis, [(i, i ^ distance) for i in range(lax.axis_size(axis))])


def tree_sum(terms):
    while len(terms) > 1:
        terms = [terms[i] + terms[i + 1] for i in range(0, len(terms), 2)]
    return terms[0]


def span(index, width):
    return pl.ds(pl.multiple_of(index * width, width), width)


def call(kernel, outs, *args, scratch=(), flops=0):
    whole = pl.BlockSpec(memory_space=pltpu.VMEM)
    moved = sum(a.size * a.dtype.itemsize for a in args)
    return pl.pallas_call(
        kernel,
        in_specs=[whole] * len(args),
        out_specs=[whole] * len(outs),
        out_shape=[jax.ShapeDtypeStruct(s, d) for s, d in outs],
        scratch_shapes=list(scratch),
        compiler_params=pltpu.CompilerParams(vmem_limit_bytes=24 << 20),
        cost_estimate=pl.CostEstimate(flops=flops, bytes_accessed=moved, transcendentals=0),
    )(*args)


def gradients(columns, user_of, item_ref, item_t_ref, labels_ref, grad_item_ref, keep):
    start, width = columns
    tile_users, tile_items = min(TILE_USERS, width), min(TILE_ITEMS, labels_ref.shape[0])
    for at in range(0, width, tile_users):
        here = pl.ds(pl.multiple_of(start + at, tile_users), tile_users)
        user = user_of(at, tile_users)
        total = None
        for row in range(0, labels_ref.shape[0], tile_items):
            rows = pl.ds(row, tile_items)
            half_scores = jnp.dot(item_t_ref[rows, :], user, preferred_element_type=f32)
            weights = labels_ref[rows, here].astype(f32)
            residual = (jnp.abs(weights) * jnp.tanh(half_scores) - weights).astype(bf16)
            term = jnp.dot(item_ref[:, rows], residual, preferred_element_type=f32)
            total = term if total is None else total + term
            grad_item_ref[:, rows] += lax.dot_general(
                user, residual, (((1,), (1,)), ((), ())), preferred_element_type=f32
            )
        keep(at, tile_users, total)


def store_into(ref, offset=0):
    def keep(at, width, value):
        ref[:, pl.ds(offset + at, width)] = value.astype(ref.dtype)

    return keep


def put_items(item, item_ref, item_t_ref):
    rounded = item.astype(bf16)
    item_ref[...] = rounded
    item_t_ref[...] = (rounded * jnp.asarray(0.5, bf16)).T


def combine(keep_ref, recv_ref, share, own_ref, send_refs):
    z = lax.axis_index("col") // CORES
    for o in range(len(send_refs) + 1):
        at = span(z ^ o, share)
        piece = keep_ref[:, at] + recv_ref[:, at].astype(f32)
        if o == 0:
            own_ref[...] = piece
        else:
            send_refs[o - 1][...] = piece.astype(bf16)


def first_peer(rows_count, half, *refs):
    blocks, (users, labels) = refs[:rows_count], refs[rows_count : rows_count + 2]
    send, grad_item, item_all, item, item_t = refs[rows_count + 2 :]
    row, core = lax.axis_index("row"), lax.axis_index("col") % CORES
    for o, block in enumerate(blocks):
        item_all[:, span(row ^ o, block.shape[1])] = block[...]
    put_items(item_all[...], item, item_t)
    grad_item[...] = jnp.zeros_like(grad_item)
    start = (1 - core) * half

    def user_of(at, width):
        return users[:, pl.ds(pl.multiple_of(start + at, width), width)].astype(bf16)

    gradients((start, half), user_of, item, item_t, labels, grad_item, store_into(send))


def first_own(part, width, half, users, labels, item, item_t, grad_in, kept, grad_item):
    start = (lax.axis_index("col") % CORES) * half + part
    grad_item[...] = grad_in[...]

    def user_of(at, w):
        return users[:, pl.ds(pl.multiple_of(start + at, w), w)].astype(bf16)

    gradients((start, width), user_of, item, item_t, labels, grad_item, store_into(kept))


def first_last(part, width, half, share, chips, users, labels, item, item_t, grad_in, kept_in, recv, *refs):
    own, sends, grad_out = refs[0], refs[1:chips], refs[chips]
    kept, grad_item = refs[chips + 1 :]
    start = (lax.axis_index("col") % CORES) * half + part
    grad_item[...] = grad_in[...]
    kept[:, pl.ds(0, part)] = kept_in[...]

    def user_of(at, w):
        return users[:, pl.ds(pl.multiple_of(start + at, w), w)].astype(bf16)

    gradients((start, width), user_of, item, item_t, labels, grad_item, store_into(kept, part))
    grad_out[...] = grad_item[...].astype(bf16)
    combine(kept, recv, share, own, sends)


def share_at(half, share):
    col = lax.axis_index("col")
    return pl.ds(pl.multiple_of((col % CORES) * half + (col // CORES) * share, share), share)


def update_share(rate, half, share, own, *refs):
    recvs, (users, new, new_b) = refs[:-3], refs[-3:]
    grad = tree_sum([own[...]] + [r[...].astype(f32) for r in recvs])
    new[...] = users[:, share_at(half, share)] - rate * grad
    new_b[...] = new[...].astype(bf16)


def update_last(rate, half, share, own, *refs):
    recvs, (users, new, delta_b) = refs[:-3], refs[-3:]
    grad = tree_sum([own[...]] + [r[...].astype(f32) for r in recvs])
    delta_b[...] = (new[...] - rate * grad - users[:, share_at(half, share)]).astype(bf16)


def second_start(rate, rows_count, chips, *refs):
    grads, item_all = refs[:rows_count], refs[rows_count]
    pieces = refs[rows_count + 1 : rows_count + 1 + chips]
    item_own, item, item_t, user_half = refs[rows_count + 1 + chips :]
    assemble(pieces, user_half)
    new = item_all[...] - rate * tree_sum([g[...].astype(f32) for g in grads])
    put_items(new, item, item_t)
    block = item_own.shape[1]
    at = span(lax.axis_index("row"), block)
    grad = tree_sum([g[:, at].astype(f32) for g in grads])
    item_own[...] = item_all[:, at] - rate * grad


def assemble(pieces, user_half):
    z = lax.axis_index("col") // CORES
    for o, piece in enumerate(pieces):
        user_half[:, span(z ^ o, piece.shape[1])] = piece[...]


def second_own(part, width, half, user_half, labels, item, item_t, grad_in, kept, grad_item):
    start = (lax.axis_index("col") % CORES) * half + part
    if grad_in is None:
        grad_item[...] = jnp.zeros_like(grad_item)
    else:
        grad_item[...] = grad_in[...]

    def user_of(at, w):
        return user_half[:, pl.ds(part + at, w)]

    gradients((start, width), user_of, item, item_t, labels, grad_item, store_into(kept))


def second_open(part, width, half, user_half, labels, item, item_t, kept, grad_item):
    second_own(part, width, half, user_half, labels, item, item_t, None, kept, grad_item)


def second_peer(half, user_half, labels, item, item_t, grad_in, send, grad_item):
    start = (1 - lax.axis_index("col") % CORES) * half
    grad_item[...] = grad_in[...]

    def user_of(at, w):
        return user_half[:, pl.ds(at, w)]

    gradients((start, half), user_of, item, item_t, labels, grad_item, store_into(send))


def second_last(parts, half, share, chips, rows_count, user_half, labels, item, item_t, grad_in, kept0, kept1, recv, *refs):
    own, sends = refs[0], refs[1:chips]
    item_own, item_sends = refs[chips], refs[chips + 1 : chips + rows_count]
    kept, grad_item = refs[chips + rows_count :]
    first, second = parts
    start = (lax.axis_index("col") % CORES) * half
    grad_item[...] = grad_in[...]
    kept[:, pl.ds(0, first)] = kept0[...]
    kept[:, pl.ds(first, second)] = kept1[...]
    part = first + second

    def user_of(at, w):
        return user_half[:, pl.ds(part + at, w)]

    gradients((start + part, half - part), user_of, item, item_t, labels, grad_item, store_into(kept, part))
    combine(kept, recv, share, own, sends)
    row, block = lax.axis_index("row"), item_own.shape[1]
    for o in range(rows_count):
        piece = grad_item[:, span(row ^ o, block)]
        if o == 0:
            item_own[...] = piece
        else:
            item_sends[o - 1][...] = piece.astype(bf16)


def gather_half(chips, *refs):
    assemble(refs[:chips], refs[chips])


def finish_items(rate, item, own, *refs):
    recvs, out = refs[:-1], refs[-1]
    out[...] = item[...] - rate * tree_sum([own[...]] + [r[...].astype(f32) for r in recvs])


def finish_users(half, users, own, peer, out):
    core = lax.axis_index("col") % CORES
    mine, other = span(core, half), span(1 - core, half)
    out[:, mine] = users[:, mine] + own[...].astype(f32)
    out[:, other] = users[:, other] + peer[...].astype(f32)


def body(preference, users, items):
    rows_count, cols_count = lax.axis_size("row"), lax.axis_size("col")
    items_dev, users_dev = preference.shape
    rank, block = items.shape
    chips = cols_count // CORES
    half, share = users_dev // CORES, users_dev // cols_count
    user_rate = 0.5 / math.sqrt(items_dev * cols_count)
    item_rate = 0.5 / math.sqrt(users_dev * rows_count)
    work = lambda width: 6 * rank * items_dev * width
    grad_items = ((rank, items_dev), f32)
    item_pair = [((rank, items_dev), bf16), ((items_dev, rank), bf16)]
    others_z = sorted(range(1, chips), key=lambda o: (o == 2, o))
    others_row = list(range(1, rows_count))

    def z_exchange(blocks):
        got = {o: swap(blocks[o - 1], "col", o * CORES) for o in others_z}
        return [got[o] for o in range(1, chips)]

    blocks = [items] + [swap(items, "row", o) for o in others_row]
    send, grad, item_all, item, item_t = call(
        functools.partial(first_peer, rows_count, half),
        [((rank, half), bf16), grad_items, ((rank, items_dev), f32)] + item_pair,
        *blocks, users, preference, flops=work(half),
    )
    recv = swap(send, "col", 1)
    part = half // 2
    kept, grad = call(
        functools.partial(first_own, 0, part, half),
        [((rank, part), f32), grad_items],
        users, preference, item, item_t, grad, flops=work(part),
    )
    piece_outs = [((rank, share), f32)] + [((rank, share), bf16)] * (chips - 1)
    *pieces, grad_b = call(
        functools.partial(first_last, part, half - part, half, share, chips),
        piece_outs + [((rank, items_dev), bf16)],
        users, preference, item, item_t, grad, kept, recv,
        scratch=[pltpu.VMEM((rank, half), f32), pltpu.VMEM((rank, items_dev), f32)],
        flops=work(half - part),
    )
    recvs = z_exchange(pieces[1:])
    grads = [grad_b] + [swap(grad_b, "row", o) for o in others_row]
    new, new_b = call(
        functools.partial(update_share, user_rate, half, share),
        [((rank, share), f32), ((rank, share), bf16)],
        pieces[0], *recvs, users,
    )
    spread = [new_b] + z_exchange([new_b] * (chips - 1))
    item_own, item, item_t, user_half = call(
        functools.partial(second_start, item_rate, rows_count, chips),
        [((rank, block), f32)] + item_pair + [((rank, half), bf16)],
        *grads, item_all, *spread,
    )
    user_peer = swap(user_half, "col", 1)
    first, second = half // 4, half // 2
    kept0, grad = call(
        functools.partial(second_open, 0, first, half),
        [((rank, first), f32), grad_items],
        user_half, preference, item, item_t, flops=work(first),
    )
    send, grad = call(
        functools.partial(second_peer, half),
        [((rank, half), bf16), grad_items],
        user_peer, preference, item, item_t, grad, flops=work(half),
    )
    recv = swap(send, "col", 1)
    kept1, grad = call(
        functools.partial(second_own, first, second, half),
        [((rank, second), f32), grad_items],
        user_half, preference, item, item_t, grad, flops=work(second),
    )
    outs = call(
        functools.partial(second_last, (first, second), half, share, chips, rows_count),
        piece_outs + [((rank, block), f32)] + [((rank, block), bf16)] * (rows_count - 1),
        user_half, preference, item, item_t, grad, kept0, kept1, recv,
        scratch=[pltpu.VMEM((rank, half), f32), pltpu.VMEM((rank, items_dev), f32)],
        flops=work(half - first - second),
    )
    pieces, item_pieces = outs[:chips], outs[chips:]
    recvs = z_exchange(pieces[1:])
    item_recvs = [swap(item_pieces[o], "row", o) for o in others_row]
    (delta_b,) = call(
        functools.partial(update_last, user_rate, half, share),
        [((rank, share), bf16)],
        pieces[0], *recvs, users, new,
    )
    spread = [delta_b] + z_exchange([delta_b] * (chips - 1))
    (new_items,) = call(
        functools.partial(finish_items, item_rate),
        [((rank, block), f32)],
        item_own, item_pieces[0], *item_recvs,
    )
    (delta_half,) = call(functools.partial(gather_half, chips), [((rank, half), bf16)], *spread)
    delta_peer = swap(delta_half, "col", 1)
    (new_users,) = call(
        functools.partial(finish_users, half),
        [((rank, users_dev), f32)],
        users, delta_half, delta_peer,
    )
    return new_users, new_items


def solution(mesh):
    return jax.shard_map(
        body,
        mesh=mesh,
        in_specs=(P("col", "row"), P(None, "row"), P(None, ("col", "row"))),
        out_specs=(P(None, "row"), P(None, ("col", "row"))),
        check_vma=False,
    )
```

time: 183 us -> 79.1 us (0.43)
  waiting for transfers between devices: 107 us -> 26.4 us
  matrix products: 39.1 us -> 0 us
  starting transfers between devices: 10.7 us -> 29.9 us
  Pallas kernels: 0 us -> 16.4 us
  between operations: 14.1 us -> 0.77 us
  other arithmetic: 7.53 us -> 0 us
    reduce_scatter x2 -> x0, waiting for transfers between devices: 63.7 us -> none  [body(): lax.psum_scatter(grad_user, 'col', scatter_dimension=1, tiled=True)]
    dot_general x24 -> x0, matrix products: 39.1 us -> none  [the longest x8 21.2 us: body(): jnp.einsum('kn,km->nm', visitor, user_b, preferred_element_type=jnp.float32)]
    ppermute x14 -> x25, starting transfers between devices: 10.6 us -> 29.9 us  [swap(): lax.ppermute(block, axis, [(i, i ^ distance) for i in range(lax.axis_size...]
    ppermute x14 -> x25, waiting for transfers between devices: 43.7 us -> 26.4 us  [swap(): lax.ppermute(block, axis, [(i, i ^ distance) for i in range(lax.axis_size...]
    pallas_call x0 -> x13, Pallas kernels: none -> 16.4 us  [call(): pl.pallas_call(kernel, in_specs=[whole] * len(args), out_specs=[whole] *...]
    sub x3 -> x0, other arithmetic: 3.93 us -> none  [the longest x2 3.29 us: body(): own_users - user_rate * user_share]
    convert_element_type x4 -> x0, other arithmetic: 3.56 us -> none  [the longest x2 2.71 us: body(): user_b = users.astype(jnp.bfloat16)]
    unnamed x27 -> x10, local copies, waits for them, and re-layouts: 3.69 us -> 5.45 us
  transfers between devices with their start and end apart: 18 -> 25, of which waited for: 12 -> 15; matrix products, arithmetic and copies ran while one was open for 19% -> 0% of each run, Pallas kernels for 0% -> 7%
where the time goes in v1:
time: 79.1 us; the launch traced here: 78.9 us
  starting transfers between devices  29.9 us (38%)
  waiting for transfers between devices  26.4 us (33%)
  Pallas kernels  16.4 us (21%)
  local copies, waits for them, and re-layouts  5.45 us (7%)
    ppermute x25, starting transfers between devices, swap(): lax.ppermute(block, axis, [(i, i ^ distance) for i in range(lax.axis_size...  29.9 us
    ppermute x25, waiting for transfers between devices, swap(): lax.ppermute(block, axis, [(i, i ^ distance) for i in range(lax.axis_size...  26.4 us
    pallas_call x13, Pallas kernels, call(): pl.pallas_call(kernel, in_specs=[whole] * len(args), out_specs=[whole] *...  16.4 us
    unnamed x10, local copies, waits for them, and re-layouts  5.45 us
  transfers between devices with their start and end apart: 25, of which 15 were waited for; matrix products, arithmetic and copies ran while one was open for 0% of the time, Pallas kernels for 7%

profile of v1, /device:TPU:0, one launch (start us, length us, event | category | flops | bytes accessed | tf_op | source)
XLA Modules:
  0.0 78.9 jit_solution(14927663456563296625)
XLA Ops:
  0.6 3.0 %collective-permute-start.1 = (f32[64,256]{1,0:T(8,128)}, f32[64,256]{1,0:T(8,128)S(1)}, u32[]{:S(2)}, u32[]{:S(2)}) collective-permute-start(f32[64,256]{1,0:T(8,128)} %refs_0_.1), channel_id=1, source_target_pairs={{0,16},{8,24},{16,0},{24,8},{1,17},{9,25},{17,1},{25,9},{2,18},{10... | collective-permute-start | bytes 196616 | tf_op jit(solution)/shard_map/ppermute | solution.py:20
  3.7 1.5 %collective-permute-start = (f32[64,256]{1,0:T(8,128)}, f32[64,256]{1,0:T(8,128)S(1)}, u32[]{:S(2)}, u32[]{:S(2)}) collective-permute-start(f32[64,256]{1,0:T(8,128)} %refs_0_.1), channel_id=1, source_target_pairs={{0,8},{8,0},{16,24},{24,16},{1,9},{9,1},{17,25},{25,17},{2,10},{10... | collective-permute-start | bytes 196616 | tf_op jit(solution)/shard_map/ppermute | solution.py:20
  5.2 0.9 %collective-permute-done.1.refs_2_ = f32[64,256]{1,0:T(8,128)S(1)} collective-permute-done((f32[64,256]{1,0:T(8,128)}, f32[64,256]{1,0:T(8,128)S(1)}, u32[]{:S(2)}, u32[]{:S(2)}) %collective-permute-start.1) | collective-permute-done | bytes 65568 | tf_op jit(solution)/shard_map/ppermute | solution.py:20
  6.1 2.5 %collective-permute-done.refs_1_ = f32[64,256]{1,0:T(8,128)S(1)} collective-permute-done((f32[64,256]{1,0:T(8,128)}, f32[64,256]{1,0:T(8,128)S(1)}, u32[]{:S(2)}, u32[]{:S(2)}) %collective-permute-start) | collective-permute-done | bytes 65568 | tf_op jit(solution)/shard_map/ppermute | solution.py:20
  8.6 1.9 %collective-permute-done.2.refs_3_ = f32[64,256]{1,0:T(8,128)S(1)} collective-permute-done((f32[64,256]{1,0:T(8,128)}, f32[64,256]{1,0:T(8,128)S(1)}, u32[]{:S(2)}, u32[]{:S(2)}) %collective-permute-start.2) | collective-permute-done | bytes 65568 | tf_op jit(solution)/shard_map/ppermute | solution.py:20
  10.5 3.4 %copy-done = bf16[1024,4096]{1,0:T(8,128)(2,1)S(1)} copy-done((bf16[1024,4096]{1,0:T(8,128)(2,1)S(1)}, bf16[1024,4096]{1,0:T(8,128)(2,1)}, u32[]{:S(2)}) %copy-start) | copy-done | bytes 8388632
  13.9 1.2 %copy-done.2 = f32[64,4096]{1,0:T(8,128)S(1)} copy-done((f32[64,4096]{1,0:T(8,128)S(1)}, f32[64,4096]{1,0:T(8,128)}, u32[]{:S(2)}) %copy-start.2) | copy-done | bytes 1048600
  15.1 0.8 %copy-done.4 = f32[64,256]{1,0:T(8,128)S(1)} copy-done((f32[64,256]{1,0:T(8,128)S(1)}, f32[64,256]{1,0:T(8,128)}, u32[]{:S(2)}) %copy-start.4) | copy-done | bytes 65560
  16.0 3.5 %shard_map.50 = (bf16[64,2048]{1,0:T(8,128)(2,1)S(1)}, f32[64,1024]{1,0:T(8,128)S(1)}, f32[64,1024]{1,0:T(8,128)S(1)}, bf16[64,1024]{1,0:T(8,128)(2,1)S(1)}, bf16[1024,64]{1,0:T(8,128)(2,1)S(1)}) custom-call(f32[64,256]{1,0:T(8,128)S(1)} %copy-done.4, f32[64,256]{1,0:T(8,128)S(1)} %collective-permute-done.refs_1_, ...), custom_call_target="tpu_custom_call" | custom-call | flops 805306368 | bytes 9699328 | tf_op jit(solution)/shard_map/pallas_call | solution.py:36
  19.6 1.8 %shard_map.51 = (f32[64,1024]{1,0:T(8,128)S(1)}, f32[64,1024]{1,0:T(8,128)S(1)}) custom-call(f32[64,4096]{1,0:T(8,128)S(1)} %copy-done.2, bf16[1024,4096]{1,0:T(8,128)(2,1)S(1)} %copy-done.1, bf16[64,1024]{1,0:T(8,128)(2,1)S(1)} %get-tuple-element.34.item, bf16[1024,64]{1,0:T(8,128)(2,1)S(1)} %get-tuple-element.35.item_t, ...), custom_call_target="tpu_custom_call" | custom-call | flops 402653184 | bytes 9961472 | tf_op jit(solution)/shard_map/pallas_call | solution.py:36
  21.4 1.8 %shard_map.52 = (f32[64,512]{1,0:T(8,128)S(1)}, bf16[64,512]{1,0:T(8,128)(2,1)S(1)}, bf16[64,512]{1,0:T(8,128)(2,1)S(1)}, bf16[64,512]{1,0:T(8,128)(2,1)S(1)}, bf16[64,1024]{1,0:T(8,128)(2,1)S(1)}) custom-call(f32[64,4096]{1,0:T(8,128)S(1)} %copy-done.2, bf16[1024,4096]{1,0:T(8,128)(2,1)S(1)} %copy-done.1, bf16[64,1024]{1,0:T(8,128)(2,1)S(1)} %get-tuple-element.34.item, ...), custom_call_target="tpu_custom_call" | custom-call | flops 402653184 | bytes 10485760 | tf_op jit(solution)/shard_map/pallas_call | solution.py:36
  23.1 1.6 %collective-permute-start.7 = (bf16[64,512]{1,0:T(8,128)(2,1)S(1)}, bf16[64,512]{1,0:T(8,128)(2,1)S(1)}, u32[]{:S(2)}, u32[]{:S(2)}) collective-permute-start(bf16[64,512]{1,0:T(8,128)(2,1)S(1)} %get-tuple-element.43), channel_id=1, source_target_pairs={{0,2},{1,3},{2,0},{3,1},{4,6},{5,7},{6,4},{7,5},{8,10},{9,11},{10,... | collective-permute-start | bytes 196616 | tf_op jit(solution)/shard_map/ppermute | solution.py:20
  24.8 2.6 %collective-permute-start.8 = (bf16[64,512]{1,0:T(8,128)(2,1)S(1)}, bf16[64,512]{1,0:T(8,128)(2,1)S(1)}, u32[]{:S(2)}, u32[]{:S(2)}) collective-permute-start(bf16[64,512]{1,0:T(8,128)(2,1)S(1)} %get-tuple-element.44), channel_id=1, source_target_pairs={{0,4},{1,5},{2,6},{3,7},{4,0},{5,1},{6,2},{7,3},{8,12},{9,13},{10,... | collective-permute-start | bytes 196616 | tf_op jit(solution)/shard_map/ppermute | solution.py:20
  27.4 0.2 collective-permute-start.9
  27.7 4.8 %collective-permute-done.8.refs_1_ = bf16[64,512]{1,0:T(8,128)(2,1)S(1)} collective-permute-done((bf16[64,512]{1,0:T(8,128)(2,1)S(1)}, bf16[64,512]{1,0:T(8,128)(2,1)S(1)}, u32[]{:S(2)}, u32[]{:S(2)}) %collective-permute-start.8) | collective-permute-done | bytes 65568 | tf_op jit(solution)/shard_map/ppermute | solution.py:20
  32.5 1.0 %collective-permute-done.9.refs_2_ = bf16[64,512]{1,0:T(8,128)(2,1)S(1)} collective-permute-done((bf16[64,512]{1,0:T(8,128)(2,1)S(1)}, bf16[64,512]{1,0:T(8,128)(2,1)S(1)}, u32[]{:S(2)}, u32[]{:S(2)}) %collective-permute-start.9) | collective-permute-done | bytes 65568 | tf_op jit(solution)/shard_map/ppermute | solution.py:20
  33.6 2.4 %collective-permute-start.12 = (bf16[64,512]{1,0:T(8,128)(2,1)S(1)}, bf16[64,512]{1,0:T(8,128)(2,1)S(1)}, u32[]{:S(2)}, u32[]{:S(2)}) collective-permute-start(bf16[64,512]{1,0:T(8,128)(2,1)S(1)} %get-tuple-element.46.refs_5_), channel_id=1, source_target_pairs={{0,6},{1,7},{2,4},{3,5},{4,2},{5,3},{6,0},{7,1},{8,14},{9,15},{10,... | collective-permute-start | bytes 196616 | tf_op jit(solution)/shard_map/ppermute | solution.py:20
  36.0 0.7 collective-permute-start.6
  36.7 1.3 %collective-permute-start.5 = (bf16[64,1024]{1,0:T(8,128)(2,1)S(1)}, bf16[64,1024]{1,0:T(8,128)(2,1)S(1)}, u32[]{:S(2)}, u32[]{:S(2)}) collective-permute-start(bf16[64,1024]{1,0:T(8,128)(2,1)S(1)} %get-tuple-element.40.refs_0_), channel_id=1, source_target_pairs={{0,16},{8,24},{16,0},{24,8},{1,17},{9,25},{17,1},{25,9},{2,18},{10... | collective-permute-start | bytes 393224 | tf_op jit(solution)/shard_map/ppermute | solution.py:20
  38.0 1.5 %collective-permute-start.4 = (bf16[64,1024]{1,0:T(8,128)(2,1)S(1)}, bf16[64,1024]{1,0:T(8,128)(2,1)S(1)}, u32[]{:S(2)}, u32[]{:S(2)}) collective-permute-start(bf16[64,1024]{1,0:T(8,128)(2,1)S(1)} %get-tuple-element.40.refs_0_), channel_id=1, source_target_pairs={{0,8},{8,0},{16,24},{24,16},{1,9},{9,1},{17,25},{25,17},{2,10},{10... | collective-permute-start | bytes 393224 | tf_op jit(solution)/shard_map/ppermute | solution.py:20
  39.5 0.3 collective-permute-start.11
  39.8 1.7 %collective-permute-start.10 = (bf16[64,512]{1,0:T(8,128)(2,1)S(1)}, bf16[64,512]{1,0:T(8,128)(2,1)S(1)}, u32[]{:S(2)}, u32[]{:S(2)}) collective-permute-start(bf16[64,512]{1,0:T(8,128)(2,1)S(1)} %get-tuple-element.46.refs_5_), channel_id=1, source_target_pairs={{0,2},{1,3},{2,0},{3,1},{4,6},{5,7},{6,4},{7,5},{8,10},{9,11},{10,... | collective-permute-start | bytes 196616 | tf_op jit(solution)/shard_map/ppermute | solution.py:20
  41.5 3.6 %collective-permute-done.11.refs_7_ = bf16[64,512]{1,0:T(8,128)(2,1)S(1)} collective-permute-done((bf16[64,512]{1,0:T(8,128)(2,1)S(1)}, bf16[64,512]{1,0:T(8,128)(2,1)S(1)}, u32[]{:S(2)}, u32[]{:S(2)}) %collective-permute-start.11) | collective-permute-done | bytes 65568 | tf_op jit(solution)/shard_map/ppermute | solution.py:20
  45.2 0.2 shard_map.54
  45.4 1.1 %shard_map.55 = (f32[64,512]{1,0:T(8,128)S(1)}, f32[64,1024]{1,0:T(8,128)S(1)}) custom-call(bf16[64,2048]{1,0:T(8,128)(2,1)S(1)} %get-tuple-element.47.user_half, bf16[1024,4096]{1,0:T(8,128)(2,1)S(1)} %copy-done.1, bf16[64,1024]{1,0:T(8,128)(2,1)S(1)} %get-tuple-element.48.item, bf16[1024,64]{1,0:T(8,128)(2,1)S(1)} %get-tuple-element.49.item_t), custom_call_target="tpu_custom_call" | custom-call | flops 201326592 | bytes 8912896 | tf_op jit(solution)/shard_map/pallas_call | solution.py:36
  46.5 0.5 collective-permute-done.13.user_half
  46.9 3.4 %shard_map.56 = (bf16[64,2048]{1,0:T(8,128)(2,1)S(1)}, f32[64,1024]{1,0:T(8,128)S(1)}) custom-call(bf16[64,2048]{1,0:T(8,128)(2,1)S(1)} %collective-permute-done.13.user_half, bf16[1024,4096]{1,0:T(8,128)(2,1)S(1)} %copy-done.1, bf16[64,1024]{1,0:T(8,128)(2,1)S(1)} %get-tuple-element.48.item, bf16[1024,64]{1,0:T(8,128)(2,1)S(1)} %get-tuple-element.49.item_t, ...), custom_call_target="tpu_custom_call" | custom-call | flops 805306368 | bytes 9175040 | tf_op jit(solution)/shard_map/pallas_call | solution.py:36
  50.3 0.2 collective-permute-start.14
  50.5 1.8 %shard_map.57 = (f32[64,1024]{1,0:T(8,128)S(1)}, f32[64,1024]{1,0:T(8,128)S(1)}) custom-call(bf16[64,2048]{1,0:T(8,128)(2,1)S(1)} %get-tuple-element.47.user_half, bf16[1024,4096]{1,0:T(8,128)(2,1)S(1)} %copy-done.1, bf16[64,1024]{1,0:T(8,128)(2,1)S(1)} %get-tuple-element.48.item, bf16[1024,64]{1,0:T(8,128)(2,1)S(1)} %get-tuple-element.49.item_t, ...), custom_call_target="tpu_custom_call" | custom-call | flops 402653184 | bytes 9175040 | tf_op jit(solution)/shard_map/pallas_call | solution.py:36
  52.3 1.1 %shard_map.58 = (f32[64,512]{1,0:T(8,128)S(1)}, bf16[64,512]{1,0:T(8,128)(2,1)S(1)}, bf16[64,512]{1,0:T(8,128)(2,1)S(1)}, bf16[64,512]{1,0:T(8,128)(2,1)S(1)}, f...) custom-call(bf16[64,2048]{1,0:T(8,128)(2,1)S(1)} %get-tuple-element., ...), custom_call_target="tpu_custom_call" | custom-call | flops 201326592 | bytes 9830400 | tf_op jit(solution)/shard_map/pallas_call | solution.py:36
  53.5 0.7 collective-permute-start.15
  54.2 1.9 %collective-permute-start.16 = (bf16[64,512]{1,0:T(8,128)(2,1)S(1)}, bf16[64,512]{1,0:T(8,128)(2,1)S(1)}, u32[]{:S(2)}, u32[]{:S(2)}) collective-permute-start(bf16[64,512]{1,0:T(8,128)(2,1)S(1)} %get-tuple-element.58), channel_id=1, source_target_pairs={{0,4},{1,5},{2,6},{3,7},{4,0},{5,1},{6,2},{7,3},{8,12},{9,13},{10,... | collective-permute-start | bytes 196616 | tf_op jit(solution)/shard_map/ppermute | solution.py:20
  56.1 1.8 %collective-permute-start.17 = (bf16[64,512]{1,0:T(8,128)(2,1)S(1)}, bf16[64,512]{1,0:T(8,128)(2,1)S(1)}, u32[]{:S(2)}, u32[]{:S(2)}) collective-permute-start(bf16[64,512]{1,0:T(8,128)(2,1)S(1)} %get-tuple-element.59), channel_id=1, source_target_pairs={{0,6},{1,7},{2,4},{3,5},{4,2},{5,3},{6,0},{7,1},{8,14},{9,15},{10,... | collective-permute-start | bytes 196616 | tf_op jit(solution)/shard_map/ppermute | solution.py:20
  57.9 0.7 collective-permute-done.15.refs_0_
  58.6 4.1 %collective-permute-done.16.refs_1_ = bf16[64,512]{1,0:T(8,128)(2,1)S(1)} collective-permute-done((bf16[64,512]{1,0:T(8,128)(2,1)S(1)}, bf16[64,512]{1,0:T(8,128)(2,1)S(1)}, u32[]{:S(2)}, u32[]{:S(2)}) %collective-permute-start.16) | collective-permute-done | bytes 65568 | tf_op jit(solution)/shard_map/ppermute | solution.py:20
  62.7 2.3 %collective-permute-start.20 = (bf16[64,512]{1,0:T(8,128)(2,1)S(1)}, bf16[64,512]{1,0:T(8,128)(2,1)S(1)}, u32[]{:S(2)}, u32[]{:S(2)}) collective-permute-start(bf16[64,512]{1,0:T(8,128)(2,1)S(1)} %shard_map.59.refs_0_), channel_id=1, source_target_pairs={{0,6},{1,7},{2,4},{3,5},{4,2},{5,3},{6,0},{7,1},{8,14},{9,15},{10,... | collective-permute-start | bytes 196616 | tf_op jit(solution)/shard_map/ppermute | solution.py:20
  65.0 0.6 collective-permute-start.19
  65.6 1.5 %collective-permute-start.18 = (bf16[64,512]{1,0:T(8,128)(2,1)S(1)}, bf16[64,512]{1,0:T(8,128)(2,1)S(1)}, u32[]{:S(2)}, u32[]{:S(2)}) collective-permute-start(bf16[64,512]{1,0:T(8,128)(2,1)S(1)} %shard_map.59.refs_0_), channel_id=1, source_target_pairs={{0,2},{1,3},{2,0},{3,1},{4,6},{5,7},{6,4},{7,5},{8,10},{9,11},{10,... | collective-permute-start | bytes 196616 | tf_op jit(solution)/shard_map/ppermute | solution.py:20
  67.1 2.3 %collective-permute-done.20.refs_3_ = bf16[64,512]{1,0:T(8,128)(2,1)S(1)} collective-permute-done((bf16[64,512]{1,0:T(8,128)(2,1)S(1)}, bf16[64,512]{1,0:T(8,128)(2,1)S(1)}, u32[]{:S(2)}, u32[]{:S(2)}) %collective-permute-start.20) | collective-permute-done | bytes 65568 | tf_op jit(solution)/shard_map/ppermute | solution.py:20
  69.5 1.4 %collective-permute-done.19.refs_2_ = bf16[64,512]{1,0:T(8,128)(2,1)S(1)} collective-permute-done((bf16[64,512]{1,0:T(8,128)(2,1)S(1)}, bf16[64,512]{1,0:T(8,128)(2,1)S(1)}, u32[]{:S(2)}, u32[]{:S(2)}) %collective-permute-start.19) | collective-permute-done | bytes 65568 | tf_op jit(solution)/shard_map/ppermute | solution.py:20
  71.0 0.6 collective-permute-start.22
  71.6 0.7 collective-permute-start.23
  72.4 2.2 %collective-permute-start.24 = (bf16[64,256]{1,0:T(8,128)(2,1)S(1)}, bf16[64,256]{1,0:T(8,128)(2,1)S(1)}, u32[]{:S(2)}, u32[]{:S(2)}) collective-permute-start(bf16[64,256]{1,0:T(8,128)(2,1)S(1)} %get-tuple-element.65), channel_id=1, source_target_pairs={{0,24},{8,16},{16,8},{24,0},{1,25},{9,17},{17,9},{25,1},{2,26},{10... | collective-permute-start | bytes 98312 | tf_op jit(solution)/shard_map/ppermute | solution.py:20
  74.6 0.4 collective-permute-done.22.refs_0_
  75.0 0.5 collective-permute-done.23.refs_1_
  75.6 1.6 %collective-permute-done.24.refs_2_ = bf16[64,256]{1,0:T(8,128)(2,1)S(1)} collective-permute-done((bf16[64,256]{1,0:T(8,128)(2,1)S(1)}, bf16[64,256]{1,0:T(8,128)(2,1)S(1)}, u32[]{:S(2)}, u32[]{:S(2)}) %collective-permute-start.24) | collective-permute-done | bytes 32800 | tf_op jit(solution)/shard_map/ppermute | solution.py:20
  77.2 0.7 shard_map.62
  77.8 1.1 %shard_map.61 = f32[64,4096]{1,0:T(8,128)} custom-call(f32[64,4096]{1,0:T(8,128)S(1)} %copy-done.3, bf16[64,2048]{1,0:T(8,128)(2,1)S(1)} %shard_map.60.own, bf16[64,2048]{1,0:T(8,128)(2,1)S(1)} %collective-permute-done.21.peer), custom_call_target="tpu_custom_call" | custom-call | bytes 1572864 | tf_op jit(solution)/shard_map/pallas_call | solution.py:36
  (25 shorter events, 0.5 us)
Async XLA Ops:
  0.6 5.5 %collective-permute-start.1 = (f32[64,256]{1,0:T(8,128)}, f32[64,256]{1,0:T(8,128)S(1)}, u32[]{:S(2)}, u32[]{:S(2)}) collective-permute-start(f32[64,256]{1,0:T(8,128)} %refs_0_.1), channel_id=1, source_target_pairs={{0,16},{8,24},{16,0},{24,8},{1,17},{9,25},{17,1},{25,9},{2,18},{10... | collective-permute-start | bytes 196616 | tf_op jit(solution)/shard_map/ppermute | solution.py:20
  3.7 4.9 %collective-permute-start = (f32[64,256]{1,0:T(8,128)}, f32[64,256]{1,0:T(8,128)S(1)}, u32[]{:S(2)}, u32[]{:S(2)}) collective-permute-start(f32[64,256]{1,0:T(8,128)} %refs_0_.1), channel_id=1, source_target_pairs={{0,8},{8,0},{16,24},{24,16},{1,9},{9,1},{17,25},{25,17},{2,10},{10... | collective-permute-start | bytes 196616 | tf_op jit(solution)/shard_map/ppermute | solution.py:20
  5.2 5.4 %collective-permute-start.2 = (f32[64,256]{1,0:T(8,128)}, f32[64,256]{1,0:T(8,128)S(1)}, u32[]{:S(2)}, u32[]{:S(2)}) collective-permute-start(f32[64,256]{1,0:T(8,128)} %refs_0_.1), channel_id=1, source_target_pairs={{0,24},{8,16},{16,8},{24,0},{1,25},{9,17},{17,9},{25,1},{2,26},{10... | collective-permute-start | bytes 196616 | tf_op jit(solution)/shard_map/ppermute | solution.py:20
  10.5 3.4 %copy-start = (bf16[1024,4096]{1,0:T(8,128)(2,1)S(1)}, bf16[1024,4096]{1,0:T(8,128)(2,1)}, u32[]{:S(2)}) copy-start(bf16[1024,4096]{1,0:T(8,128)(2,1)} %labels.11) | copy-start | bytes 25165828
  13.9 1.2 %copy-start.2 = (f32[64,4096]{1,0:T(8,128)S(1)}, f32[64,4096]{1,0:T(8,128)}, u32[]{:S(2)}) copy-start(f32[64,4096]{1,0:T(8,128)} %users.5) | copy-start | bytes 3145732
  15.1 0.8 %copy-start.4 = (f32[64,256]{1,0:T(8,128)S(1)}, f32[64,256]{1,0:T(8,128)}, u32[]{:S(2)}) copy-start(f32[64,256]{1,0:T(8,128)} %refs_0_.1) | copy-start | bytes 196612
  16.0 3.6 %copy-start.1 = (bf16[1024,4096]{1,0:T(8,128)(2,1)S(1)}, bf16[1024,4096]{1,0:T(8,128)(2,1)}, u32[]{:S(2)}) copy-start(bf16[1024,4096]{1,0:T(8,128)(2,1)} %labels.11) | copy-start | bytes 25165828
  19.5 1.9 %collective-permute-start.3 = (bf16[64,2048]{1,0:T(8,128)(2,1)S(1)}, bf16[64,2048]{1,0:T(8,128)(2,1)S(1)}, u32[]{:S(2)}, u32[]{:S(2)}) collective-permute-start(bf16[64,2048]{1,0:T(8,128)(2,1)S(1)} %get-tuple-element.39), channel_id=1, source_target_pairs={{0,1},{1,0},{2,3},{3,2},{4,5},{5,4},{6,7},{7,6},{8,9},{9,8},{10,11... | collective-permute-start | bytes 786440 | tf_op jit(solution)/shard_map/ppermute | solution.py:20
  19.6 13.9 %copy-start.3 = (f32[64,4096]{1,0:T(8,128)S(1)}, f32[64,4096]{1,0:T(8,128)}, u32[]{:S(2)}) copy-start(f32[64,4096]{1,0:T(8,128)} %users.5) | copy-start | bytes 3145732
  23.1 4.5 %collective-permute-start.7 = (bf16[64,512]{1,0:T(8,128)(2,1)S(1)}, bf16[64,512]{1,0:T(8,128)(2,1)S(1)}, u32[]{:S(2)}, u32[]{:S(2)}) collective-permute-start(bf16[64,512]{1,0:T(8,128)(2,1)S(1)} %get-tuple-element.43), channel_id=1, source_target_pairs={{0,2},{1,3},{2,0},{3,1},{4,6},{5,7},{6,4},{7,5},{8,10},{9,11},{10,... | collective-permute-start | bytes 196616 | tf_op jit(solution)/shard_map/ppermute | solution.py:20
  24.8 7.7 %collective-permute-start.8 = (bf16[64,512]{1,0:T(8,128)(2,1)S(1)}, bf16[64,512]{1,0:T(8,128)(2,1)S(1)}, u32[]{:S(2)}, u32[]{:S(2)}) collective-permute-start(bf16[64,512]{1,0:T(8,128)(2,1)S(1)} %get-tuple-element.44), channel_id=1, source_target_pairs={{0,4},{1,5},{2,6},{3,7},{4,0},{5,1},{6,2},{7,3},{8,12},{9,13},{10,... | collective-permute-start | bytes 196616 | tf_op jit(solution)/shard_map/ppermute | solution.py:20
  27.4 6.1 %collective-permute-start.9 = (bf16[64,512]{1,0:T(8,128)(2,1)S(1)}, bf16[64,512]{1,0:T(8,128)(2,1)S(1)}, u32[]{:S(2)}, u32[]{:S(2)}) collective-permute-start(bf16[64,512]{1,0:T(8,128)(2,1)S(1)} %get-tuple-element.45), channel_id=1, source_target_pairs={{0,6},{1,7},{2,4},{3,5},{4,2},{5,3},{6,0},{7,1},{8,14},{9,15},{10,... | collective-permute-start | bytes 196616 | tf_op jit(solution)/shard_map/ppermute | solution.py:20
  33.6 6.2 %collective-permute-start.12 = (bf16[64,512]{1,0:T(8,128)(2,1)S(1)}, bf16[64,512]{1,0:T(8,128)(2,1)S(1)}, u32[]{:S(2)}, u32[]{:S(2)}) collective-permute-start(bf16[64,512]{1,0:T(8,128)(2,1)S(1)} %get-tuple-element.46.refs_5_), channel_id=1, source_target_pairs={{0,6},{1,7},{2,4},{3,5},{4,2},{5,3},{6,0},{7,1},{8,14},{9,15},{10,... | collective-permute-start | bytes 196616 | tf_op jit(solution)/shard_map/ppermute | solution.py:20
  36.0 9.2 %collective-permute-start.6 = (bf16[64,1024]{1,0:T(8,128)(2,1)S(1)}, bf16[64,1024]{1,0:T(8,128)(2,1)S(1)}, u32[]{:S(2)}, u32[]{:S(2)}) collective-permute-start(bf16[64,1024]{1,0:T(8,128)(2,1)S(1)} %get-tuple-element.40.refs_0_), channel_id=1, source_target_pairs={{0,24},{8,16},{16,8},{24,0},{1,25},{9,17},{17,9},{25,1},{2,26},{10... | collective-permute-start | bytes 393224 | tf_op jit(solution)/shard_map/ppermute | solution.py:20
  36.7 8.5 %collective-permute-start.5 = (bf16[64,1024]{1,0:T(8,128)(2,1)S(1)}, bf16[64,1024]{1,0:T(8,128)(2,1)S(1)}, u32[]{:S(2)}, u32[]{:S(2)}) collective-permute-start(bf16[64,1024]{1,0:T(8,128)(2,1)S(1)} %get-tuple-element.40.refs_0_), channel_id=1, source_target_pairs={{0,16},{8,24},{16,0},{24,8},{1,17},{9,25},{17,1},{25,9},{2,18},{10... | collective-permute-start | bytes 393224 | tf_op jit(solution)/shard_map/ppermute | solution.py:20
  38.0 7.2 %collective-permute-start.4 = (bf16[64,1024]{1,0:T(8,128)(2,1)S(1)}, bf16[64,1024]{1,0:T(8,128)(2,1)S(1)}, u32[]{:S(2)}, u32[]{:S(2)}) collective-permute-start(bf16[64,1024]{1,0:T(8,128)(2,1)S(1)} %get-tuple-element.40.refs_0_), channel_id=1, source_target_pairs={{0,8},{8,0},{16,24},{24,16},{1,9},{9,1},{17,25},{25,17},{2,10},{10... | collective-permute-start | bytes 393224 | tf_op jit(solution)/shard_map/ppermute | solution.py:20
  39.5 5.7 %collective-permute-start.11 = (bf16[64,512]{1,0:T(8,128)(2,1)S(1)}, bf16[64,512]{1,0:T(8,128)(2,1)S(1)}, u32[]{:S(2)}, u32[]{:S(2)}) collective-permute-start(bf16[64,512]{1,0:T(8,128)(2,1)S(1)} %get-tuple-element.46.refs_5_), channel_id=1, source_target_pairs={{0,4},{1,5},{2,6},{3,7},{4,0},{5,1},{6,2},{7,3},{8,12},{9,13},{10,... | collective-permute-start | bytes 196616 | tf_op jit(solution)/shard_map/ppermute | solution.py:20
  39.8 5.3 %collective-permute-start.10 = (bf16[64,512]{1,0:T(8,128)(2,1)S(1)}, bf16[64,512]{1,0:T(8,128)(2,1)S(1)}, u32[]{:S(2)}, u32[]{:S(2)}) collective-permute-start(bf16[64,512]{1,0:T(8,128)(2,1)S(1)} %get-tuple-element.46.refs_5_), channel_id=1, source_target_pairs={{0,2},{1,3},{2,0},{3,1},{4,6},{5,7},{6,4},{7,5},{8,10},{9,11},{10,... | collective-permute-start | bytes 196616 | tf_op jit(solution)/shard_map/ppermute | solution.py:20
  45.3 1.6 %collective-permute-start.13 = (bf16[64,2048]{1,0:T(8,128)(2,1)S(1)}, bf16[64,2048]{1,0:T(8,128)(2,1)S(1)}, u32[]{:S(2)}, u32[]{:S(2)}) collective-permute-start(bf16[64,2048]{1,0:T(8,128)(2,1)S(1)} %get-tuple-element.47.user_half), channel_id=1, source_target_pairs={{0,1},{1,0},{2,3},{3,2},{4,5},{5,4},{6,7},{7,6},{8,9},{9,8},{10,11... | collective-permute-start | bytes 786440 | tf_op jit(solution)/shard_map/ppermute | solution.py:20
  50.3 2.0 %collective-permute-start.14 = (bf16[64,2048]{1,0:T(8,128)(2,1)S(1)}, bf16[64,2048]{1,0:T(8,128)(2,1)S(1)}, u32[]{:S(2)}, u32[]{:S(2)}) collective-permute-start(bf16[64,2048]{1,0:T(8,128)(2,1)S(1)} %get-tuple-element.55), channel_id=1, source_target_pairs={{0,1},{1,0},{2,3},{3,2},{4,5},{5,4},{6,7},{7,6},{8,9},{9,8},{10,11... | collective-permute-start | bytes 786440 | tf_op jit(solution)/shard_map/ppermute | solution.py:20
  53.5 5.1 %collective-permute-start.15 = (bf16[64,512]{1,0:T(8,128)(2,1)S(1)}, bf16[64,512]{1,0:T(8,128)(2,1)S(1)}, u32[]{:S(2)}, u32[]{:S(2)}) collective-permute-start(bf16[64,512]{1,0:T(8,128)(2,1)S(1)} %get-tuple-element.57), channel_id=1, source_target_pairs={{0,2},{1,3},{2,0},{3,1},{4,6},{5,7},{6,4},{7,5},{8,10},{9,11},{10,... | collective-permute-start | bytes 196616 | tf_op jit(solution)/shard_map/ppermute | solution.py:20
  54.2 8.5 %collective-permute-start.16 = (bf16[64,512]{1,0:T(8,128)(2,1)S(1)}, bf16[64,512]{1,0:T(8,128)(2,1)S(1)}, u32[]{:S(2)}, u32[]{:S(2)}) collective-permute-start(bf16[64,512]{1,0:T(8,128)(2,1)S(1)} %get-tuple-element.58), channel_id=1, source_target_pairs={{0,4},{1,5},{2,6},{3,7},{4,0},{5,1},{6,2},{7,3},{8,12},{9,13},{10,... | collective-permute-start | bytes 196616 | tf_op jit(solution)/shard_map/ppermute | solution.py:20
  56.1 6.6 %collective-permute-start.17 = (bf16[64,512]{1,0:T(8,128)(2,1)S(1)}, bf16[64,512]{1,0:T(8,128)(2,1)S(1)}, u32[]{:S(2)}, u32[]{:S(2)}) collective-permute-start(bf16[64,512]{1,0:T(8,128)(2,1)S(1)} %get-tuple-element.59), channel_id=1, source_target_pairs={{0,6},{1,7},{2,4},{3,5},{4,2},{5,3},{6,0},{7,1},{8,14},{9,15},{10,... | collective-permute-start | bytes 196616 | tf_op jit(solution)/shard_map/ppermute | solution.py:20
  62.7 6.8 %collective-permute-start.20 = (bf16[64,512]{1,0:T(8,128)(2,1)S(1)}, bf16[64,512]{1,0:T(8,128)(2,1)S(1)}, u32[]{:S(2)}, u32[]{:S(2)}) collective-permute-start(bf16[64,512]{1,0:T(8,128)(2,1)S(1)} %shard_map.59.refs_0_), channel_id=1, source_target_pairs={{0,6},{1,7},{2,4},{3,5},{4,2},{5,3},{6,0},{7,1},{8,14},{9,15},{10,... | collective-permute-start | bytes 196616 | tf_op jit(solution)/shard_map/ppermute | solution.py:20
  65.0 6.0 %collective-permute-start.19 = (bf16[64,512]{1,0:T(8,128)(2,1)S(1)}, bf16[64,512]{1,0:T(8,128)(2,1)S(1)}, u32[]{:S(2)}, u32[]{:S(2)}) collective-permute-start(bf16[64,512]{1,0:T(8,128)(2,1)S(1)} %shard_map.59.refs_0_), channel_id=1, source_target_pairs={{0,4},{1,5},{2,6},{3,7},{4,0},{5,1},{6,2},{7,3},{8,12},{9,13},{10,... | collective-permute-start | bytes 196616 | tf_op jit(solution)/shard_map/ppermute | solution.py:20
  65.6 5.3 %collective-permute-start.18 = (bf16[64,512]{1,0:T(8,128)(2,1)S(1)}, bf16[64,512]{1,0:T(8,128)(2,1)S(1)}, u32[]{:S(2)}, u32[]{:S(2)}) collective-permute-start(bf16[64,512]{1,0:T(8,128)(2,1)S(1)} %shard_map.59.refs_0_), channel_id=1, source_target_pairs={{0,2},{1,3},{2,0},{3,1},{4,6},{5,7},{6,4},{7,5},{8,10},{9,11},{10,... | collective-permute-start | bytes 196616 | tf_op jit(solution)/shard_map/ppermute | solution.py:20
  71.0 6.9 %collective-permute-start.21 = (bf16[64,2048]{1,0:T(8,128)(2,1)S(1)}, bf16[64,2048]{1,0:T(8,128)(2,1)S(1)}, u32[]{:S(2)}, u32[]{:S(2)}) collective-permute-start(bf16[64,2048]{1,0:T(8,128)(2,1)S(1)} %shard_map.60.own), channel_id=1, source_target_pairs={{0,1},{1,0},{2,3},{3,2},{4,5},{5,4},{6,7},{7,6},{8,9},{9,8},{10,11... | collective-permute-start | bytes 786440 | tf_op jit(solution)/shard_map/ppermute | solution.py:20
  71.0 4.0 %collective-permute-start.22 = (bf16[64,256]{1,0:T(8,128)(2,1)S(1)}, bf16[64,256]{1,0:T(8,128)(2,1)S(1)}, u32[]{:S(2)}, u32[]{:S(2)}) collective-permute-start(bf16[64,256]{1,0:T(8,128)(2,1)S(1)} %get-tuple-element.63), channel_id=1, source_target_pairs={{0,8},{8,0},{16,24},{24,16},{1,9},{9,1},{17,25},{25,17},{2,10},{10... | collective-permute-start | bytes 98312 | tf_op jit(solution)/shard_map/ppermute | solution.py:20
  71.6 3.9 %collective-permute-start.23 = (bf16[64,256]{1,0:T(8,128)(2,1)S(1)}, bf16[64,256]{1,0:T(8,128)(2,1)S(1)}, u32[]{:S(2)}, u32[]{:S(2)}) collective-permute-start(bf16[64,256]{1,0:T(8,128)(2,1)S(1)} %get-tuple-element.64), channel_id=1, source_target_pairs={{0,16},{8,24},{16,0},{24,8},{1,17},{9,25},{17,1},{25,9},{2,18},{10... | collective-permute-start | bytes 98312 | tf_op jit(solution)/shard_map/ppermute | solution.py:20
  72.4 4.8 %collective-permute-start.24 = (bf16[64,256]{1,0:T(8,128)(2,1)S(1)}, bf16[64,256]{1,0:T(8,128)(2,1)S(1)}, u32[]{:S(2)}, u32[]{:S(2)}) collective-permute-start(bf16[64,256]{1,0:T(8,128)(2,1)S(1)} %get-tuple-element.65), channel_id=1, source_target_pairs={{0,24},{8,16},{16,8},{24,0},{1,25},{9,17},{17,9},{25,1},{2,26},{10... | collective-permute-start | bytes 98312 | tf_op jit(solution)/shard_map/ppermute | solution.py:20

commit v2 on v0

v2 whole, which is shorter than its diff:
```python
import functools
import math

import jax
import jax.numpy as jnp
from jax import lax
from jax.experimental import pallas as pl
from jax.experimental.pallas import tpu as pltpu
from jax.sharding import PartitionSpec as P

CORES = 2
TILE_USERS = 1024
TILE_ITEMS = 512

f32, bf16 = jnp.float32, jnp.bfloat16
VMEM, ANY = pltpu.VMEM, pl.ANY


def swap(block, axis, distance):
    return lax.ppermute(block, axis, [(i, i ^ distance) for i in range(lax.axis_size(axis))])


def tree_sum(terms):
    while len(terms) > 1:
        terms = [terms[i] + terms[i + 1] for i in range(0, len(terms), 2)]
    return terms[0]


def span(index, width):
    return pl.ds(pl.multiple_of(index * width, width), width)


def call(kernel, outs, *args, scratch=(), flops=0, space=VMEM):
    return pl.pallas_call(
        kernel,
        in_specs=[pl.BlockSpec(memory_space=space)] * len(args),
        out_specs=[pl.BlockSpec(memory_space=VMEM)] * len(outs),
        out_shape=[jax.ShapeDtypeStruct(s, d) for s, d in outs],
        scratch_shapes=list(scratch),
        compiler_params=pltpu.CompilerParams(vmem_limit_bytes=24 << 20),
        cost_estimate=pl.CostEstimate(flops=flops, bytes_accessed=1 << 20, transcendentals=0),
    )(*args)


def place():
    col = lax.axis_index("col")
    return lax.axis_index("row"), col // CORES, col % CORES


def group_start(own, near, half):
    _, z, core = place()
    quarter = half // 2
    upper = z // (lax.axis_size("col") // CORES // 2)
    core = core if own else 1 - core
    upper = upper if near else 1 - upper
    return pl.multiple_of(core * half + upper * quarter, quarter)


def row_tiles(items_dev, block, everything):
    if everything:
        tile = min(TILE_ITEMS, items_dev)
        return [(at, tile) for at in range(0, items_dev, tile)]
    row, tiles, size = lax.axis_index("row"), [], 1
    while size * block < items_dev:
        tiles.append((pl.multiple_of(((row // size) ^ 1) * (size * block), size * block), size * block))
        size *= 2
    return tiles


def gradients(tiles, start, width, user_of, item, item_t, labels, grad_item, keep):
    tile_users = min(TILE_USERS, width)
    for at in range(0, width, tile_users):
        here = pl.ds(pl.multiple_of(start + at, tile_users), tile_users)
        user = user_of(at, tile_users)
        total = None
        for first, size in tiles:
            rows = pl.ds(first, size)
            half_scores = jnp.dot(item_t[rows, :], user, preferred_element_type=f32)
            weights = labels[rows, here].astype(f32)
            residual = (jnp.abs(weights) * jnp.tanh(half_scores) - weights).astype(bf16)
            term = jnp.dot(item[:, rows], residual, preferred_element_type=f32)
            total = term if total is None else total + term
            grad_item[:, rows] += lax.dot_general(
                user, residual, (((1,), (1,)), ((), ())), preferred_element_type=f32
            )
        keep(at, tile_users, total)


def put_items(value, item, item_t):
    rounded = value.astype(bf16)
    item[...] = rounded
    item_t[...] = (rounded * jnp.asarray(0.5, bf16)).T


def load_and_own_rows(rows_count, labels_hbm, users_hbm, items_hbm, labels, users, items, grad_user, grad_item, item, item_t, sems):
    row, block = lax.axis_index("row"), items.shape[1]

    def rows_of(o):
        at = span(row ^ o, block)
        return pltpu.make_async_copy(labels_hbm.at[at, :], labels.at[at, :], sems.at[2 + o])

    copies = [
        pltpu.make_async_copy(items_hbm, items, sems.at[0]),
        pltpu.make_async_copy(users_hbm, users, sems.at[1]),
    ] + [rows_of(o) for o in range(rows_count)]
    for copy in copies:
        copy.start()
    copies[0].wait()
    own = span(row, block)
    put_items(items[...], item, item_t)
    grad_item[...] = jnp.zeros_like(grad_item)
    copies[1].wait()
    copies[2].wait()
    width = users.shape[1]
    tile = min(TILE_USERS, width)
    for at in range(0, width, tile):
        here = pl.ds(at, tile)
        user = users[:, here].astype(bf16)
        half_scores = jnp.dot(item_t[...], user, preferred_element_type=f32)
        weights = labels[own, here].astype(f32)
        residual = (jnp.abs(weights) * jnp.tanh(half_scores) - weights).astype(bf16)
        grad_user[:, here] = jnp.dot(item[...], residual, preferred_element_type=f32)
        grad_item[:, own] += lax.dot_general(user, residual, (((1,), (1,)), ((), ())), preferred_element_type=f32)
    for copy in copies[3:]:
        copy.wait()


def first_open(rows_count, half, *refs):
    blocks = refs[:rows_count]
    users, labels, grad_user, grad_in = refs[rows_count : rows_count + 4]
    send, grad_item, item_all, item, item_t = refs[rows_count + 4 :]
    row, block = lax.axis_index("row"), blocks[0].shape[1]
    for o, values in enumerate(blocks):
        item_all[:, span(row ^ o, block)] = values[...]
    put_items(item_all[...], item, item_t)
    first_group(False, False, half, block, users, labels, grad_user, item, item_t, grad_in, send, grad_item)


def first_group(own, near, half, block, users, labels, grad_user, item, item_t, grad_in, out, grad_item):
    start = group_start(own, near, half)
    grad_item[...] = grad_in[...]

    def columns(at, width):
        return pl.ds(pl.multiple_of(start + at, width), width)

    def keep(at, width, total):
        out[:, pl.ds(at, width)] = (total + grad_user[:, columns(at, width)]).astype(out.dtype)

    gradients(
        row_tiles(labels.shape[0], block, False), start, half // 2,
        lambda at, width: users[:, columns(at, width)].astype(bf16),
        item, item_t, labels, grad_item, keep,
    )


def second_group(own, near, half, user_half, labels, item, item_t, grad_in, out, grad_item):
    quarter = half // 2
    start = group_start(own, near, half)
    if grad_in is None:
        grad_item[...] = jnp.zeros_like(grad_item)
    else:
        grad_item[...] = grad_in[...]
    within = lax.rem(start, half)

    def keep(at, width, total):
        out[:, pl.ds(at, width)] = total.astype(out.dtype)

    gradients(
        row_tiles(labels.shape[0], None, True), start, quarter,
        lambda at, width: user_half[:, pl.ds(pl.multiple_of(within + at, width), width)],
        item, item_t, labels, grad_item, keep,
    )


def second_open(near, half, user_half, labels, item, item_t, out, grad_item):
    second_group(True, near, half, user_half, labels, item, item_t, None, out, grad_item)


def combine_far(share, kept, recv, *outs):
    _, z, _ = place()
    far = len(outs)
    for i, out in enumerate(outs):
        at = span(lax.rem(z ^ (far + i), far), share)
        out[...] = (kept[:, at] + recv[:, at].astype(f32)).astype(bf16)


def combine_near(share, kept, recv, own, *outs):
    _, z, _ = place()
    near = len(outs) + 1
    for o in range(near):
        at = span(lax.rem(z ^ o, near), share)
        piece = kept[:, at] + recv[:, at].astype(f32)
        if o == 0:
            own[...] = piece
        else:
            outs[o - 1][...] = piece.astype(bf16)


def combine_near_round(share, kept, recv, grad_item, grad_b, *outs):
    grad_b[...] = grad_item[...].astype(bf16)
    combine_near(share, kept, recv, *outs)


def combine_near_cut(share, rows_count, kept, recv, grad_item, *outs):
    row, block = lax.axis_index("row"), outs[0].shape[1]
    for o in range(rows_count):
        outs[o][...] = grad_item[:, span(row ^ o, block)].astype(outs[o].dtype)
    combine_near(share, kept, recv, *outs[rows_count:])


def share_at(half, share):
    _, z, core = place()
    return pl.ds(pl.multiple_of(core * half + z * share, share), share)


def update_share(rate, half, share, own, *refs):
    recvs, (users, new, new_b) = refs[:-3], refs[-3:]
    grad = tree_sum([own[...]] + [r[...].astype(f32) for r in recvs])
    new[...] = users[:, share_at(half, share)] - rate * grad
    new_b[...] = new[...].astype(bf16)


def update_last(rate, half, share, own, *refs):
    recvs, (users, new, delta_b) = refs[:-3], refs[-3:]
    grad = tree_sum([own[...]] + [r[...].astype(f32) for r in recvs])
    delta_b[...] = (new[...] - rate * grad - users[:, share_at(half, share)]).astype(bf16)


def second_start(rate, rows_count, item_all, *refs):
    grads, (item_own, item, item_t) = refs[:rows_count], refs[rows_count:]
    new = item_all[...] - rate * tree_sum([g[...].astype(f32) for g in grads])
    put_items(new, item, item_t)
    at = span(lax.axis_index("row"), item_own.shape[1])
    item_own[...] = item_all[:, at] - rate * tree_sum([g[:, at].astype(f32) for g in grads])


def assemble(*refs):
    pieces, user_half = refs[:-1], refs[-1]
    _, z, _ = place()
    for o, piece in enumerate(pieces):
        user_half[:, span(z ^ o, piece.shape[1])] = piece[...]


def finish_items(rate, item, own, *refs):
    recvs, out = refs[:-1], refs[-1]
    out[...] = item[...] - rate * tree_sum([own[...]] + [r[...].astype(f32) for r in recvs])


def finish_users(half, users, own, peer, out):
    _, _, core = place()
    mine, other = span(core, half), span(1 - core, half)
    out[:, mine] = users[:, mine] + own[...].astype(f32)
    out[:, other] = users[:, other] + peer[...].astype(f32)


def body(preference, users, items):
    rows_count, cols_count = lax.axis_size("row"), lax.axis_size("col")
    items_dev, users_dev = preference.shape
    rank, block = items.shape
    chips = cols_count // CORES
    half, share = users_dev // CORES, users_dev // cols_count
    quarter = half // 2
    user_rate = 0.5 / math.sqrt(items_dev * cols_count)
    item_rate = 0.5 / math.sqrt(users_dev * rows_count)
    work = 6 * rank * items_dev * quarter
    wide = ((rank, items_dev), f32)
    item_pair = [((rank, items_dev), bf16), ((items_dev, rank), bf16)]
    sent, kept = ((rank, quarter), bf16), ((rank, quarter), f32)
    piece, piece_b = ((rank, share), f32), ((rank, share), bf16)
    half_b = ((rank, half), bf16)
    near, far = list(range(1, chips // 2)), list(range(chips // 2, chips))
    others = list(range(1, rows_count))

    def along_z(block, o):
        return swap(block, "col", o * CORES)

    item_blocks = [swap(items, "row", o) for o in others]
    labels, users_v, items_v, grad_user, grad = call(
        functools.partial(load_and_own_rows, rows_count),
        [(preference.shape, bf16), (users.shape, f32), (items.shape, f32), (users.shape, f32), wide],
        preference, users, items,
        scratch=[VMEM((rank, block), bf16), VMEM((block, rank), bf16), pltpu.SemaphoreType.DMA((rows_count + 2,))],
        space=ANY, flops=work,
    )
    send, grad, item_all, item, item_t = call(
        functools.partial(first_open, rows_count, half), [sent, wide, wide] + item_pair,
        items_v, *item_blocks, users_v, labels, grad_user, grad, flops=work,
    )

    def first(own, near, grad):
        return call(
            functools.partial(first_group, own, near, half, block), [kept if own else sent, wide],
            users_v, labels, grad_user, item, item_t, grad, flops=work,
        )

    recv = swap(send, "col", 1)
    mine, grad = first(True, False, grad)
    far_pieces = call(functools.partial(combine_far, share), [piece_b] * len(far), mine, recv)
    far_got = [along_z(p, o) for p, o in zip(far_pieces, far)]
    *_, grad = lax.optimization_barrier((*far_pieces, grad))
    send, grad = first(False, True, grad)
    recv = swap(send, "col", 1)
    mine, grad = first(True, True, grad)
    grad_b, own, *near_pieces = call(
        functools.partial(combine_near_round, share), [(wide[0], bf16), piece] + [piece_b] * len(near), mine, recv, grad
    )
    near_got = [along_z(p, o) for p, o in zip(near_pieces, near)]
    grads = [grad_b] + [swap(grad_b, "row", o) for o in others]
    new, new_b = call(
        functools.partial(update_share, user_rate, half, share), [piece, piece_b], own, *near_got, *far_got, users_v
    )
    spread = [new_b] + [along_z(new_b, o) for o in near + far]

    item_own, item, item_t = call(
        functools.partial(second_start, item_rate, rows_count), [(items.shape, f32)] + item_pair, item_all, *grads
    )
    (user_half,) = call(assemble, [half_b], *spread)
    user_peer = swap(user_half, "col", 1)
    far_mine, grad = call(
        functools.partial(second_open, False, half), [kept, wide], user_half, labels, item, item_t, flops=work
    )

    def second(own, near, grad):
        return call(
            functools.partial(second_group, own, near, half), [kept if own else sent, wide],
            user_half if own else user_peer, labels, item, item_t, grad, flops=work,
        )

    send, grad = second(False, False, grad)
    far_recv = swap(send, "col", 1)
    send, grad = second(False, True, grad)
    near_recv = swap(send, "col", 1)
    far_pieces = call(functools.partial(combine_far, share), [piece_b] * len(far), far_mine, far_recv)
    far_got = [along_z(p, o) for p, o in zip(far_pieces, far)]
    *_, grad = lax.optimization_barrier((*far_pieces, grad))
    near_mine, grad = second(True, True, grad)
    outs = call(
        functools.partial(combine_near_cut, share, rows_count),
        [(items.shape, f32)] + [(items.shape, bf16)] * len(others) + [piece] + [piece_b] * len(near),
        near_mine, near_recv, grad,
    )
    item_grad, item_pieces, own, near_pieces = outs[0], outs[1:rows_count], outs[rows_count], outs[rows_count + 1 :]
    near_got = [along_z(p, o) for p, o in zip(near_pieces, near)]
    item_got = [swap(p, "row", o) for p, o in zip(item_pieces, others)]
    (delta,) = call(
        functools.partial(update_last, user_rate, half, share), [piece_b], own, *near_got, *far_got, users_v, new
    )
    spread = [delta] + [along_z(delta, o) for o in near + far]
    (new_items,) = call(
        functools.partial(finish_items, item_rate), [(items.shape, f32)], item_own, item_grad, *item_got
    )
    (delta_half,) = call(assemble, [half_b], *spread)
    delta_peer = swap(delta_half, "col", 1)
    (new_users,) = call(functools.partial(finish_users, half), [(users.shape, f32)], users_v, delta_half, delta_peer)
    return new_users, new_items


def solution(mesh):
    return jax.shard_map(
        body,
        mesh=mesh,
        in_specs=(P("col", "row"), P(None, "row"), P(None, ("col", "row"))),
        out_specs=(P(None, "row"), P(None, ("col", "row"))),
        check_vma=False,
    )
```

time: 183 us -> 81.5 us (0.45)
  waiting for transfers between devices: 107 us -> 26.5 us
  matrix products: 39.1 us -> 0 us
  starting transfers between devices: 10.7 us -> 31.1 us
  Pallas kernels: 0 us -> 17.5 us
  between operations: 14.1 us -> 0.84 us
  other arithmetic: 7.53 us -> 0 us
    reduce_scatter x2 -> x0, waiting for transfers between devices: 63.7 us -> none  [body(): lax.psum_scatter(grad_user, 'col', scatter_dimension=1, tiled=True)]
    dot_general x24 -> x0, matrix products: 39.1 us -> none  [the longest x8 21.2 us: body(): jnp.einsum('kn,km->nm', visitor, user_b, preferred_element_type=jnp.float32)]
    ppermute x14 -> x27, starting transfers between devices: 10.6 us -> 31.1 us  [swap(): lax.ppermute(block, axis, [(i, i ^ distance) for i in range(lax.axis_size...]
    pallas_call x0 -> x20, Pallas kernels: none -> 17.5 us  [call(): pl.pallas_call(kernel, in_specs=[pl.BlockSpec(memory_space=space)] * len(...]
    ppermute x14 -> x27, waiting for transfers between devices: 43.7 us -> 26.5 us  [swap(): lax.ppermute(block, axis, [(i, i ^ distance) for i in range(lax.axis_size...]
    sub x3 -> x0, other arithmetic: 3.93 us -> none  [the longest x2 3.29 us: body(): own_users - user_rate * user_share]
    convert_element_type x4 -> x0, other arithmetic: 3.56 us -> none  [the longest x2 2.71 us: body(): user_b = users.astype(jnp.bfloat16)]
    unnamed x27 -> x6, local copies, waits for them, and re-layouts: 3.69 us -> 5.44 us
  transfers between devices with their start and end apart: 18 -> 27, of which waited for: 12 -> 15; matrix products, arithmetic and copies ran while one was open for 19% -> 0% of each run, Pallas kernels for 0% -> 14%
where the time goes in v2:
time: 81.5 us; the launch traced here: 81.3 us
  starting transfers between devices  31.1 us (38%)
  waiting for transfers between devices  26.5 us (33%)
  Pallas kernels  17.5 us (21%)
  local copies, waits for them, and re-layouts  5.44 us (7%)
  between operations  0.84 us (1%)
    ppermute x27, starting transfers between devices, swap(): lax.ppermute(block, axis, [(i, i ^ distance) for i in range(lax.axis_size...  31.1 us
    ppermute x27, waiting for transfers between devices, swap(): lax.ppermute(block, axis, [(i, i ^ distance) for i in range(lax.axis_size...  26.5 us
    pallas_call x20, Pallas kernels, call(): pl.pallas_call(kernel, in_specs=[pl.BlockSpec(memory_space=space)] * len(...  17.5 us
    unnamed x6, local copies, waits for them, and re-layouts  5.44 us
  transfers between devices with their start and end apart: 27, of which 15 were waited for; matrix products, arithmetic and copies ran while one was open for 0% of the time, Pallas kernels for 14%

profile of v2, /device:TPU:0, one launch (start us, length us, event | category | flops | bytes accessed | tf_op | source)
XLA Modules:
  0.0 81.3 jit_solution(9001666636113787470)
XLA Ops:
  0.6 3.0 %collective-permute-start = (f32[64,256]{1,0:T(8,128)}, f32[64,256]{1,0:T(8,128)S(1)}, u32[]{:S(2)}, u32[]{:S(2)}) collective-permute-start(f32[64,256]{1,0:T(8,128)} %items_hbm.1), channel_id=1, source_target_pairs={{0,8},{8,0},{16,24},{24,16},{1,9},{9,1},{17,25},{25,17},{2,10},{10... | collective-permute-start | bytes 196616 | tf_op jit(solution)/shard_map/ppermute | solution.py:20
  3.6 1.5 %collective-permute-start.2 = (f32[64,256]{1,0:T(8,128)}, f32[64,256]{1,0:T(8,128)S(1)}, u32[]{:S(2)}, u32[]{:S(2)}) collective-permute-start(f32[64,256]{1,0:T(8,128)} %items_hbm.1), channel_id=1, source_target_pairs={{0,24},{8,16},{16,8},{24,0},{1,25},{9,17},{17,9},{25,1},{2,26},{10... | collective-permute-start | bytes 196616 | tf_op jit(solution)/shard_map/ppermute | solution.py:20
  5.2 3.4 %copy-done = bf16[1024,4096]{1,0:T(8,128)(2,1)S(1)} copy-done((bf16[1024,4096]{1,0:T(8,128)(2,1)S(1)}, bf16[1024,4096]{1,0:T(8,128)(2,1)}, u32[]{:S(2)}) %copy-start) | copy-done | bytes 8388632
  8.6 1.2 %copy-done.1 = f32[64,4096]{1,0:T(8,128)S(1)} copy-done((f32[64,4096]{1,0:T(8,128)S(1)}, f32[64,4096]{1,0:T(8,128)}, u32[]{:S(2)}) %copy-start.1) | copy-done | bytes 1048600
  9.8 0.8 %copy-done.2 = f32[64,256]{1,0:T(8,128)S(1)} copy-done((f32[64,256]{1,0:T(8,128)S(1)}, f32[64,256]{1,0:T(8,128)}, u32[]{:S(2)}) %copy-start.2) | copy-done | bytes 65560
  10.6 2.8 %shard_map.50 = (bf16[1024,4096]{1,0:T(8,128)(2,1)S(1)}, f32[64,4096]{1,0:T(8,128)S(1)}, f32[64,256]{1,0:T(8,128)S(1)}, f32[64,4096]{1,0:T(8,128)S(1)}, f32[64,1024]{1,0:T(8,128)S(1)}) custom-call(bf16[1024,4096]{1,0:T(8,128)(2,1)S(1)} %copy-done, f32[64,4096]{1,0:T(8,128)S(1)} %copy-done.1, f32[64,256]{1,0:T(8,128)S(1)} %copy-done.2), custom_call_target="tpu_custom_call" | custom-call | flops 402653184 | bytes 1048576 | tf_op jit(solution)/shard_map/pallas_call | solution.py:34
  13.5 1.4 %shard_map.51 = (bf16[64,1024]{1,0:T(8,128)(2,1)S(1)}, f32[64,1024]{1,0:T(8,128)S(1)}, f32[64,1024]{1,0:T(8,128)S(1)}, bf16[64,1024]{1,0:T(8,128)(2,1)S(1)}, bf16[1024,64]{1,0:T(8,128)(2,1)S(1)}) custom-call(f32[64,256]{1,0:T(8,128)S(1)} %get-tuple-element.49.refs_0_, f32[64,256]{1,0:T(8,128)S(1)} %collective-permute-done.refs_1_, ...), custom_call_target="tpu_custom_call" | custom-call | flops 402653184 | bytes 1048576 | tf_op jit(solution)/shard_map/pallas_call | solution.py:34
  15.0 1.3 %shard_map.52 = (f32[64,1024]{1,0:T(8,128)S(1)}, f32[64,1024]{1,0:T(8,128)S(1)}) custom-call(f32[64,4096]{1,0:T(8,128)S(1)} %get-tuple-element.46.refs_4_.users.refs_3_, bf16[1024,4096]{1,0:T(8,128)(2,1)S(1)} %get-tuple-element.47.refs_5_.labels, f32[64,4096]{1,0:T(8,128)S(1)} %get-tuple-element.48.refs_6_.grad_user, ...), custom_call_target="tpu_custom_call" | custom-call | flops 402653184 | bytes 1048576 | tf_op jit(solution)/shard_map/pallas_call | solution.py:34
  16.4 1.3 %shard_map.54 = (bf16[64,1024]{1,0:T(8,128)(2,1)S(1)}, f32[64,1024]{1,0:T(8,128)S(1)}) custom-call(f32[64,4096]{1,0:T(8,128)S(1)} %get-tuple-element.46.refs_4_.users.refs_3_, bf16[1024,4096]{1,0:T(8,128)(2,1)S(1)} %get-tuple-element.47.refs_5_.labels, f32[64,4096]{1,0:T(8,128)S(1)} %get-tuple-element.48.refs_6_.grad_user, ...), custom_call_target="tpu_custom_call" | custom-call | flops 402653184 | bytes 1048576 | tf_op jit(solution)/shard_map/pallas_call | solution.py:34
  17.7 0.5 collective-permute-start.4
  18.2 3.0 %collective-permute-start.6 = (bf16[64,512]{1,0:T(8,128)(2,1)S(1)}, bf16[64,512]{1,0:T(8,128)(2,1)S(1)}, u32[]{:S(2)}, u32[]{:S(2)}) collective-permute-start(bf16[64,512]{1,0:T(8,128)(2,1)S(1)} %get-tuple-element.56), channel_id=1, source_target_pairs={{0,4},{1,5},{2,6},{3,7},{4,0},{5,1},{6,2},{7,3},{8,12},{9,13},{10,... | collective-permute-start | bytes 196616 | tf_op jit(solution)/shard_map/ppermute | solution.py:20
  21.3 1.3 %collective-permute-start.7 = (bf16[64,512]{1,0:T(8,128)(2,1)S(1)}, bf16[64,512]{1,0:T(8,128)(2,1)S(1)}, u32[]{:S(2)}, u32[]{:S(2)}) collective-permute-start(bf16[64,512]{1,0:T(8,128)(2,1)S(1)} %get-tuple-element.57), channel_id=1, source_target_pairs={{0,6},{1,7},{2,4},{3,5},{4,2},{5,3},{6,0},{7,1},{8,14},{9,15},{10,... | collective-permute-start | bytes 196616 | tf_op jit(solution)/shard_map/ppermute | solution.py:20
  22.6 1.3 %shard_map.55 = (f32[64,1024]{1,0:T(8,128)S(1)}, f32[64,1024]{1,0:T(8,128)S(1)}) custom-call(f32[64,4096]{1,0:T(8,128)S(1)} %get-tuple-element.46.refs_4_.users.refs_3_, bf16[1024,4096]{1,0:T(8,128)(2,1)S(1)} %get-tuple-element.47.refs_5_.labels, f32[64,4096]{1,0:T(8,128)S(1)} %get-tuple-element.48.refs_6_.grad_user, ...), custom_call_target="tpu_custom_call" | custom-call | flops 402653184 | bytes 1048576 | tf_op jit(solution)/shard_map/pallas_call | solution.py:34
  24.3 0.8 %collective-permute-done.6.refs_1_ = bf16[64,512]{1,0:T(8,128)(2,1)S(1)} collective-permute-done((bf16[64,512]{1,0:T(8,128)(2,1)S(1)}, bf16[64,512]{1,0:T(8,128)(2,1)S(1)}, u32[]{:S(2)}, u32[]{:S(2)}) %collective-permute-start.6) | collective-permute-done | bytes 65568 | tf_op jit(solution)/shard_map/ppermute | solution.py:20
  25.1 2.4 %collective-permute-done.7.refs_2_ = bf16[64,512]{1,0:T(8,128)(2,1)S(1)} collective-permute-done((bf16[64,512]{1,0:T(8,128)(2,1)S(1)}, bf16[64,512]{1,0:T(8,128)(2,1)S(1)}, u32[]{:S(2)}, u32[]{:S(2)}) %collective-permute-start.7) | collective-permute-done | bytes 65568 | tf_op jit(solution)/shard_map/ppermute | solution.py:20
  27.5 0.9 %collective-permute-done.5.refs_0_ = bf16[64,512]{1,0:T(8,128)(2,1)S(1)} collective-permute-done((bf16[64,512]{1,0:T(8,128)(2,1)S(1)}, bf16[64,512]{1,0:T(8,128)(2,1)S(1)}, u32[]{:S(2)}, u32[]{:S(2)}) %collective-permute-start.5) | collective-permute-done | bytes 65568 | tf_op jit(solution)/shard_map/ppermute | solution.py:20
  28.4 3.1 %collective-permute-start.10 = (bf16[64,512]{1,0:T(8,128)(2,1)S(1)}, bf16[64,512]{1,0:T(8,128)(2,1)S(1)}, u32[]{:S(2)}, u32[]{:S(2)}) collective-permute-start(bf16[64,512]{1,0:T(8,128)(2,1)S(1)} %get-tuple-element.66.refs_0_), channel_id=1, source_target_pairs={{0,6},{1,7},{2,4},{3,5},{4,2},{5,3},{6,0},{7,1},{8,14},{9,15},{10,... | collective-permute-start | bytes 196616 | tf_op jit(solution)/shard_map/ppermute | solution.py:20
  31.5 1.4 %collective-permute-start.8 = (bf16[64,512]{1,0:T(8,128)(2,1)S(1)}, bf16[64,512]{1,0:T(8,128)(2,1)S(1)}, u32[]{:S(2)}, u32[]{:S(2)}) collective-permute-start(bf16[64,512]{1,0:T(8,128)(2,1)S(1)} %get-tuple-element.66.refs_0_), channel_id=1, source_target_pairs={{0,2},{1,3},{2,0},{3,1},{4,6},{5,7},{6,4},{7,5},{8,10},{9,11},{10,... | collective-permute-start | bytes 196616 | tf_op jit(solution)/shard_map/ppermute | solution.py:20
  32.9 2.3 %collective-permute-done.10.refs_3_ = bf16[64,512]{1,0:T(8,128)(2,1)S(1)} collective-permute-done((bf16[64,512]{1,0:T(8,128)(2,1)S(1)}, bf16[64,512]{1,0:T(8,128)(2,1)S(1)}, u32[]{:S(2)}, u32[]{:S(2)}) %collective-permute-start.10) | collective-permute-done | bytes 65568 | tf_op jit(solution)/shard_map/ppermute | solution.py:20
  35.2 2.1 %collective-permute-done.9.refs_2_ = bf16[64,512]{1,0:T(8,128)(2,1)S(1)} collective-permute-done((bf16[64,512]{1,0:T(8,128)(2,1)S(1)}, bf16[64,512]{1,0:T(8,128)(2,1)S(1)}, u32[]{:S(2)}, u32[]{:S(2)}) %collective-permute-start.9) | collective-permute-done | bytes 65568 | tf_op jit(solution)/shard_map/ppermute | solution.py:20
  37.4 2.5 %collective-permute-start.13 = (bf16[64,1024]{1,0:T(8,128)(2,1)S(1)}, bf16[64,1024]{1,0:T(8,128)(2,1)S(1)}, u32[]{:S(2)}, u32[]{:S(2)}) collective-permute-start(bf16[64,1024]{1,0:T(8,128)(2,1)S(1)} %get-tuple-element.68.refs_0_), channel_id=1, source_target_pairs={{0,24},{8,16},{16,8},{24,0},{1,25},{9,17},{17,9},{25,1},{2,26},{10... | collective-permute-start | bytes 393224 | tf_op jit(solution)/shard_map/ppermute | solution.py:20
  39.9 0.5 collective-permute-start.12
  40.4 0.6 collective-permute-start.11
  41.0 3.6 %collective-permute-done.13.refs_3_ = bf16[64,1024]{1,0:T(8,128)(2,1)S(1)} collective-permute-done((bf16[64,1024]{1,0:T(8,128)(2,1)S(1)}, bf16[64,1024]{1,0:T(8,128)(2,1)S(1)}, u32[]{:S(2)}, u32[]{:S(2)}) %collective-permute-start.13) | collective-permute-done | bytes 131104 | tf_op jit(solution)/shard_map/ppermute | solution.py:20
  44.5 2.5 %collective-permute-done.12.refs_2_ = bf16[64,1024]{1,0:T(8,128)(2,1)S(1)} collective-permute-done((bf16[64,1024]{1,0:T(8,128)(2,1)S(1)}, bf16[64,1024]{1,0:T(8,128)(2,1)S(1)}, u32[]{:S(2)}, u32[]{:S(2)}) %collective-permute-start.12) | collective-permute-done | bytes 131104 | tf_op jit(solution)/shard_map/ppermute | solution.py:20
  47.3 1.8 %shard_map.60 = (f32[64,1024]{1,0:T(8,128)S(1)}, f32[64,1024]{1,0:T(8,128)S(1)}) custom-call(bf16[64,2048]{1,0:T(8,128)(2,1)S(1)} %shard_map.58.user_half, bf16[1024,4096]{1,0:T(8,128)(2,1)S(1)} %get-tuple-element.47.refs_5_.labels, bf16[64,1024]{1,0:T(8,128)(2,1)S(1)} %get-tuple-element.69.item, bf16[1024,64]{1,0:T(8,128)(2,1)S(1)} %get-tuple-element.70.item_t), custom_call_target="tpu_custom_call" | custom-call | flops 402653184 | bytes 1048576 | tf_op jit(solution)/shard_map/pallas_call | solution.py:34
  49.1 1.8 %shard_map.61 = (bf16[64,1024]{1,0:T(8,128)(2,1)S(1)}, f32[64,1024]{1,0:T(8,128)S(1)}) custom-call(bf16[64,2048]{1,0:T(8,128)(2,1)S(1)} %collective-permute-done.14.user_half, bf16[1024,4096]{1,0:T(8,128)(2,1)S(1)} %get-tuple-element.47.refs_5_.labels, bf16[64,1024]{1,0:T(8,128)(2,1)S(1)} %get-tuple-element.69.item, ...), custom_call_target="tpu_custom_call" | custom-call | flops 402653184 | bytes 1048576 | tf_op jit(solution)/shard_map/pallas_call | solution.py:34
  50.9 1.8 %shard_map.63 = (bf16[64,1024]{1,0:T(8,128)(2,1)S(1)}, f32[64,1024]{1,0:T(8,128)S(1)}) custom-call(bf16[64,2048]{1,0:T(8,128)(2,1)S(1)} %collective-permute-done.14.user_half, bf16[1024,4096]{1,0:T(8,128)(2,1)S(1)} %get-tuple-element.47.refs_5_.labels, bf16[64,1024]{1,0:T(8,128)(2,1)S(1)} %get-tuple-element.69.item, ...), custom_call_target="tpu_custom_call" | custom-call | flops 402653184 | bytes 1048576 | tf_op jit(solution)/shard_map/pallas_call | solution.py:34
  52.7 0.5 collective-permute-start.16
  53.3 1.8 %shard_map.64 = (f32[64,1024]{1,0:T(8,128)S(1)}, f32[64,1024]{1,0:T(8,128)S(1)}) custom-call(bf16[64,2048]{1,0:T(8,128)(2,1)S(1)} %shard_map.58.user_half, bf16[1024,4096]{1,0:T(8,128)(2,1)S(1)} %get-tuple-element.47.refs_5_.labels, bf16[64,1024]{1,0:T(8,128)(2,1)S(1)} %get-tuple-element.69.item, bf16[1024,64]{1,0:T(8,128)(2,1)S(1)} %get-tuple-element.70.item_t, ...), custom_call_target="tpu_custom_call" | custom-call | flops 402653184 | bytes 1048576 | tf_op jit(solution)/shard_map/pallas_call | solution.py:34
  55.1 1.1 %collective-permute-start.17 = (bf16[64,512]{1,0:T(8,128)(2,1)S(1)}, bf16[64,512]{1,0:T(8,128)(2,1)S(1)}, u32[]{:S(2)}, u32[]{:S(2)}) collective-permute-start(bf16[64,512]{1,0:T(8,128)(2,1)S(1)} %get-tuple-element.83), channel_id=1, source_target_pairs={{0,2},{1,3},{2,0},{3,1},{4,6},{5,7},{6,4},{7,5},{8,10},{9,11},{10,... | collective-permute-start | bytes 196616 | tf_op jit(solution)/shard_map/ppermute | solution.py:20
  56.2 2.2 %collective-permute-start.18 = (bf16[64,512]{1,0:T(8,128)(2,1)S(1)}, bf16[64,512]{1,0:T(8,128)(2,1)S(1)}, u32[]{:S(2)}, u32[]{:S(2)}) collective-permute-start(bf16[64,512]{1,0:T(8,128)(2,1)S(1)} %get-tuple-element.74), channel_id=1, source_target_pairs={{0,4},{1,5},{2,6},{3,7},{4,0},{5,1},{6,2},{7,3},{8,12},{9,13},{10,... | collective-permute-start | bytes 196616 | tf_op jit(solution)/shard_map/ppermute | solution.py:20
  58.5 1.1 %collective-permute-start.19 = (bf16[64,512]{1,0:T(8,128)(2,1)S(1)}, bf16[64,512]{1,0:T(8,128)(2,1)S(1)}, u32[]{:S(2)}, u32[]{:S(2)}) collective-permute-start(bf16[64,512]{1,0:T(8,128)(2,1)S(1)} %get-tuple-element.75), channel_id=1, source_target_pairs={{0,6},{1,7},{2,4},{3,5},{4,2},{5,3},{6,0},{7,1},{8,14},{9,15},{10,... | collective-permute-start | bytes 196616 | tf_op jit(solution)/shard_map/ppermute | solution.py:20
  59.6 4.1 %collective-permute-done.18.refs_1_ = bf16[64,512]{1,0:T(8,128)(2,1)S(1)} collective-permute-done((bf16[64,512]{1,0:T(8,128)(2,1)S(1)}, bf16[64,512]{1,0:T(8,128)(2,1)S(1)}, u32[]{:S(2)}, u32[]{:S(2)}) %collective-permute-start.18) | collective-permute-done | bytes 65568 | tf_op jit(solution)/shard_map/ppermute | solution.py:20
  63.7 0.9 %collective-permute-done.19.refs_2_ = bf16[64,512]{1,0:T(8,128)(2,1)S(1)} collective-permute-done((bf16[64,512]{1,0:T(8,128)(2,1)S(1)}, bf16[64,512]{1,0:T(8,128)(2,1)S(1)}, u32[]{:S(2)}, u32[]{:S(2)}) %collective-permute-start.19) | collective-permute-done | bytes 65568 | tf_op jit(solution)/shard_map/ppermute | solution.py:20
  64.7 1.9 %collective-permute-start.22 = (bf16[64,512]{1,0:T(8,128)(2,1)S(1)}, bf16[64,512]{1,0:T(8,128)(2,1)S(1)}, u32[]{:S(2)}, u32[]{:S(2)}) collective-permute-start(bf16[64,512]{1,0:T(8,128)(2,1)S(1)} %shard_map.66.refs_0_), channel_id=1, source_target_pairs={{0,6},{1,7},{2,4},{3,5},{4,2},{5,3},{6,0},{7,1},{8,14},{9,15},{10,... | collective-permute-start | bytes 196616 | tf_op jit(solution)/shard_map/ppermute | solution.py:20
  66.5 0.7 collective-permute-start.21
  67.2 1.9 %collective-permute-start.20 = (bf16[64,512]{1,0:T(8,128)(2,1)S(1)}, bf16[64,512]{1,0:T(8,128)(2,1)S(1)}, u32[]{:S(2)}, u32[]{:S(2)}) collective-permute-start(bf16[64,512]{1,0:T(8,128)(2,1)S(1)} %shard_map.66.refs_0_), channel_id=1, source_target_pairs={{0,2},{1,3},{2,0},{3,1},{4,6},{5,7},{6,4},{7,5},{8,10},{9,11},{10,... | collective-permute-start | bytes 196616 | tf_op jit(solution)/shard_map/ppermute | solution.py:20
  69.1 1.8 %collective-permute-done.22.refs_3_ = bf16[64,512]{1,0:T(8,128)(2,1)S(1)} collective-permute-done((bf16[64,512]{1,0:T(8,128)(2,1)S(1)}, bf16[64,512]{1,0:T(8,128)(2,1)S(1)}, u32[]{:S(2)}, u32[]{:S(2)}) %collective-permute-start.22) | collective-permute-done | bytes 65568 | tf_op jit(solution)/shard_map/ppermute | solution.py:20
  70.9 1.5 %collective-permute-done.21.refs_2_ = bf16[64,512]{1,0:T(8,128)(2,1)S(1)} collective-permute-done((bf16[64,512]{1,0:T(8,128)(2,1)S(1)}, bf16[64,512]{1,0:T(8,128)(2,1)S(1)}, u32[]{:S(2)}, u32[]{:S(2)}) %collective-permute-start.21) | collective-permute-done | bytes 65568 | tf_op jit(solution)/shard_map/ppermute | solution.py:20
  72.5 1.5 %collective-permute-start.24 = (bf16[64,256]{1,0:T(8,128)(2,1)S(1)}, bf16[64,256]{1,0:T(8,128)(2,1)S(1)}, u32[]{:S(2)}, u32[]{:S(2)}) collective-permute-start(bf16[64,256]{1,0:T(8,128)(2,1)S(1)} %get-tuple-element.87), channel_id=1, source_target_pairs={{0,8},{8,0},{16,24},{24,16},{1,9},{9,1},{17,25},{25,17},{2,10},{10... | collective-permute-start | bytes 98312 | tf_op jit(solution)/shard_map/ppermute | solution.py:20
  74.0 0.7 collective-permute-start.25
  74.8 1.3 %collective-permute-start.26 = (bf16[64,256]{1,0:T(8,128)(2,1)S(1)}, bf16[64,256]{1,0:T(8,128)(2,1)S(1)}, u32[]{:S(2)}, u32[]{:S(2)}) collective-permute-start(bf16[64,256]{1,0:T(8,128)(2,1)S(1)} %get-tuple-element.89), channel_id=1, source_target_pairs={{0,24},{8,16},{16,8},{24,0},{1,25},{9,17},{17,9},{25,1},{2,26},{10... | collective-permute-start | bytes 98312 | tf_op jit(solution)/shard_map/ppermute | solution.py:20
  76.0 0.4 collective-permute-done.24.refs_0_
  76.5 1.5 %collective-permute-done.25.refs_1_ = bf16[64,256]{1,0:T(8,128)(2,1)S(1)} collective-permute-done((bf16[64,256]{1,0:T(8,128)(2,1)S(1)}, bf16[64,256]{1,0:T(8,128)(2,1)S(1)}, u32[]{:S(2)}, u32[]{:S(2)}) %collective-permute-start.25) | collective-permute-done | bytes 32800 | tf_op jit(solution)/shard_map/ppermute | solution.py:20
  77.9 1.6 %collective-permute-done.26.refs_2_ = bf16[64,256]{1,0:T(8,128)(2,1)S(1)} collective-permute-done((bf16[64,256]{1,0:T(8,128)(2,1)S(1)}, bf16[64,256]{1,0:T(8,128)(2,1)S(1)}, u32[]{:S(2)}, u32[]{:S(2)}) %collective-permute-start.26) | collective-permute-done | bytes 32800 | tf_op jit(solution)/shard_map/ppermute | solution.py:20
  79.6 0.7 shard_map.69
  80.2 1.1 %shard_map.68 = f32[64,4096]{1,0:T(8,128)} custom-call(f32[64,4096]{1,0:T(8,128)S(1)} %get-tuple-element.46.refs_4_.users.refs_3_, bf16[64,2048]{1,0:T(8,128)(2,1)S(1)} %shard_map.67.own, bf16[64,2048]{1,0:T(8,128)(2,1)S(1)} %collective-permute-done.23.peer), custom_call_target="tpu_custom_call" | custom-call | bytes 1048576 | tf_op jit(solution)/shard_map/pallas_call | solution.py:34
  (32 shorter events, 1.3 us)
Async XLA Ops:
  0.6 12.8 %collective-permute-start = (f32[64,256]{1,0:T(8,128)}, f32[64,256]{1,0:T(8,128)S(1)}, u32[]{:S(2)}, u32[]{:S(2)}) collective-permute-start(f32[64,256]{1,0:T(8,128)} %items_hbm.1), channel_id=1, source_target_pairs={{0,8},{8,0},{16,24},{24,16},{1,9},{9,1},{17,25},{25,17},{2,10},{10... | collective-permute-start | bytes 196616 | tf_op jit(solution)/shard_map/ppermute | solution.py:20
  3.6 9.8 %collective-permute-start.2 = (f32[64,256]{1,0:T(8,128)}, f32[64,256]{1,0:T(8,128)S(1)}, u32[]{:S(2)}, u32[]{:S(2)}) collective-permute-start(f32[64,256]{1,0:T(8,128)} %items_hbm.1), channel_id=1, source_target_pairs={{0,24},{8,16},{16,8},{24,0},{1,25},{9,17},{17,9},{25,1},{2,26},{10... | collective-permute-start | bytes 196616 | tf_op jit(solution)/shard_map/ppermute | solution.py:20
  5.1 8.3 %collective-permute-start.1 = (f32[64,256]{1,0:T(8,128)}, f32[64,256]{1,0:T(8,128)S(1)}, u32[]{:S(2)}, u32[]{:S(2)}) collective-permute-start(f32[64,256]{1,0:T(8,128)} %items_hbm.1), channel_id=1, source_target_pairs={{0,16},{8,24},{16,0},{24,8},{1,17},{9,25},{17,1},{25,9},{2,18},{10... | collective-permute-start | bytes 196616 | tf_op jit(solution)/shard_map/ppermute | solution.py:20
  5.2 3.4 %copy-start = (bf16[1024,4096]{1,0:T(8,128)(2,1)S(1)}, bf16[1024,4096]{1,0:T(8,128)(2,1)}, u32[]{:S(2)}) copy-start(bf16[1024,4096]{1,0:T(8,128)(2,1)} %labels_hbm.1) | copy-start | bytes 25165828
  8.6 1.2 %copy-start.1 = (f32[64,4096]{1,0:T(8,128)S(1)}, f32[64,4096]{1,0:T(8,128)}, u32[]{:S(2)}) copy-start(f32[64,4096]{1,0:T(8,128)} %users_hbm.1) | copy-start | bytes 3145732
  9.8 0.8 %copy-start.2 = (f32[64,256]{1,0:T(8,128)S(1)}, f32[64,256]{1,0:T(8,128)}, u32[]{:S(2)}) copy-start(f32[64,256]{1,0:T(8,128)} %items_hbm.1) | copy-start | bytes 196612
  14.9 1.4 %collective-permute-start.3 = (bf16[64,1024]{1,0:T(8,128)(2,1)S(1)}, bf16[64,1024]{1,0:T(8,128)(2,1)S(1)}, u32[]{:S(2)}, u32[]{:S(2)}) collective-permute-start(bf16[64,1024]{1,0:T(8,128)(2,1)S(1)} %get-tuple-element.55), channel_id=1, source_target_pairs={{0,1},{1,0},{2,3},{3,2},{4,5},{5,4},{6,7},{7,6},{8,9},{9,8},{10,11... | collective-permute-start | bytes 393224 | tf_op jit(solution)/shard_map/ppermute | solution.py:20
  17.7 6.2 %collective-permute-start.4 = (bf16[64,1024]{1,0:T(8,128)(2,1)S(1)}, bf16[64,1024]{1,0:T(8,128)(2,1)S(1)}, u32[]{:S(2)}, u32[]{:S(2)}) collective-permute-start(bf16[64,1024]{1,0:T(8,128)(2,1)S(1)} %get-tuple-element.62), channel_id=1, source_target_pairs={{0,1},{1,0},{2,3},{3,2},{4,5},{5,4},{6,7},{7,6},{8,9},{9,8},{10,11... | collective-permute-start | bytes 393224 | tf_op jit(solution)/shard_map/ppermute | solution.py:20
  18.2 6.9 %collective-permute-start.6 = (bf16[64,512]{1,0:T(8,128)(2,1)S(1)}, bf16[64,512]{1,0:T(8,128)(2,1)S(1)}, u32[]{:S(2)}, u32[]{:S(2)}) collective-permute-start(bf16[64,512]{1,0:T(8,128)(2,1)S(1)} %get-tuple-element.56), channel_id=1, source_target_pairs={{0,4},{1,5},{2,6},{3,7},{4,0},{5,1},{6,2},{7,3},{8,12},{9,13},{10,... | collective-permute-start | bytes 196616 | tf_op jit(solution)/shard_map/ppermute | solution.py:20
  21.3 6.2 %collective-permute-start.7 = (bf16[64,512]{1,0:T(8,128)(2,1)S(1)}, bf16[64,512]{1,0:T(8,128)(2,1)S(1)}, u32[]{:S(2)}, u32[]{:S(2)}) collective-permute-start(bf16[64,512]{1,0:T(8,128)(2,1)S(1)} %get-tuple-element.57), channel_id=1, source_target_pairs={{0,6},{1,7},{2,4},{3,5},{4,2},{5,3},{6,0},{7,1},{8,14},{9,15},{10,... | collective-permute-start | bytes 196616 | tf_op jit(solution)/shard_map/ppermute | solution.py:20
  24.0 4.4 %collective-permute-start.5 = (bf16[64,512]{1,0:T(8,128)(2,1)S(1)}, bf16[64,512]{1,0:T(8,128)(2,1)S(1)}, u32[]{:S(2)}, u32[]{:S(2)}) collective-permute-start(bf16[64,512]{1,0:T(8,128)(2,1)S(1)} %get-tuple-element.65), channel_id=1, source_target_pairs={{0,2},{1,3},{2,0},{3,1},{4,6},{5,7},{6,4},{7,5},{8,10},{9,11},{10,... | collective-permute-start | bytes 196616 | tf_op jit(solution)/shard_map/ppermute | solution.py:20
  28.4 6.8 %collective-permute-start.10 = (bf16[64,512]{1,0:T(8,128)(2,1)S(1)}, bf16[64,512]{1,0:T(8,128)(2,1)S(1)}, u32[]{:S(2)}, u32[]{:S(2)}) collective-permute-start(bf16[64,512]{1,0:T(8,128)(2,1)S(1)} %get-tuple-element.66.refs_0_), channel_id=1, source_target_pairs={{0,6},{1,7},{2,4},{3,5},{4,2},{5,3},{6,0},{7,1},{8,14},{9,15},{10,... | collective-permute-start | bytes 196616 | tf_op jit(solution)/shard_map/ppermute | solution.py:20
  31.5 5.8 %collective-permute-start.9 = (bf16[64,512]{1,0:T(8,128)(2,1)S(1)}, bf16[64,512]{1,0:T(8,128)(2,1)S(1)}, u32[]{:S(2)}, u32[]{:S(2)}) collective-permute-start(bf16[64,512]{1,0:T(8,128)(2,1)S(1)} %get-tuple-element.66.refs_0_), channel_id=1, source_target_pairs={{0,4},{1,5},{2,6},{3,7},{4,0},{5,1},{6,2},{7,3},{8,12},{9,13},{10,... | collective-permute-start | bytes 196616 | tf_op jit(solution)/shard_map/ppermute | solution.py:20
  31.5 5.8 %collective-permute-start.8 = (bf16[64,512]{1,0:T(8,128)(2,1)S(1)}, bf16[64,512]{1,0:T(8,128)(2,1)S(1)}, u32[]{:S(2)}, u32[]{:S(2)}) collective-permute-start(bf16[64,512]{1,0:T(8,128)(2,1)S(1)} %get-tuple-element.66.refs_0_), channel_id=1, source_target_pairs={{0,2},{1,3},{2,0},{3,1},{4,6},{5,7},{6,4},{7,5},{8,10},{9,11},{10,... | collective-permute-start | bytes 196616 | tf_op jit(solution)/shard_map/ppermute | solution.py:20
  37.3 11.7 %collective-permute-start.14 = (bf16[64,2048]{1,0:T(8,128)(2,1)S(1)}, bf16[64,2048]{1,0:T(8,128)(2,1)S(1)}, u32[]{:S(2)}, u32[]{:S(2)}) collective-permute-start(bf16[64,2048]{1,0:T(8,128)(2,1)S(1)} %shard_map.58.user_half), channel_id=1, source_target_pairs={{0,1},{1,0},{2,3},{3,2},{4,5},{5,4},{6,7},{7,6},{8,9},{9,8},{10,11... | collective-permute-start | bytes 786440 | tf_op jit(solution)/shard_map/ppermute | solution.py:20
  37.4 7.1 %collective-permute-start.13 = (bf16[64,1024]{1,0:T(8,128)(2,1)S(1)}, bf16[64,1024]{1,0:T(8,128)(2,1)S(1)}, u32[]{:S(2)}, u32[]{:S(2)}) collective-permute-start(bf16[64,1024]{1,0:T(8,128)(2,1)S(1)} %get-tuple-element.68.refs_0_), channel_id=1, source_target_pairs={{0,24},{8,16},{16,8},{24,0},{1,25},{9,17},{17,9},{25,1},{2,26},{10... | collective-permute-start | bytes 393224 | tf_op jit(solution)/shard_map/ppermute | solution.py:20
  39.9 7.1 %collective-permute-start.12 = (bf16[64,1024]{1,0:T(8,128)(2,1)S(1)}, bf16[64,1024]{1,0:T(8,128)(2,1)S(1)}, u32[]{:S(2)}, u32[]{:S(2)}) collective-permute-start(bf16[64,1024]{1,0:T(8,128)(2,1)S(1)} %get-tuple-element.68.refs_0_), channel_id=1, source_target_pairs={{0,16},{8,24},{16,0},{24,8},{1,17},{9,25},{17,1},{25,9},{2,18},{10... | collective-permute-start | bytes 393224 | tf_op jit(solution)/shard_map/ppermute | solution.py:20
  40.4 6.7 %collective-permute-start.11 = (bf16[64,1024]{1,0:T(8,128)(2,1)S(1)}, bf16[64,1024]{1,0:T(8,128)(2,1)S(1)}, u32[]{:S(2)}, u32[]{:S(2)}) collective-permute-start(bf16[64,1024]{1,0:T(8,128)(2,1)S(1)} %get-tuple-element.68.refs_0_), channel_id=1, source_target_pairs={{0,8},{8,0},{16,24},{24,16},{1,9},{9,1},{17,25},{25,17},{2,10},{10... | collective-permute-start | bytes 393224 | tf_op jit(solution)/shard_map/ppermute | solution.py:20
  50.9 2.4 %collective-permute-start.15 = (bf16[64,1024]{1,0:T(8,128)(2,1)S(1)}, bf16[64,1024]{1,0:T(8,128)(2,1)S(1)}, u32[]{:S(2)}, u32[]{:S(2)}) collective-permute-start(bf16[64,1024]{1,0:T(8,128)(2,1)S(1)} %get-tuple-element.73), channel_id=1, source_target_pairs={{0,1},{1,0},{2,3},{3,2},{4,5},{5,4},{6,7},{7,6},{8,9},{9,8},{10,11... | collective-permute-start | bytes 393224 | tf_op jit(solution)/shard_map/ppermute | solution.py:20
  52.7 2.4 %collective-permute-start.16 = (bf16[64,1024]{1,0:T(8,128)(2,1)S(1)}, bf16[64,1024]{1,0:T(8,128)(2,1)S(1)}, u32[]{:S(2)}, u32[]{:S(2)}) collective-permute-start(bf16[64,1024]{1,0:T(8,128)(2,1)S(1)} %get-tuple-element.80), channel_id=1, source_target_pairs={{0,1},{1,0},{2,3},{3,2},{4,5},{5,4},{6,7},{7,6},{8,9},{9,8},{10,11... | collective-permute-start | bytes 393224 | tf_op jit(solution)/shard_map/ppermute | solution.py:20
  55.1 4.5 %collective-permute-start.17 = (bf16[64,512]{1,0:T(8,128)(2,1)S(1)}, bf16[64,512]{1,0:T(8,128)(2,1)S(1)}, u32[]{:S(2)}, u32[]{:S(2)}) collective-permute-start(bf16[64,512]{1,0:T(8,128)(2,1)S(1)} %get-tuple-element.83), channel_id=1, source_target_pairs={{0,2},{1,3},{2,0},{3,1},{4,6},{5,7},{6,4},{7,5},{8,10},{9,11},{10,... | collective-permute-start | bytes 196616 | tf_op jit(solution)/shard_map/ppermute | solution.py:20
  56.2 7.5 %collective-permute-start.18 = (bf16[64,512]{1,0:T(8,128)(2,1)S(1)}, bf16[64,512]{1,0:T(8,128)(2,1)S(1)}, u32[]{:S(2)}, u32[]{:S(2)}) collective-permute-start(bf16[64,512]{1,0:T(8,128)(2,1)S(1)} %get-tuple-element.74), channel_id=1, source_target_pairs={{0,4},{1,5},{2,6},{3,7},{4,0},{5,1},{6,2},{7,3},{8,12},{9,13},{10,... | collective-permute-start | bytes 196616 | tf_op jit(solution)/shard_map/ppermute | solution.py:20
  58.5 6.2 %collective-permute-start.19 = (bf16[64,512]{1,0:T(8,128)(2,1)S(1)}, bf16[64,512]{1,0:T(8,128)(2,1)S(1)}, u32[]{:S(2)}, u32[]{:S(2)}) collective-permute-start(bf16[64,512]{1,0:T(8,128)(2,1)S(1)} %get-tuple-element.75), channel_id=1, source_target_pairs={{0,6},{1,7},{2,4},{3,5},{4,2},{5,3},{6,0},{7,1},{8,14},{9,15},{10,... | collective-permute-start | bytes 196616 | tf_op jit(solution)/shard_map/ppermute | solution.py:20
  64.7 6.2 %collective-permute-start.22 = (bf16[64,512]{1,0:T(8,128)(2,1)S(1)}, bf16[64,512]{1,0:T(8,128)(2,1)S(1)}, u32[]{:S(2)}, u32[]{:S(2)}) collective-permute-start(bf16[64,512]{1,0:T(8,128)(2,1)S(1)} %shard_map.66.refs_0_), channel_id=1, source_target_pairs={{0,6},{1,7},{2,4},{3,5},{4,2},{5,3},{6,0},{7,1},{8,14},{9,15},{10,... | collective-permute-start | bytes 196616 | tf_op jit(solution)/shard_map/ppermute | solution.py:20
  66.5 5.8 %collective-permute-start.21 = (bf16[64,512]{1,0:T(8,128)(2,1)S(1)}, bf16[64,512]{1,0:T(8,128)(2,1)S(1)}, u32[]{:S(2)}, u32[]{:S(2)}) collective-permute-start(bf16[64,512]{1,0:T(8,128)(2,1)S(1)} %shard_map.66.refs_0_), channel_id=1, source_target_pairs={{0,4},{1,5},{2,6},{3,7},{4,0},{5,1},{6,2},{7,3},{8,12},{9,13},{10,... | collective-permute-start | bytes 196616 | tf_op jit(solution)/shard_map/ppermute | solution.py:20
  67.2 5.1 %collective-permute-start.20 = (bf16[64,512]{1,0:T(8,128)(2,1)S(1)}, bf16[64,512]{1,0:T(8,128)(2,1)S(1)}, u32[]{:S(2)}, u32[]{:S(2)}) collective-permute-start(bf16[64,512]{1,0:T(8,128)(2,1)S(1)} %shard_map.66.refs_0_), channel_id=1, source_target_pairs={{0,2},{1,3},{2,0},{3,1},{4,6},{5,7},{6,4},{7,5},{8,10},{9,11},{10,... | collective-permute-start | bytes 196616 | tf_op jit(solution)/shard_map/ppermute | solution.py:20
  72.4 7.8 %collective-permute-start.23 = (bf16[64,2048]{1,0:T(8,128)(2,1)S(1)}, bf16[64,2048]{1,0:T(8,128)(2,1)S(1)}, u32[]{:S(2)}, u32[]{:S(2)}) collective-permute-start(bf16[64,2048]{1,0:T(8,128)(2,1)S(1)} %shard_map.67.own), channel_id=1, source_target_pairs={{0,1},{1,0},{2,3},{3,2},{4,5},{5,4},{6,7},{7,6},{8,9},{9,8},{10,11... | collective-permute-start | bytes 786440 | tf_op jit(solution)/shard_map/ppermute | solution.py:20
  72.5 4.0 %collective-permute-start.24 = (bf16[64,256]{1,0:T(8,128)(2,1)S(1)}, bf16[64,256]{1,0:T(8,128)(2,1)S(1)}, u32[]{:S(2)}, u32[]{:S(2)}) collective-permute-start(bf16[64,256]{1,0:T(8,128)(2,1)S(1)} %get-tuple-element.87), channel_id=1, source_target_pairs={{0,8},{8,0},{16,24},{24,16},{1,9},{9,1},{17,25},{25,17},{2,10},{10... | collective-permute-start | bytes 98312 | tf_op jit(solution)/shard_map/ppermute | solution.py:20
  74.0 3.9 %collective-permute-start.25 = (bf16[64,256]{1,0:T(8,128)(2,1)S(1)}, bf16[64,256]{1,0:T(8,128)(2,1)S(1)}, u32[]{:S(2)}, u32[]{:S(2)}) collective-permute-start(bf16[64,256]{1,0:T(8,128)(2,1)S(1)} %get-tuple-element.88), channel_id=1, source_target_pairs={{0,16},{8,24},{16,0},{24,8},{1,17},{9,25},{17,1},{25,9},{2,18},{10... | collective-permute-start | bytes 98312 | tf_op jit(solution)/shard_map/ppermute | solution.py:20
  74.8 4.8 %collective-permute-start.26 = (bf16[64,256]{1,0:T(8,128)(2,1)S(1)}, bf16[64,256]{1,0:T(8,128)(2,1)S(1)}, u32[]{:S(2)}, u32[]{:S(2)}) collective-permute-start(bf16[64,256]{1,0:T(8,128)(2,1)S(1)} %get-tuple-element.89), channel_id=1, source_target_pairs={{0,24},{8,16},{16,8},{24,0},{1,25},{9,17},{17,9},{25,1},{2,26},{10... | collective-permute-start | bytes 98312 | tf_op jit(solution)/shard_map/ppermute | solution.py:20

commit v3 on v2

--- a/solution.py
+++ b/solution.py
@@ -13,7 +13,7 @@
 TILE_ITEMS = 512
 
 f32, bf16 = jnp.float32, jnp.bfloat16
-VMEM, ANY = pltpu.VMEM, pl.ANY
+VMEM, HBM = pltpu.VMEM, pltpu.HBM
 
 
 def swap(block, axis, distance):
@@ -30,14 +30,14 @@
     return pl.ds(pl.multiple_of(index * width, width), width)
 
 
-def call(kernel, outs, *args, scratch=(), flops=0, space=VMEM):
+def call(kernel, outs, *args, scratch=(), flops=0, space=VMEM, grant=24):
     return pl.pallas_call(
         kernel,
         in_specs=[pl.BlockSpec(memory_space=space)] * len(args),
         out_specs=[pl.BlockSpec(memory_space=VMEM)] * len(outs),
         out_shape=[jax.ShapeDtypeStruct(s, d) for s, d in outs],
         scratch_shapes=list(scratch),
-        compiler_params=pltpu.CompilerParams(vmem_limit_bytes=24 << 20),
+        compiler_params=pltpu.CompilerParams(vmem_limit_bytes=grant << 20),
         cost_estimate=pl.CostEstimate(flops=flops, bytes_accessed=1 << 20, transcendentals=0),
     )(*args)
 
@@ -262,7 +262,7 @@
     quarter = half // 2
     user_rate = 0.5 / math.sqrt(items_dev * cols_count)
     item_rate = 0.5 / math.sqrt(users_dev * rows_count)
-    work = 6 * rank * items_dev * quarter
+    work = 3 * 10**9
     wide = ((rank, items_dev), f32)
     item_pair = [((rank, items_dev), bf16), ((items_dev, rank), bf16)]
     sent, kept = ((rank, quarter), bf16), ((rank, quarter), f32)
@@ -280,7 +280,7 @@
         [(preference.shape, bf16), (users.shape, f32), (items.shape, f32), (users.shape, f32), wide],
         preference, users, items,
         scratch=[VMEM((rank, block), bf16), VMEM((block, rank), bf16), pltpu.SemaphoreType.DMA((rows_count + 2,))],
-        space=ANY, flops=work,
+        space=HBM, flops=work, grant=42,
     )
     send, grad, item_all, item, item_t = call(
         functools.partial(first_open, rows_count, half), [sent, wide, wide] + item_pair,
@@ -297,7 +297,6 @@
     mine, grad = first(True, False, grad)
     far_pieces = call(functools.partial(combine_far, share), [piece_b] * len(far), mine, recv)
     far_got = [along_z(p, o) for p, o in zip(far_pieces, far)]
-    *_, grad = lax.optimization_barrier((*far_pieces, grad))
     send, grad = first(False, True, grad)
     recv = swap(send, "col", 1)
     mine, grad = first(True, True, grad)
@@ -306,6 +305,7 @@
     )
     near_got = [along_z(p, o) for p, o in zip(near_pieces, near)]
     grads = [grad_b] + [swap(grad_b, "row", o) for o in others]
+    own, grads[1] = lax.optimization_barrier((own, grads[1]))
     new, new_b = call(
         functools.partial(update_share, user_rate, half, share), [piece, piece_b], own, *near_got, *far_got, users_v
     )
@@ -332,7 +332,6 @@
     near_recv = swap(send, "col", 1)
     far_pieces = call(functools.partial(combine_far, share), [piece_b] * len(far), far_mine, far_recv)
     far_got = [along_z(p, o) for p, o in zip(far_pieces, far)]
-    *_, grad = lax.optimization_barrier((*far_pieces, grad))
     near_mine, grad = second(True, True, grad)
     outs = call(
         functools.partial(combine_near_cut, share, rows_count),
@@ -342,6 +341,7 @@
     item_grad, item_pieces, own, near_pieces = outs[0], outs[1:rows_count], outs[rows_count], outs[rows_count + 1 :]
     near_got = [along_z(p, o) for p, o in zip(near_pieces, near)]
     item_got = [swap(p, "row", o) for p, o in zip(item_pieces, others)]
+    own, *item_got = lax.optimization_barrier((own, *item_got))
     (delta,) = call(
         functools.partial(update_last, user_rate, half, share), [piece_b], own, *near_got, *far_got, users_v, new
     )

time: 81.5 us -> 69.4 us (0.85)
  waiting for transfers between devices: 26.5 us -> 16.8 us
  local copies, waits for them, and re-layouts: 5.44 us -> 2.06 us
  Pallas kernels: 17.5 us -> 18.4 us
    ppermute x27, waiting for transfers between devices: 26.5 us -> 16.8 us  [swap(): lax.ppermute(block, axis, [(i, i ^ distance) for i in range(lax.axis_size...]
    unnamed x6 -> x4, local copies, waits for them, and re-layouts: 5.44 us -> 2.06 us
    pallas_call x20, Pallas kernels: 17.5 us -> 18.4 us  [call(): pl.pallas_call(kernel, in_specs=[pl.BlockSpec(memory_space=space)] * len(...]
  transfers between devices with their start and end apart: 27 -> 27, of which waited for: 15 -> 10; matrix products, arithmetic and copies ran while one was open for 0% -> 0% of each run, Pallas kernels for 14% -> 18%
where the time goes in v3:
time: 69.4 us; the launch traced here: 69.2 us
  starting transfers between devices  31.1 us (45%)
  Pallas kernels  18.4 us (27%)
  waiting for transfers between devices  16.8 us (24%)
  local copies, waits for them, and re-layouts  2.06 us (3%)
  between operations  0.83 us (1%)
    ppermute x27, starting transfers between devices, swap(): lax.ppermute(block, axis, [(i, i ^ distance) for i in range(lax.axis_size...  31.1 us
    pallas_call x20, Pallas kernels, call(): pl.pallas_call(kernel, in_specs=[pl.BlockSpec(memory_space=space)] * len(...  18.4 us
    ppermute x27, waiting for transfers between devices, swap(): lax.ppermute(block, axis, [(i, i ^ distance) for i in range(lax.axis_size...  16.8 us
    unnamed x4, local copies, waits for them, and re-layouts  2.06 us
  transfers between devices with their start and end apart: 27, of which 10 were waited for; matrix products, arithmetic and copies ran while one was open for 0% of the time, Pallas kernels for 18%

profile of v3, /device:TPU:0, one launch (start us, length us, event | category | flops | bytes accessed | tf_op | source)
XLA Modules:
  0.0 69.2 jit_solution(9121531679629881623)
XLA Ops:
  0.6 3.0 %collective-permute-start = (f32[64,256]{1,0:T(8,128)}, f32[64,256]{1,0:T(8,128)S(1)}, u32[]{:S(2)}, u32[]{:S(2)}) collective-permute-start(f32[64,256]{1,0:T(8,128)} %items_hbm.1), channel_id=1, source_target_pairs={{0,8},{8,0},{16,24},{24,16},{1,9},{9,1},{17,25},{25,17},{2,10},{10... | collective-permute-start | bytes 196616 | tf_op jit(solution)/shard_map/ppermute | solution.py:20
  3.6 1.5 %collective-permute-start.2 = (f32[64,256]{1,0:T(8,128)}, f32[64,256]{1,0:T(8,128)S(1)}, u32[]{:S(2)}, u32[]{:S(2)}) collective-permute-start(f32[64,256]{1,0:T(8,128)} %items_hbm.1), channel_id=1, source_target_pairs={{0,24},{8,16},{16,8},{24,0},{1,25},{9,17},{17,9},{25,1},{2,26},{10... | collective-permute-start | bytes 196616 | tf_op jit(solution)/shard_map/ppermute | solution.py:20
  5.2 1.2 %copy-done = f32[64,4096]{1,0:T(8,128)S(1)} copy-done((f32[64,4096]{1,0:T(8,128)S(1)}, f32[64,4096]{1,0:T(8,128)}, u32[]{:S(2)}) %copy-start) | copy-done | bytes 1048600
  6.4 0.8 %copy-done.1 = f32[64,256]{1,0:T(8,128)S(1)} copy-done((f32[64,256]{1,0:T(8,128)S(1)}, f32[64,256]{1,0:T(8,128)}, u32[]{:S(2)}) %copy-start.1) | copy-done | bytes 65560
  7.2 3.8 %shard_map.50 = (bf16[1024,4096]{1,0:T(8,128)(2,1)S(1)}, f32[64,4096]{1,0:T(8,128)S(1)}, f32[64,256]{1,0:T(8,128)S(1)}, f32[64,4096]{1,0:T(8,128)S(1)}, f32[64,1024]{1,0:T(8,128)S(1)}) custom-call(bf16[1024,4096]{1,0:T(8,128)(2,1)} %labels_hbm.1, f32[64,4096]{1,0:T(8,128)S(1)} %copy-done, f32[64,256]{1,0:T(8,128)S(1)} %copy-done.1), custom_call_target="tpu_custom_call" | custom-call | flops 3000000000 | bytes 1048576 | tf_op jit(solution)/shard_map/pallas_call | solution.py:34
  11.0 1.4 %shard_map.51 = (bf16[64,1024]{1,0:T(8,128)(2,1)S(1)}, f32[64,1024]{1,0:T(8,128)S(1)}, f32[64,1024]{1,0:T(8,128)S(1)}, bf16[64,1024]{1,0:T(8,128)(2,1)S(1)}, bf16[1024,64]{1,0:T(8,128)(2,1)S(1)}) custom-call(f32[64,256]{1,0:T(8,128)S(1)} %get-tuple-element.53.refs_0_, f32[64,256]{1,0:T(8,128)S(1)} %collective-permute-done.refs_1_, ...), custom_call_target="tpu_custom_call" | custom-call | flops 3000000000 | bytes 1048576 | tf_op jit(solution)/shard_map/pallas_call | solution.py:34
  12.5 0.1 collective-permute-start.6
  12.6 1.3 %shard_map.52 = (f32[64,1024]{1,0:T(8,128)S(1)}, f32[64,1024]{1,0:T(8,128)S(1)}) custom-call(f32[64,4096]{1,0:T(8,128)S(1)} %get-tuple-element.50.refs_4_.users.refs_3_, bf16[1024,4096]{1,0:T(8,128)(2,1)S(1)} %get-tuple-element.51.refs_5_.labels, f32[64,4096]{1,0:T(8,128)S(1)} %get-tuple-element.52.refs_6_.grad_user, ...), custom_call_target="tpu_custom_call" | custom-call | flops 3000000000 | bytes 1048576 | tf_op jit(solution)/shard_map/pallas_call | solution.py:34
  13.9 1.3 %shard_map.53 = (bf16[64,1024]{1,0:T(8,128)(2,1)S(1)}, f32[64,1024]{1,0:T(8,128)S(1)}) custom-call(f32[64,4096]{1,0:T(8,128)S(1)} %get-tuple-element.50.refs_4_.users.refs_3_, bf16[1024,4096]{1,0:T(8,128)(2,1)S(1)} %get-tuple-element.51.refs_5_.labels, f32[64,4096]{1,0:T(8,128)S(1)} %get-tuple-element.52.refs_6_.grad_user, ...), custom_call_target="tpu_custom_call" | custom-call | flops 3000000000 | bytes 1048576 | tf_op jit(solution)/shard_map/pallas_call | solution.py:34
  15.2 0.5 collective-permute-start.3
  15.7 1.3 %shard_map.54 = (f32[64,1024]{1,0:T(8,128)S(1)}, f32[64,1024]{1,0:T(8,128)S(1)}) custom-call(f32[64,4096]{1,0:T(8,128)S(1)} %get-tuple-element.50.refs_4_.users.refs_3_, bf16[1024,4096]{1,0:T(8,128)(2,1)S(1)} %get-tuple-element.51.refs_5_.labels, f32[64,4096]{1,0:T(8,128)S(1)} %get-tuple-element.52.refs_6_.grad_user, ...), custom_call_target="tpu_custom_call" | custom-call | flops 3000000000 | bytes 1048576 | tf_op jit(solution)/shard_map/pallas_call | solution.py:34
  17.1 2.0 %collective-permute-start.4 = (bf16[64,1024]{1,0:T(8,128)(2,1)S(1)}, bf16[64,1024]{1,0:T(8,128)(2,1)S(1)}, u32[]{:S(2)}, u32[]{:S(2)}) collective-permute-start(bf16[64,1024]{1,0:T(8,128)(2,1)S(1)} %get-tuple-element.64.refs_0_), channel_id=1, source_target_pairs={{0,8},{8,0},{16,24},{24,16},{1,9},{9,1},{17,25},{25,17},{2,10},{10... | collective-permute-start | bytes 393224 | tf_op jit(solution)/shard_map/ppermute | solution.py:20
  19.1 1.5 %collective-permute-start.13 = (bf16[64,1024]{1,0:T(8,128)(2,1)S(1)}, bf16[64,1024]{1,0:T(8,128)(2,1)S(1)}, u32[]{:S(2)}, u32[]{:S(2)}) collective-permute-start(bf16[64,1024]{1,0:T(8,128)(2,1)S(1)} %get-tuple-element.64.refs_0_), channel_id=1, source_target_pairs={{0,24},{8,16},{16,8},{24,0},{1,25},{9,17},{17,9},{25,1},{2,26},{10... | collective-permute-start | bytes 393224 | tf_op jit(solution)/shard_map/ppermute | solution.py:20
  20.6 0.1 collective-permute-start.12
  20.7 3.1 %collective-permute-start.7 = (bf16[64,512]{1,0:T(8,128)(2,1)S(1)}, bf16[64,512]{1,0:T(8,128)(2,1)S(1)}, u32[]{:S(2)}, u32[]{:S(2)}) collective-permute-start(bf16[64,512]{1,0:T(8,128)(2,1)S(1)} %get-tuple-element.69), channel_id=1, source_target_pairs={{0,4},{1,5},{2,6},{3,7},{4,0},{5,1},{6,2},{7,3},{8,12},{9,13},{10,... | collective-permute-start | bytes 196616 | tf_op jit(solution)/shard_map/ppermute | solution.py:20
  23.8 1.4 %collective-permute-start.8 = (bf16[64,512]{1,0:T(8,128)(2,1)S(1)}, bf16[64,512]{1,0:T(8,128)(2,1)S(1)}, u32[]{:S(2)}, u32[]{:S(2)}) collective-permute-start(bf16[64,512]{1,0:T(8,128)(2,1)S(1)} %get-tuple-element.70), channel_id=1, source_target_pairs={{0,6},{1,7},{2,4},{3,5},{4,2},{5,3},{6,0},{7,1},{8,14},{9,15},{10,... | collective-permute-start | bytes 196616 | tf_op jit(solution)/shard_map/ppermute | solution.py:20
  25.2 0.2 collective-permute-start.5
  25.4 0.9 %collective-permute-done.7.refs_1_ = bf16[64,512]{1,0:T(8,128)(2,1)S(1)} collective-permute-done((bf16[64,512]{1,0:T(8,128)(2,1)S(1)}, bf16[64,512]{1,0:T(8,128)(2,1)S(1)}, u32[]{:S(2)}, u32[]{:S(2)}) %collective-permute-start.7) | collective-permute-done | bytes 65568 | tf_op jit(solution)/shard_map/ppermute | solution.py:20
  26.3 3.6 %collective-permute-done.8.refs_2_ = bf16[64,512]{1,0:T(8,128)(2,1)S(1)} collective-permute-done((bf16[64,512]{1,0:T(8,128)(2,1)S(1)}, bf16[64,512]{1,0:T(8,128)(2,1)S(1)}, u32[]{:S(2)}, u32[]{:S(2)}) %collective-permute-start.8) | collective-permute-done | bytes 65568 | tf_op jit(solution)/shard_map/ppermute | solution.py:20
  30.0 0.2 collective-permute-done.5.refs_0_
  30.2 2.3 %collective-permute-start.11 = (bf16[64,512]{1,0:T(8,128)(2,1)S(1)}, bf16[64,512]{1,0:T(8,128)(2,1)S(1)}, u32[]{:S(2)}, u32[]{:S(2)}) collective-permute-start(bf16[64,512]{1,0:T(8,128)(2,1)S(1)} %get-tuple-element.71.refs_0_), channel_id=1, source_target_pairs={{0,6},{1,7},{2,4},{3,5},{4,2},{5,3},{6,0},{7,1},{8,14},{9,15},{10,... | collective-permute-start | bytes 196616 | tf_op jit(solution)/shard_map/ppermute | solution.py:20
  32.5 2.1 %collective-permute-start.9 = (bf16[64,512]{1,0:T(8,128)(2,1)S(1)}, bf16[64,512]{1,0:T(8,128)(2,1)S(1)}, u32[]{:S(2)}, u32[]{:S(2)}) collective-permute-start(bf16[64,512]{1,0:T(8,128)(2,1)S(1)} %get-tuple-element.71.refs_0_), channel_id=1, source_target_pairs={{0,2},{1,3},{2,0},{3,1},{4,6},{5,7},{6,4},{7,5},{8,10},{9,11},{10,... | collective-permute-start | bytes 196616 | tf_op jit(solution)/shard_map/ppermute | solution.py:20
  34.7 0.2 shard_map.59
  34.8 2.2 %collective-permute-done.11.refs_3_ = bf16[64,512]{1,0:T(8,128)(2,1)S(1)} collective-permute-done((bf16[64,512]{1,0:T(8,128)(2,1)S(1)}, bf16[64,512]{1,0:T(8,128)(2,1)S(1)}, u32[]{:S(2)}, u32[]{:S(2)}) %collective-permute-start.11) | collective-permute-done | bytes 65568 | tf_op jit(solution)/shard_map/ppermute | solution.py:20
  37.0 1.4 %collective-permute-done.10.refs_2_ = bf16[64,512]{1,0:T(8,128)(2,1)S(1)} collective-permute-done((bf16[64,512]{1,0:T(8,128)(2,1)S(1)}, bf16[64,512]{1,0:T(8,128)(2,1)S(1)}, u32[]{:S(2)}, u32[]{:S(2)}) %collective-permute-start.10) | collective-permute-done | bytes 65568 | tf_op jit(solution)/shard_map/ppermute | solution.py:20
  38.4 0.1 collective-permute-start.14
  38.5 1.8 %shard_map.60 = (f32[64,1024]{1,0:T(8,128)S(1)}, f32[64,1024]{1,0:T(8,128)S(1)}) custom-call(bf16[64,2048]{1,0:T(8,128)(2,1)S(1)} %shard_map.58.user_half, bf16[1024,4096]{1,0:T(8,128)(2,1)S(1)} %get-tuple-element.51.refs_5_.labels, bf16[64,1024]{1,0:T(8,128)(2,1)S(1)} %get-tuple-element.74.item, bf16[1024,64]{1,0:T(8,128)(2,1)S(1)} %get-tuple-element.75.item_t), custom_call_target="tpu_custom_call" | custom-call | flops 3000000000 | bytes 1048576 | tf_op jit(solution)/shard_map/pallas_call | solution.py:34
  40.3 1.8 %shard_map.61 = (bf16[64,1024]{1,0:T(8,128)(2,1)S(1)}, f32[64,1024]{1,0:T(8,128)S(1)}) custom-call(bf16[64,2048]{1,0:T(8,128)(2,1)S(1)} %collective-permute-done.14.user_half, bf16[1024,4096]{1,0:T(8,128)(2,1)S(1)} %get-tuple-element.51.refs_5_.labels, bf16[64,1024]{1,0:T(8,128)(2,1)S(1)} %get-tuple-element.74.item, ...), custom_call_target="tpu_custom_call" | custom-call | flops 3000000000 | bytes 1048576 | tf_op jit(solution)/shard_map/pallas_call | solution.py:34
  42.1 1.8 %shard_map.62 = (bf16[64,1024]{1,0:T(8,128)(2,1)S(1)}, f32[64,1024]{1,0:T(8,128)S(1)}) custom-call(bf16[64,2048]{1,0:T(8,128)(2,1)S(1)} %collective-permute-done.14.user_half, bf16[1024,4096]{1,0:T(8,128)(2,1)S(1)} %get-tuple-element.51.refs_5_.labels, bf16[64,1024]{1,0:T(8,128)(2,1)S(1)} %get-tuple-element.74.item, ...), custom_call_target="tpu_custom_call" | custom-call | flops 3000000000 | bytes 1048576 | tf_op jit(solution)/shard_map/pallas_call | solution.py:34
  43.9 0.5 collective-permute-start.15
  44.4 0.1 collective-permute-start.20
  44.5 1.8 %shard_map.63 = (f32[64,1024]{1,0:T(8,128)S(1)}, f32[64,1024]{1,0:T(8,128)S(1)}) custom-call(bf16[64,2048]{1,0:T(8,128)(2,1)S(1)} %shard_map.58.user_half, bf16[1024,4096]{1,0:T(8,128)(2,1)S(1)} %get-tuple-element.51.refs_5_.labels, bf16[64,1024]{1,0:T(8,128)(2,1)S(1)} %get-tuple-element.74.item, bf16[1024,64]{1,0:T(8,128)(2,1)S(1)} %get-tuple-element.75.item_t, ...), custom_call_target="tpu_custom_call" | custom-call | flops 3000000000 | bytes 1048576 | tf_op jit(solution)/shard_map/pallas_call | solution.py:34
  46.3 1.5 %collective-permute-start.16 = (bf16[64,256]{1,0:T(8,128)(2,1)S(1)}, bf16[64,256]{1,0:T(8,128)(2,1)S(1)}, u32[]{:S(2)}, u32[]{:S(2)}) collective-permute-start(bf16[64,256]{1,0:T(8,128)(2,1)S(1)} %get-tuple-element.83), channel_id=1, source_target_pairs={{0,8},{8,0},{16,24},{24,16},{1,9},{9,1},{17,25},{25,17},{2,10},{10... | collective-permute-start | bytes 98312 | tf_op jit(solution)/shard_map/ppermute | solution.py:20
  47.8 0.5 collective-permute-start.19
  48.4 2.5 %collective-permute-start.21 = (bf16[64,512]{1,0:T(8,128)(2,1)S(1)}, bf16[64,512]{1,0:T(8,128)(2,1)S(1)}, u32[]{:S(2)}, u32[]{:S(2)}) collective-permute-start(bf16[64,512]{1,0:T(8,128)(2,1)S(1)} %get-tuple-element.90), channel_id=1, source_target_pairs={{0,4},{1,5},{2,6},{3,7},{4,0},{5,1},{6,2},{7,3},{8,12},{9,13},{10,... | collective-permute-start | bytes 196616 | tf_op jit(solution)/shard_map/ppermute | solution.py:20
  50.8 1.5 %collective-permute-start.22 = (bf16[64,512]{1,0:T(8,128)(2,1)S(1)}, bf16[64,512]{1,0:T(8,128)(2,1)S(1)}, u32[]{:S(2)}, u32[]{:S(2)}) collective-permute-start(bf16[64,512]{1,0:T(8,128)(2,1)S(1)} %get-tuple-element.91), channel_id=1, source_target_pairs={{0,6},{1,7},{2,4},{3,5},{4,2},{5,3},{6,0},{7,1},{8,14},{9,15},{10,... | collective-permute-start | bytes 196616 | tf_op jit(solution)/shard_map/ppermute | solution.py:20
  52.3 1.5 %collective-permute-start.17 = (bf16[64,256]{1,0:T(8,128)(2,1)S(1)}, bf16[64,256]{1,0:T(8,128)(2,1)S(1)}, u32[]{:S(2)}, u32[]{:S(2)}) collective-permute-start(bf16[64,256]{1,0:T(8,128)(2,1)S(1)} %get-tuple-element.84), channel_id=1, source_target_pairs={{0,16},{8,24},{16,0},{24,8},{1,17},{9,25},{17,1},{25,9},{2,18},{10... | collective-permute-start | bytes 98312 | tf_op jit(solution)/shard_map/ppermute | solution.py:20
  53.9 0.5 collective-permute-start.18
  54.3 1.9 %collective-permute-done.17.refs_1_ = bf16[64,256]{1,0:T(8,128)(2,1)S(1)} collective-permute-done((bf16[64,256]{1,0:T(8,128)(2,1)S(1)}, bf16[64,256]{1,0:T(8,128)(2,1)S(1)}, u32[]{:S(2)}, u32[]{:S(2)}) %collective-permute-start.17) | collective-permute-done | bytes 32800 | tf_op jit(solution)/shard_map/ppermute | solution.py:20
  56.2 2.4 %collective-permute-done.18.refs_2_ = bf16[64,256]{1,0:T(8,128)(2,1)S(1)} collective-permute-done((bf16[64,256]{1,0:T(8,128)(2,1)S(1)}, bf16[64,256]{1,0:T(8,128)(2,1)S(1)}, u32[]{:S(2)}, u32[]{:S(2)}) %collective-permute-start.18) | collective-permute-done | bytes 32800 | tf_op jit(solution)/shard_map/ppermute | solution.py:20
  58.7 2.4 %collective-permute-start.25 = (bf16[64,512]{1,0:T(8,128)(2,1)S(1)}, bf16[64,512]{1,0:T(8,128)(2,1)S(1)}, u32[]{:S(2)}, u32[]{:S(2)}) collective-permute-start(bf16[64,512]{1,0:T(8,128)(2,1)S(1)} %shard_map.66.refs_0_), channel_id=1, source_target_pairs={{0,6},{1,7},{2,4},{3,5},{4,2},{5,3},{6,0},{7,1},{8,14},{9,15},{10,... | collective-permute-start | bytes 196616 | tf_op jit(solution)/shard_map/ppermute | solution.py:20
  61.1 2.0 %collective-permute-start.23 = (bf16[64,512]{1,0:T(8,128)(2,1)S(1)}, bf16[64,512]{1,0:T(8,128)(2,1)S(1)}, u32[]{:S(2)}, u32[]{:S(2)}) collective-permute-start(bf16[64,512]{1,0:T(8,128)(2,1)S(1)} %shard_map.66.refs_0_), channel_id=1, source_target_pairs={{0,2},{1,3},{2,0},{3,1},{4,6},{5,7},{6,4},{7,5},{8,10},{9,11},{10,... | collective-permute-start | bytes 196616 | tf_op jit(solution)/shard_map/ppermute | solution.py:20
  63.2 1.9 %collective-permute-done.25.refs_3_ = bf16[64,512]{1,0:T(8,128)(2,1)S(1)} collective-permute-done((bf16[64,512]{1,0:T(8,128)(2,1)S(1)}, bf16[64,512]{1,0:T(8,128)(2,1)S(1)}, u32[]{:S(2)}, u32[]{:S(2)}) %collective-permute-start.25) | collective-permute-done | bytes 65568 | tf_op jit(solution)/shard_map/ppermute | solution.py:20
  65.1 1.4 %collective-permute-done.24.refs_2_ = bf16[64,512]{1,0:T(8,128)(2,1)S(1)} collective-permute-done((bf16[64,512]{1,0:T(8,128)(2,1)S(1)}, bf16[64,512]{1,0:T(8,128)(2,1)S(1)}, u32[]{:S(2)}, u32[]{:S(2)}) %collective-permute-start.24) | collective-permute-done | bytes 65568 | tf_op jit(solution)/shard_map/ppermute | solution.py:20
  66.5 0.1 collective-permute-start.26
  66.6 0.7 shard_map.69
  67.2 0.9 %collective-permute-done.26.peer = bf16[64,2048]{1,0:T(8,128)(2,1)S(1)} collective-permute-done((bf16[64,2048]{1,0:T(8,128)(2,1)S(1)}, bf16[64,2048]{1,0:T(8,128)(2,1)S(1)}, u32[]{:S(2)}, u32[]{:S(2)}) %collective-permute-start.26) | collective-permute-done | bytes 262176 | tf_op jit(solution)/shard_map/ppermute | solution.py:20
  68.1 1.1 %shard_map.68 = f32[64,4096]{1,0:T(8,128)} custom-call(f32[64,4096]{1,0:T(8,128)S(1)} %get-tuple-element.50.refs_4_.users.refs_3_, bf16[64,2048]{1,0:T(8,128)(2,1)S(1)} %shard_map.67.own, bf16[64,2048]{1,0:T(8,128)(2,1)S(1)} %collective-permute-done.26.peer), custom_call_target="tpu_custom_call" | custom-call | bytes 1048576 | tf_op jit(solution)/shard_map/pallas_call | solution.py:34
  (30 shorter events, 0.4 us)
Async XLA Ops:
  0.6 10.4 %collective-permute-start = (f32[64,256]{1,0:T(8,128)}, f32[64,256]{1,0:T(8,128)S(1)}, u32[]{:S(2)}, u32[]{:S(2)}) collective-permute-start(f32[64,256]{1,0:T(8,128)} %items_hbm.1), channel_id=1, source_target_pairs={{0,8},{8,0},{16,24},{24,16},{1,9},{9,1},{17,25},{25,17},{2,10},{10... | collective-permute-start | bytes 196616 | tf_op jit(solution)/shard_map/ppermute | solution.py:20
  3.6 7.4 %collective-permute-start.2 = (f32[64,256]{1,0:T(8,128)}, f32[64,256]{1,0:T(8,128)S(1)}, u32[]{:S(2)}, u32[]{:S(2)}) collective-permute-start(f32[64,256]{1,0:T(8,128)} %items_hbm.1), channel_id=1, source_target_pairs={{0,24},{8,16},{16,8},{24,0},{1,25},{9,17},{17,9},{25,1},{2,26},{10... | collective-permute-start | bytes 196616 | tf_op jit(solution)/shard_map/ppermute | solution.py:20
  5.1 5.9 %collective-permute-start.1 = (f32[64,256]{1,0:T(8,128)}, f32[64,256]{1,0:T(8,128)S(1)}, u32[]{:S(2)}, u32[]{:S(2)}) collective-permute-start(f32[64,256]{1,0:T(8,128)} %items_hbm.1), channel_id=1, source_target_pairs={{0,16},{8,24},{16,0},{24,8},{1,17},{9,25},{17,1},{25,9},{2,18},{10... | collective-permute-start | bytes 196616 | tf_op jit(solution)/shard_map/ppermute | solution.py:20
  5.2 1.2 %copy-start = (f32[64,4096]{1,0:T(8,128)S(1)}, f32[64,4096]{1,0:T(8,128)}, u32[]{:S(2)}) copy-start(f32[64,4096]{1,0:T(8,128)} %users_hbm.1) | copy-start | bytes 3145732
  6.4 0.8 %copy-start.1 = (f32[64,256]{1,0:T(8,128)S(1)}, f32[64,256]{1,0:T(8,128)}, u32[]{:S(2)}) copy-start(f32[64,256]{1,0:T(8,128)} %items_hbm.1) | copy-start | bytes 196612
  12.5 8.2 %collective-permute-start.6 = (bf16[64,1024]{1,0:T(8,128)(2,1)S(1)}, bf16[64,1024]{1,0:T(8,128)(2,1)S(1)}, u32[]{:S(2)}, u32[]{:S(2)}) collective-permute-start(bf16[64,1024]{1,0:T(8,128)(2,1)S(1)} %get-tuple-element.68), channel_id=1, source_target_pairs={{0,1},{1,0},{2,3},{3,2},{4,5},{5,4},{6,7},{7,6},{8,9},{9,8},{10,11... | collective-permute-start | bytes 393224 | tf_op jit(solution)/shard_map/ppermute | solution.py:20
  15.2 1.8 %collective-permute-start.3 = (bf16[64,1024]{1,0:T(8,128)(2,1)S(1)}, bf16[64,1024]{1,0:T(8,128)(2,1)S(1)}, u32[]{:S(2)}, u32[]{:S(2)}) collective-permute-start(bf16[64,1024]{1,0:T(8,128)(2,1)S(1)} %get-tuple-element.61), channel_id=1, source_target_pairs={{0,1},{1,0},{2,3},{3,2},{4,5},{5,4},{6,7},{7,6},{8,9},{9,8},{10,11... | collective-permute-start | bytes 393224 | tf_op jit(solution)/shard_map/ppermute | solution.py:20
  17.1 8.1 %collective-permute-start.4 = (bf16[64,1024]{1,0:T(8,128)(2,1)S(1)}, bf16[64,1024]{1,0:T(8,128)(2,1)S(1)}, u32[]{:S(2)}, u32[]{:S(2)}) collective-permute-start(bf16[64,1024]{1,0:T(8,128)(2,1)S(1)} %get-tuple-element.64.refs_0_), channel_id=1, source_target_pairs={{0,8},{8,0},{16,24},{24,16},{1,9},{9,1},{17,25},{25,17},{2,10},{10... | collective-permute-start | bytes 393224 | tf_op jit(solution)/shard_map/ppermute | solution.py:20
  19.1 15.6 %collective-permute-start.13 = (bf16[64,1024]{1,0:T(8,128)(2,1)S(1)}, bf16[64,1024]{1,0:T(8,128)(2,1)S(1)}, u32[]{:S(2)}, u32[]{:S(2)}) collective-permute-start(bf16[64,1024]{1,0:T(8,128)(2,1)S(1)} %get-tuple-element.64.refs_0_), channel_id=1, source_target_pairs={{0,24},{8,16},{16,8},{24,0},{1,25},{9,17},{17,9},{25,1},{2,26},{10... | collective-permute-start | bytes 393224 | tf_op jit(solution)/shard_map/ppermute | solution.py:20
  20.6 14.1 %collective-permute-start.12 = (bf16[64,1024]{1,0:T(8,128)(2,1)S(1)}, bf16[64,1024]{1,0:T(8,128)(2,1)S(1)}, u32[]{:S(2)}, u32[]{:S(2)}) collective-permute-start(bf16[64,1024]{1,0:T(8,128)(2,1)S(1)} %get-tuple-element.64.refs_0_), channel_id=1, source_target_pairs={{0,16},{8,24},{16,0},{24,8},{1,17},{9,25},{17,1},{25,9},{2,18},{10... | collective-permute-start | bytes 393224 | tf_op jit(solution)/shard_map/ppermute | solution.py:20
  20.7 5.6 %collective-permute-start.7 = (bf16[64,512]{1,0:T(8,128)(2,1)S(1)}, bf16[64,512]{1,0:T(8,128)(2,1)S(1)}, u32[]{:S(2)}, u32[]{:S(2)}) collective-permute-start(bf16[64,512]{1,0:T(8,128)(2,1)S(1)} %get-tuple-element.69), channel_id=1, source_target_pairs={{0,4},{1,5},{2,6},{3,7},{4,0},{5,1},{6,2},{7,3},{8,12},{9,13},{10,... | collective-permute-start | bytes 196616 | tf_op jit(solution)/shard_map/ppermute | solution.py:20
  23.8 6.2 %collective-permute-start.8 = (bf16[64,512]{1,0:T(8,128)(2,1)S(1)}, bf16[64,512]{1,0:T(8,128)(2,1)S(1)}, u32[]{:S(2)}, u32[]{:S(2)}) collective-permute-start(bf16[64,512]{1,0:T(8,128)(2,1)S(1)} %get-tuple-element.70), channel_id=1, source_target_pairs={{0,6},{1,7},{2,4},{3,5},{4,2},{5,3},{6,0},{7,1},{8,14},{9,15},{10,... | collective-permute-start | bytes 196616 | tf_op jit(solution)/shard_map/ppermute | solution.py:20
  25.2 5.0 %collective-permute-start.5 = (bf16[64,512]{1,0:T(8,128)(2,1)S(1)}, bf16[64,512]{1,0:T(8,128)(2,1)S(1)}, u32[]{:S(2)}, u32[]{:S(2)}) collective-permute-start(bf16[64,512]{1,0:T(8,128)(2,1)S(1)} %get-tuple-element.66), channel_id=1, source_target_pairs={{0,2},{1,3},{2,0},{3,1},{4,6},{5,7},{6,4},{7,5},{8,10},{9,11},{10,... | collective-permute-start | bytes 196616 | tf_op jit(solution)/shard_map/ppermute | solution.py:20
  30.2 6.8 %collective-permute-start.11 = (bf16[64,512]{1,0:T(8,128)(2,1)S(1)}, bf16[64,512]{1,0:T(8,128)(2,1)S(1)}, u32[]{:S(2)}, u32[]{:S(2)}) collective-permute-start(bf16[64,512]{1,0:T(8,128)(2,1)S(1)} %get-tuple-element.71.refs_0_), channel_id=1, source_target_pairs={{0,6},{1,7},{2,4},{3,5},{4,2},{5,3},{6,0},{7,1},{8,14},{9,15},{10,... | collective-permute-start | bytes 196616 | tf_op jit(solution)/shard_map/ppermute | solution.py:20
  32.5 5.9 %collective-permute-start.10 = (bf16[64,512]{1,0:T(8,128)(2,1)S(1)}, bf16[64,512]{1,0:T(8,128)(2,1)S(1)}, u32[]{:S(2)}, u32[]{:S(2)}) collective-permute-start(bf16[64,512]{1,0:T(8,128)(2,1)S(1)} %get-tuple-element.71.refs_0_), channel_id=1, source_target_pairs={{0,4},{1,5},{2,6},{3,7},{4,0},{5,1},{6,2},{7,3},{8,12},{9,13},{10,... | collective-permute-start | bytes 196616 | tf_op jit(solution)/shard_map/ppermute | solution.py:20
  32.5 5.9 %collective-permute-start.9 = (bf16[64,512]{1,0:T(8,128)(2,1)S(1)}, bf16[64,512]{1,0:T(8,128)(2,1)S(1)}, u32[]{:S(2)}, u32[]{:S(2)}) collective-permute-start(bf16[64,512]{1,0:T(8,128)(2,1)S(1)} %get-tuple-element.71.refs_0_), channel_id=1, source_target_pairs={{0,2},{1,3},{2,0},{3,1},{4,6},{5,7},{6,4},{7,5},{8,10},{9,11},{10,... | collective-permute-start | bytes 196616 | tf_op jit(solution)/shard_map/ppermute | solution.py:20
  38.4 1.9 %collective-permute-start.14 = (bf16[64,2048]{1,0:T(8,128)(2,1)S(1)}, bf16[64,2048]{1,0:T(8,128)(2,1)S(1)}, u32[]{:S(2)}, u32[]{:S(2)}) collective-permute-start(bf16[64,2048]{1,0:T(8,128)(2,1)S(1)} %shard_map.58.user_half), channel_id=1, source_target_pairs={{0,1},{1,0},{2,3},{3,2},{4,5},{5,4},{6,7},{7,6},{8,9},{9,8},{10,11... | collective-permute-start | bytes 786440 | tf_op jit(solution)/shard_map/ppermute | solution.py:20
  43.9 2.4 %collective-permute-start.15 = (bf16[64,1024]{1,0:T(8,128)(2,1)S(1)}, bf16[64,1024]{1,0:T(8,128)(2,1)S(1)}, u32[]{:S(2)}, u32[]{:S(2)}) collective-permute-start(bf16[64,1024]{1,0:T(8,128)(2,1)S(1)} %get-tuple-element.80), channel_id=1, source_target_pairs={{0,1},{1,0},{2,3},{3,2},{4,5},{5,4},{6,7},{7,6},{8,9},{9,8},{10,11... | collective-permute-start | bytes 393224 | tf_op jit(solution)/shard_map/ppermute | solution.py:20
  44.4 4.0 %collective-permute-start.20 = (bf16[64,1024]{1,0:T(8,128)(2,1)S(1)}, bf16[64,1024]{1,0:T(8,128)(2,1)S(1)}, u32[]{:S(2)}, u32[]{:S(2)}) collective-permute-start(bf16[64,1024]{1,0:T(8,128)(2,1)S(1)} %get-tuple-element.89), channel_id=1, source_target_pairs={{0,1},{1,0},{2,3},{3,2},{4,5},{5,4},{6,7},{7,6},{8,9},{9,8},{10,11... | collective-permute-start | bytes 393224 | tf_op jit(solution)/shard_map/ppermute | solution.py:20
  46.3 7.6 %collective-permute-start.16 = (bf16[64,256]{1,0:T(8,128)(2,1)S(1)}, bf16[64,256]{1,0:T(8,128)(2,1)S(1)}, u32[]{:S(2)}, u32[]{:S(2)}) collective-permute-start(bf16[64,256]{1,0:T(8,128)(2,1)S(1)} %get-tuple-element.83), channel_id=1, source_target_pairs={{0,8},{8,0},{16,24},{24,16},{1,9},{9,1},{17,25},{25,17},{2,10},{10... | collective-permute-start | bytes 98312 | tf_op jit(solution)/shard_map/ppermute | solution.py:20
  47.8 10.8 %collective-permute-start.19 = (bf16[64,512]{1,0:T(8,128)(2,1)S(1)}, bf16[64,512]{1,0:T(8,128)(2,1)S(1)}, u32[]{:S(2)}, u32[]{:S(2)}) collective-permute-start(bf16[64,512]{1,0:T(8,128)(2,1)S(1)} %get-tuple-element.87), channel_id=1, source_target_pairs={{0,2},{1,3},{2,0},{3,1},{4,6},{5,7},{6,4},{7,5},{8,10},{9,11},{10,... | collective-permute-start | bytes 196616 | tf_op jit(solution)/shard_map/ppermute | solution.py:20
  48.4 10.3 %collective-permute-start.21 = (bf16[64,512]{1,0:T(8,128)(2,1)S(1)}, bf16[64,512]{1,0:T(8,128)(2,1)S(1)}, u32[]{:S(2)}, u32[]{:S(2)}) collective-permute-start(bf16[64,512]{1,0:T(8,128)(2,1)S(1)} %get-tuple-element.90), channel_id=1, source_target_pairs={{0,4},{1,5},{2,6},{3,7},{4,0},{5,1},{6,2},{7,3},{8,12},{9,13},{10,... | collective-permute-start | bytes 196616 | tf_op jit(solution)/shard_map/ppermute | solution.py:20
  50.8 7.8 %collective-permute-start.22 = (bf16[64,512]{1,0:T(8,128)(2,1)S(1)}, bf16[64,512]{1,0:T(8,128)(2,1)S(1)}, u32[]{:S(2)}, u32[]{:S(2)}) collective-permute-start(bf16[64,512]{1,0:T(8,128)(2,1)S(1)} %get-tuple-element.91), channel_id=1, source_target_pairs={{0,6},{1,7},{2,4},{3,5},{4,2},{5,3},{6,0},{7,1},{8,14},{9,15},{10,... | collective-permute-start | bytes 196616 | tf_op jit(solution)/shard_map/ppermute | solution.py:20
  52.3 3.9 %collective-permute-start.17 = (bf16[64,256]{1,0:T(8,128)(2,1)S(1)}, bf16[64,256]{1,0:T(8,128)(2,1)S(1)}, u32[]{:S(2)}, u32[]{:S(2)}) collective-permute-start(bf16[64,256]{1,0:T(8,128)(2,1)S(1)} %get-tuple-element.84), channel_id=1, source_target_pairs={{0,16},{8,24},{16,0},{24,8},{1,17},{9,25},{17,1},{25,9},{2,18},{10... | collective-permute-start | bytes 98312 | tf_op jit(solution)/shard_map/ppermute | solution.py:20
  53.9 4.8 %collective-permute-start.18 = (bf16[64,256]{1,0:T(8,128)(2,1)S(1)}, bf16[64,256]{1,0:T(8,128)(2,1)S(1)}, u32[]{:S(2)}, u32[]{:S(2)}) collective-permute-start(bf16[64,256]{1,0:T(8,128)(2,1)S(1)} %get-tuple-element.85), channel_id=1, source_target_pairs={{0,24},{8,16},{16,8},{24,0},{1,25},{9,17},{17,9},{25,1},{2,26},{10... | collective-permute-start | bytes 98312 | tf_op jit(solution)/shard_map/ppermute | solution.py:20
  58.7 6.4 %collective-permute-start.25 = (bf16[64,512]{1,0:T(8,128)(2,1)S(1)}, bf16[64,512]{1,0:T(8,128)(2,1)S(1)}, u32[]{:S(2)}, u32[]{:S(2)}) collective-permute-start(bf16[64,512]{1,0:T(8,128)(2,1)S(1)} %shard_map.66.refs_0_), channel_id=1, source_target_pairs={{0,6},{1,7},{2,4},{3,5},{4,2},{5,3},{6,0},{7,1},{8,14},{9,15},{10,... | collective-permute-start | bytes 196616 | tf_op jit(solution)/shard_map/ppermute | solution.py:20
  61.1 5.3 %collective-permute-start.24 = (bf16[64,512]{1,0:T(8,128)(2,1)S(1)}, bf16[64,512]{1,0:T(8,128)(2,1)S(1)}, u32[]{:S(2)}, u32[]{:S(2)}) collective-permute-start(bf16[64,512]{1,0:T(8,128)(2,1)S(1)} %shard_map.66.refs_0_), channel_id=1, source_target_pairs={{0,4},{1,5},{2,6},{3,7},{4,0},{5,1},{6,2},{7,3},{8,12},{9,13},{10,... | collective-permute-start | bytes 196616 | tf_op jit(solution)/shard_map/ppermute | solution.py:20
  61.1 5.3 %collective-permute-start.23 = (bf16[64,512]{1,0:T(8,128)(2,1)S(1)}, bf16[64,512]{1,0:T(8,128)(2,1)S(1)}, u32[]{:S(2)}, u32[]{:S(2)}) collective-permute-start(bf16[64,512]{1,0:T(8,128)(2,1)S(1)} %shard_map.66.refs_0_), channel_id=1, source_target_pairs={{0,2},{1,3},{2,0},{3,1},{4,6},{5,7},{6,4},{7,5},{8,10},{9,11},{10,... | collective-permute-start | bytes 196616 | tf_op jit(solution)/shard_map/ppermute | solution.py:20
  66.5 1.6 %collective-permute-start.26 = (bf16[64,2048]{1,0:T(8,128)(2,1)S(1)}, bf16[64,2048]{1,0:T(8,128)(2,1)S(1)}, u32[]{:S(2)}, u32[]{:S(2)}) collective-permute-start(bf16[64,2048]{1,0:T(8,128)(2,1)S(1)} %shard_map.67.own), channel_id=1, source_target_pairs={{0,1},{1,0},{2,3},{3,2},{4,5},{5,4},{6,7},{7,6},{8,9},{9,8},{10,11... | collective-permute-start | bytes 786440 | tf_op jit(solution)/shard_map/ppermute | solution.py:20

commit v4 on v3

v4 whole, which is shorter than its diff:
```python
import functools
import math

import jax
import jax.numpy as jnp
from jax import lax
from jax.experimental import pallas as pl
from jax.experimental.pallas import tpu as pltpu
from jax.sharding import PartitionSpec as P

CORES = 2
GROUPS = ((True, True), (False, True), (True, False), (False, False))
TILE_USERS = 1024
TILE_ITEMS = 512

f32, bf16 = jnp.float32, jnp.bfloat16
VMEM, HBM = pltpu.VMEM, pltpu.HBM


def swap(block, axis, distance):
    return lax.ppermute(block, axis, [(i, i ^ distance) for i in range(lax.axis_size(axis))])


def tree_sum(terms):
    while len(terms) > 1:
        terms = [terms[i] + terms[i + 1] for i in range(0, len(terms), 2)]
    return terms[0]


def span(index, width):
    return pl.ds(pl.multiple_of(index * width, width), width)


def call(kernel, outs, *args, scratch=(), flops=0, space=VMEM, grant=24):
    return pl.pallas_call(
        kernel,
        in_specs=[pl.BlockSpec(memory_space=space)] * len(args),
        out_specs=[pl.BlockSpec(memory_space=VMEM)] * len(outs),
        out_shape=[jax.ShapeDtypeStruct(s, d) for s, d in outs],
        scratch_shapes=list(scratch),
        compiler_params=pltpu.CompilerParams(vmem_limit_bytes=grant << 20),
        cost_estimate=pl.CostEstimate(flops=flops, bytes_accessed=1 << 20, transcendentals=0),
    )(*args)


def place():
    col = lax.axis_index("col")
    return lax.axis_index("row"), col // CORES, col % CORES


def bit(level):
    _, z, _ = place()
    return (z >> level) & 1


def group_start(own, keep, half):
    _, _, core = place()
    quarter = half // 2
    core = core if own else 1 - core
    side = bit(0) if keep else 1 - bit(0)
    return pl.multiple_of(core * half + side * quarter, quarter)


def kept_at(half, width):
    _, _, core = place()
    start, level, size = core * half, 0, half // 2
    while size >= width:
        start, level, size = start + bit(level) * size, level + 1, size // 2
    return pl.ds(pl.multiple_of(start, width), width)


def row_tiles(items_dev, block, everything):
    if everything:
        tile = min(TILE_ITEMS, items_dev)
        return [(at, tile) for at in range(0, items_dev, tile)]
    row, tiles, size = lax.axis_index("row"), [], 1
    while size * block < items_dev:
        tiles.append((pl.multiple_of(((row // size) ^ 1) * (size * block), size * block), size * block))
        size *= 2
    return tiles


def gradients(tiles, start, width, user_of, item, item_t, labels, grad_item, keep):
    tile_users = min(TILE_USERS, width)
    for at in range(0, width, tile_users):
        here = pl.ds(pl.multiple_of(start + at, tile_users), tile_users)
        user = user_of(at, tile_users)
        total = None
        for first, size in tiles:
            rows = pl.ds(first, size)
            half_scores = jnp.dot(item_t[rows, :], user, preferred_element_type=f32)
            weights = labels[rows, here].astype(f32)
            residual = (jnp.abs(weights) * jnp.tanh(half_scores) - weights).astype(bf16)
            term = jnp.dot(item[:, rows], residual, preferred_element_type=f32)
            total = term if total is None else total + term
            grad_item[:, rows] += lax.dot_general(
                user, residual, (((1,), (1,)), ((), ())), preferred_element_type=f32
            )
        keep(at, tile_users, total)


def put_items(value, item, item_t):
    rounded = value.astype(bf16)
    item[...] = rounded
    item_t[...] = (rounded * jnp.asarray(0.5, bf16)).T


def load_and_own_rows(rows_count, labels_hbm, users_hbm, items_hbm, labels, users, items, grad_user, grad_item, item, item_t, sems):
    row, block = lax.axis_index("row"), items.shape[1]

    def rows_of(o):
        at = span(row ^ o, block)
        return pltpu.make_async_copy(labels_hbm.at[at, :], labels.at[at, :], sems.at[2 + o])

    copies = [
        pltpu.make_async_copy(items_hbm, items, sems.at[0]),
        pltpu.make_async_copy(users_hbm, users, sems.at[1]),
    ] + [rows_of(o) for o in range(rows_count)]
    for copy in copies:
        copy.start()
    copies[0].wait()
    own = span(row, block)
    put_items(items[...], item, item_t)
    grad_item[...] = jnp.zeros_like(grad_item)
    copies[1].wait()
    copies[2].wait()
    width = users.shape[1]
    tile = min(TILE_USERS, width)
    for at in range(0, width, tile):
        here = pl.ds(at, tile)
        user = users[:, here].astype(bf16)
        half_scores = jnp.dot(item_t[...], user, preferred_element_type=f32)
        weights = labels[own, here].astype(f32)
        residual = (jnp.abs(weights) * jnp.tanh(half_scores) - weights).astype(bf16)
        grad_user[:, here] = jnp.dot(item[...], residual, preferred_element_type=f32)
        grad_item[:, own] += lax.dot_general(user, residual, (((1,), (1,)), ((), ())), preferred_element_type=f32)
    for copy in copies[3:]:
        copy.wait()


def first_open(rows_count, half, *refs):
    blocks = refs[:rows_count]
    users, labels, grad_user, grad_in = refs[rows_count : rows_count + 4]
    send, grad_item, item_all, item, item_t = refs[rows_count + 4 :]
    row, block = lax.axis_index("row"), blocks[0].shape[1]
    for o, values in enumerate(blocks):
        item_all[:, span(row ^ o, block)] = values[...]
    put_items(item_all[...], item, item_t)
    first_group(False, False, half, block, users, labels, grad_user, item, item_t, grad_in, send, grad_item)


def first_group(own, keep_side, half, block, users, labels, grad_user, item, item_t, grad_in, out, grad_item):
    start = group_start(own, keep_side, half)
    grad_item[...] = grad_in[...]

    def columns(at, width):
        return pl.ds(pl.multiple_of(start + at, width), width)

    def keep(at, width, total):
        out[:, pl.ds(at, width)] = (total + grad_user[:, columns(at, width)]).astype(out.dtype)

    gradients(
        row_tiles(labels.shape[0], block, False), start, half // 2,
        lambda at, width: users[:, columns(at, width)].astype(bf16),
        item, item_t, labels, grad_item, keep,
    )


def second_group(own, keep_side, half, user, labels, item, item_t, grad_in, out, grad_item):
    if grad_in is None:
        grad_item[...] = jnp.zeros_like(grad_item)
    else:
        grad_item[...] = grad_in[...]

    def keep(at, width, total):
        out[:, pl.ds(at, width)] = total.astype(out.dtype)

    gradients(
        row_tiles(labels.shape[0], None, True), group_start(own, keep_side, half), half // 2,
        lambda at, width: user[:, pl.ds(at, width)], item, item_t, labels, grad_item, keep,
    )


def second_open(half, user, labels, item, item_t, out, grad_item):
    second_group(True, True, half, user, labels, item, item_t, None, out, grad_item)


def combine(*refs):
    total = refs[0][...]
    for ref in refs[1:-1]:
        total = total + ref[...].astype(f32)
    refs[-1][...] = total.astype(refs[-1].dtype)


def split(level, total, kept, sent):
    width = kept.shape[1]
    kept[...] = total[:, span(bit(level), width)]
    sent[...] = total[:, span(1 - bit(level), width)].astype(bf16)


def join(level, mine, got, out):
    width = mine.shape[1]
    out[:, span(bit(level), width)] = mine[...]
    out[:, span(1 - bit(level), width)] = got[...]


def round_items(grad_item, out):
    out[...] = grad_item[...].astype(bf16)


def cut_items(grad_item, *outs):
    row, block = lax.axis_index("row"), outs[0].shape[1]
    for o, out in enumerate(outs):
        out[...] = grad_item[:, span(row ^ o, block)].astype(out.dtype)


def update_users(rate, half, mine, got, users, new, new_b):
    grad = mine[...].astype(f32) + got[...].astype(f32)
    new[...] = users[:, kept_at(half, mine.shape[1])] - rate * grad
    new_b[...] = new[...].astype(bf16)


def update_last(rate, half, mine, got, users, new, delta):
    grad = mine[...].astype(f32) + got[...].astype(f32)
    delta[...] = (new[...] - rate * grad - users[:, kept_at(half, mine.shape[1])]).astype(bf16)


def second_start(rate, rows_count, item_all, *refs):
    grads, (item_own, item, item_t) = refs[:rows_count], refs[rows_count:]
    new = item_all[...] - rate * tree_sum([g[...].astype(f32) for g in grads])
    put_items(new, item, item_t)
    at = span(lax.axis_index("row"), item_own.shape[1])
    item_own[...] = item_all[:, at] - rate * tree_sum([g[:, at].astype(f32) for g in grads])


def finish_items(rate, item, own, *refs):
    recvs, out = refs[:-1], refs[-1]
    out[...] = item[...] - rate * tree_sum([own[...]] + [r[...].astype(f32) for r in recvs])


def finish_users(half, users, *refs):
    pieces, out = refs[:-1], refs[-1]
    for piece, (own, keep_side) in zip(pieces, GROUPS):
        at = pl.ds(group_start(own, keep_side, half), half // 2)
        out[:, at] = users[:, at] + piece[...].astype(f32)


def body(preference, users, items):
    rows_count, cols_count = lax.axis_size("row"), lax.axis_size("col")
    items_dev, users_dev = preference.shape
    rank, block = items.shape
    chips = cols_count // CORES
    half = users_dev // CORES
    quarter = half // 2
    levels = chips.bit_length() - 1
    user_rate = 0.5 / math.sqrt(items_dev * cols_count)
    item_rate = 0.5 / math.sqrt(users_dev * rows_count)
    work = 3 * 10**9
    wide = ((rank, items_dev), f32)
    item_pair = [((rank, items_dev), bf16), ((items_dev, rank), bf16)]
    sent, kept = ((rank, quarter), bf16), ((rank, quarter), f32)
    others = list(range(1, rows_count))

    def along_z(block, level):
        return swap(block, "col", CORES << level)

    def narrow(mine):
        for level in range(1, levels - 1):
            width = mine.shape[1] // 2
            mine, send = call(functools.partial(split, level), [((rank, width), f32), ((rank, width), bf16)], mine)
            (mine,) = call(combine, [((rank, width), f32)], mine, along_z(send, level))
        return mine

    def widen(block):
        for level in reversed(range(1, levels - 1)):
            outs = [((rank, 2 * block.shape[1]), bf16)]
            (block,) = call(functools.partial(join, level), outs, block, along_z(block, level))
        return block

    def meet(mine, *terms):
        if levels > 2:
            (mine,) = call(combine, [kept], mine, *terms)
            mine, terms = narrow(mine), ()
        (mine,) = call(combine, [(mine.shape, bf16)], mine, *terms)
        return mine, along_z(mine, levels - 1)

    item_blocks = [swap(items, "row", o) for o in others]
    labels, users_v, items_v, grad_user, grad = call(
        functools.partial(load_and_own_rows, rows_count),
        [(preference.shape, bf16), (users.shape, f32), (items.shape, f32), (users.shape, f32), wide],
        preference, users, items,
        scratch=[VMEM((rank, block), bf16), VMEM((block, rank), bf16), pltpu.SemaphoreType.DMA((rows_count + 2,))],
        space=HBM, flops=work, grant=42,
    )
    send, grad, item_all, item, item_t = call(
        functools.partial(first_open, rows_count, half), [sent, wide, wide] + item_pair,
        items_v, *item_blocks, users_v, labels, grad_user, grad, flops=work,
    )

    def first(own, near, grad):
        return call(
            functools.partial(first_group, own, near, half, block), [kept if own else sent, wide],
            users_v, labels, grad_user, item, item_t, grad, flops=work,
        )

    recv = swap(send, "col", 1)
    mine, grad = first(True, False, grad)
    (piece,) = call(combine, [sent], mine, recv)
    near = along_z(piece, 0)
    send, grad = first(False, True, grad)
    recv = swap(send, "col", 1)
    mine, grad = first(True, True, grad)
    (grad_b,) = call(round_items, [(wide[0], bf16)], grad)
    grads = [grad_b] + [swap(grad_b, "row", o) for o in others]
    mine, got = meet(mine, recv, near)
    updated = [(mine.shape, f32), (mine.shape, bf16)]
    new, new_b = call(functools.partial(update_users, user_rate, half), updated, mine, got, users_v)

    def gather(block):
        own_keep = widen(block)
        own_send = along_z(own_keep, 0)
        return own_keep, swap(own_keep, "col", 1), own_send, swap(own_send, "col", 1)

    own_keep, peer_keep, own_send, peer_send = gather(new_b)
    item_own, item, item_t = call(
        functools.partial(second_start, item_rate, rows_count), [(items.shape, f32)] + item_pair, item_all, *grads
    )

    def second(own, keep_side, user, grad):
        return call(
            functools.partial(second_group, own, keep_side, half), [kept if own else sent, wide],
            user, labels, item, item_t, grad, flops=work,
        )

    mine, grad = call(
        functools.partial(second_open, half), [kept, wide], own_keep, labels, item, item_t, flops=work
    )
    send, grad = second(False, True, peer_keep, grad)
    recv = swap(send, "col", 1)
    mine_send, grad = second(True, False, own_send, grad)
    send, grad = second(False, False, peer_send, grad)
    recv_send = swap(send, "col", 1)
    (piece,) = call(combine, [sent], mine_send, recv_send)
    near = along_z(piece, 0)
    item_pieces = call(cut_items, [(items.shape, f32)] + [(items.shape, bf16)] * len(others), grad)
    item_got = [swap(p, "row", o) for p, o in zip(item_pieces[1:], others)]
    mine, got = meet(mine, recv, near)
    got, *item_got = lax.optimization_barrier((got, *item_got))
    (delta,) = call(
        functools.partial(update_last, user_rate, half), [(mine.shape, bf16)], mine, got, users_v, new
    )
    (new_items,) = call(
        functools.partial(finish_items, item_rate), [(items.shape, f32)], item_own, item_pieces[0], *item_got
    )
    (new_users,) = call(functools.partial(finish_users, half), [(users.shape, f32)], users_v, *gather(delta))
    return new_users, new_items


def solution(mesh):
    return jax.shard_map(
        body,
        mesh=mesh,
        in_specs=(P("col", "row"), P(None, "row"), P(None, ("col", "row"))),
        out_specs=(P(None, "row"), P(None, ("col", "row"))),
        check_vma=False,
    )
```

time: 69.4 us -> 66.1 us (0.952)
  starting transfers between devices: 31.1 us -> 21.6 us
  waiting for transfers between devices: 16.8 us -> 23.2 us
    ppermute x27 -> x23, starting transfers between devices: 31.1 us -> 21.6 us  [swap(): lax.ppermute(block, axis, [(i, i ^ distance) for i in range(lax.axis_size...]
    ppermute x27 -> x23, waiting for transfers between devices: 16.8 us -> 23.2 us  [swap(): lax.ppermute(block, axis, [(i, i ^ distance) for i in range(lax.axis_size...]
  transfers between devices with their start and end apart: 27 -> 23, of which waited for: 10 -> 13; matrix products, arithmetic and copies ran while one was open for 0% -> 0% of each run, Pallas kernels for 18% -> 21%
where the time goes in v4:
time: 66.1 us; the launch traced here: 65.9 us
  waiting for transfers between devices  23.2 us (35%)
  starting transfers between devices  21.6 us (33%)
  Pallas kernels  18.3 us (28%)
  local copies, waits for them, and re-layouts  2.06 us (3%)
  between operations  0.79 us (1%)
    ppermute x23, waiting for transfers between devices, swap(): lax.ppermute(block, axis, [(i, i ^ distance) for i in range(lax.axis_size...  23.2 us
    ppermute x23, starting transfers between devices, swap(): lax.ppermute(block, axis, [(i, i ^ distance) for i in range(lax.axis_size...  21.6 us
    pallas_call x20, Pallas kernels, call(): pl.pallas_call(kernel, in_specs=[pl.BlockSpec(memory_space=space)] * len(...  18.3 us
    unnamed x4, local copies, waits for them, and re-layouts  2.06 us
  transfers between devices with their start and end apart: 23, of which 13 were waited for; matrix products, arithmetic and copies ran while one was open for 0% of the time, Pallas kernels for 21%

profile of v4, /device:TPU:0, one launch (start us, length us, event | category | flops | bytes accessed | tf_op | source)
XLA Modules:
  0.0 65.9 jit_solution(11529091301953296656)
XLA Ops:
  0.6 3.0 %collective-permute-start = (f32[64,256]{1,0:T(8,128)}, f32[64,256]{1,0:T(8,128)S(1)}, u32[]{:S(2)}, u32[]{:S(2)}) collective-permute-start(f32[64,256]{1,0:T(8,128)} %items_hbm.1), channel_id=1, source_target_pairs={{0,8},{8,0},{16,24},{24,16},{1,9},{9,1},{17,25},{25,17},{2,10},{10... | collective-permute-start | bytes 196616 | tf_op jit(solution)/shard_map/ppermute | solution.py:21
  3.6 1.5 %collective-permute-start.2 = (f32[64,256]{1,0:T(8,128)}, f32[64,256]{1,0:T(8,128)S(1)}, u32[]{:S(2)}, u32[]{:S(2)}) collective-permute-start(f32[64,256]{1,0:T(8,128)} %items_hbm.1), channel_id=1, source_target_pairs={{0,24},{8,16},{16,8},{24,0},{1,25},{9,17},{17,9},{25,1},{2,26},{10... | collective-permute-start | bytes 196616 | tf_op jit(solution)/shard_map/ppermute | solution.py:21
  5.2 1.2 %copy-done = f32[64,4096]{1,0:T(8,128)S(1)} copy-done((f32[64,4096]{1,0:T(8,128)S(1)}, f32[64,4096]{1,0:T(8,128)}, u32[]{:S(2)}) %copy-start) | copy-done | bytes 1048600
  6.4 0.8 %copy-done.1 = f32[64,256]{1,0:T(8,128)S(1)} copy-done((f32[64,256]{1,0:T(8,128)S(1)}, f32[64,256]{1,0:T(8,128)}, u32[]{:S(2)}) %copy-start.1) | copy-done | bytes 65560
  7.2 3.8 %shard_map.50 = (bf16[1024,4096]{1,0:T(8,128)(2,1)S(1)}, f32[64,4096]{1,0:T(8,128)S(1)}, f32[64,256]{1,0:T(8,128)S(1)}, f32[64,4096]{1,0:T(8,128)S(1)}, f32[64,1024]{1,0:T(8,128)S(1)}) custom-call(bf16[1024,4096]{1,0:T(8,128)(2,1)} %labels_hbm.1, f32[64,4096]{1,0:T(8,128)S(1)} %copy-done, f32[64,256]{1,0:T(8,128)S(1)} %copy-done.1), custom_call_target="tpu_custom_call" | custom-call | flops 3000000000 | bytes 1048576 | tf_op jit(solution)/shard_map/pallas_call | solution.py:35
  11.0 1.4 %shard_map.51 = (bf16[64,1024]{1,0:T(8,128)(2,1)S(1)}, f32[64,1024]{1,0:T(8,128)S(1)}, f32[64,1024]{1,0:T(8,128)S(1)}, bf16[64,1024]{1,0:T(8,128)(2,1)S(1)}, bf16[1024,64]{1,0:T(8,128)(2,1)S(1)}) custom-call(f32[64,256]{1,0:T(8,128)S(1)} %get-tuple-element.42.refs_0_, f32[64,256]{1,0:T(8,128)S(1)} %collective-permute-done.refs_1_, ...), custom_call_target="tpu_custom_call" | custom-call | flops 3000000000 | bytes 1048576 | tf_op jit(solution)/shard_map/pallas_call | solution.py:35
  12.5 0.1 collective-permute-start.4
  12.6 1.3 %shard_map.52 = (f32[64,1024]{1,0:T(8,128)S(1)}, f32[64,1024]{1,0:T(8,128)S(1)}) custom-call(f32[64,4096]{1,0:T(8,128)S(1)} %get-tuple-element.39.refs_4_.users, bf16[1024,4096]{1,0:T(8,128)(2,1)S(1)} %get-tuple-element.40.refs_5_.labels, f32[64,4096]{1,0:T(8,128)S(1)} %get-tuple-element.41.refs_6_.grad_user, bf16[64,1024]{1,0:T(8,128)(2,1)S(1)} %get-tuple-element.44.item, ...), custom_call_target="tpu_custom_call" | custom-call | flops 3000000000 | bytes 1048576 | tf_op jit(solution)/shard_map/pallas_call | solution.py:35
  13.9 1.3 %shard_map.53 = (bf16[64,1024]{1,0:T(8,128)(2,1)S(1)}, f32[64,1024]{1,0:T(8,128)S(1)}) custom-call(f32[64,4096]{1,0:T(8,128)S(1)} %get-tuple-element.39.refs_4_.users, bf16[1024,4096]{1,0:T(8,128)(2,1)S(1)} %get-tuple-element.40.refs_5_.labels, f32[64,4096]{1,0:T(8,128)S(1)} %get-tuple-element.41.refs_6_.grad_user, ...), custom_call_target="tpu_custom_call" | custom-call | flops 3000000000 | bytes 1048576 | tf_op jit(solution)/shard_map/pallas_call | solution.py:35
  15.2 0.6 collective-permute-start.3
  15.8 2.1 %collective-permute-start.5 = (bf16[64,1024]{1,0:T(8,128)(2,1)S(1)}, bf16[64,1024]{1,0:T(8,128)(2,1)S(1)}, u32[]{:S(2)}, u32[]{:S(2)}) collective-permute-start(bf16[64,1024]{1,0:T(8,128)(2,1)S(1)} %shard_map.55), channel_id=1, source_target_pairs={{0,2},{1,3},{2,0},{3,1},{4,6},{5,7},{6,4},{7,5},{8,10},{9,11},{10,... | collective-permute-start | bytes 393224 | tf_op jit(solution)/shard_map/ppermute | solution.py:21
  17.9 1.3 %shard_map.54 = (f32[64,1024]{1,0:T(8,128)S(1)}, f32[64,1024]{1,0:T(8,128)S(1)}) custom-call(f32[64,4096]{1,0:T(8,128)S(1)} %get-tuple-element.39.refs_4_.users, bf16[1024,4096]{1,0:T(8,128)(2,1)S(1)} %get-tuple-element.40.refs_5_.labels, f32[64,4096]{1,0:T(8,128)S(1)} %get-tuple-element.41.refs_6_.grad_user, bf16[64,1024]{1,0:T(8,128)(2,1)S(1)} %get-tuple-element.44.item, ...), custom_call_target="tpu_custom_call" | custom-call | flops 3000000000 | bytes 1048576 | tf_op jit(solution)/shard_map/pallas_call | solution.py:35
  19.2 2.5 %collective-permute-start.9 = (bf16[64,1024]{1,0:T(8,128)(2,1)S(1)}, bf16[64,1024]{1,0:T(8,128)(2,1)S(1)}, u32[]{:S(2)}, u32[]{:S(2)}) collective-permute-start(bf16[64,1024]{1,0:T(8,128)(2,1)S(1)} %shard_map.58.refs_0_), channel_id=1, source_target_pairs={{0,24},{8,16},{16,8},{24,0},{1,25},{9,17},{17,9},{25,1},{2,26},{10... | collective-permute-start | bytes 393224 | tf_op jit(solution)/shard_map/ppermute | solution.py:21
  21.7 0.5 collective-permute-start.8
  22.2 0.6 collective-permute-start.7
  22.8 2.7 %collective-permute-start.6 = (bf16[64,1024]{1,0:T(8,128)(2,1)S(1)}, bf16[64,1024]{1,0:T(8,128)(2,1)S(1)}, u32[]{:S(2)}, u32[]{:S(2)}) collective-permute-start(bf16[64,1024]{1,0:T(8,128)(2,1)S(1)} %shard_map.56.mine), channel_id=1, source_target_pairs={{0,4},{1,5},{2,6},{3,7},{4,0},{5,1},{6,2},{7,3},{8,12},{9,13},{10,... | collective-permute-start | bytes 393224 | tf_op jit(solution)/shard_map/ppermute | solution.py:21
  25.5 0.2 collective-permute-done.9.refs_3_
  25.6 2.5 %collective-permute-done.8.refs_2_ = bf16[64,1024]{1,0:T(8,128)(2,1)S(1)} collective-permute-done((bf16[64,1024]{1,0:T(8,128)(2,1)S(1)}, bf16[64,1024]{1,0:T(8,128)(2,1)S(1)}, u32[]{:S(2)}, u32[]{:S(2)}) %collective-permute-start.8) | collective-permute-done | bytes 131104 | tf_op jit(solution)/shard_map/ppermute | solution.py:21
  28.1 0.1 collective-permute-done.7.refs_1_
  28.2 0.2 shard_map.59
  28.3 2.5 %collective-permute-done.6.got = bf16[64,1024]{1,0:T(8,128)(2,1)S(1)} collective-permute-done((bf16[64,1024]{1,0:T(8,128)(2,1)S(1)}, bf16[64,1024]{1,0:T(8,128)(2,1)S(1)}, u32[]{:S(2)}, u32[]{:S(2)}) %collective-permute-start.6) | collective-permute-done | bytes 131104 | tf_op jit(solution)/shard_map/ppermute | solution.py:21
  30.9 0.1 shard_map.57
  31.0 0.1 collective-permute-start.12
  31.1 0.1 collective-permute-start.10
  31.1 1.8 %shard_map.60 = (f32[64,1024]{1,0:T(8,128)S(1)}, f32[64,1024]{1,0:T(8,128)S(1)}) custom-call(bf16[64,1024]{1,0:T(8,128)(2,1)S(1)} %get-tuple-element.53.user, bf16[1024,4096]{1,0:T(8,128)(2,1)S(1)} %get-tuple-element.40.refs_5_.labels, bf16[64,1024]{1,0:T(8,128)(2,1)S(1)} %get-tuple-element.56.item, bf16[1024,64]{1,0:T(8,128)(2,1)S(1)} %get-tuple-element.57.item_t), custom_call_target="tpu_custom_call" | custom-call | flops 3000000000 | bytes 1048576 | tf_op jit(solution)/shard_map/pallas_call | solution.py:35
  32.9 3.1 %collective-permute-done.12.user = bf16[64,1024]{1,0:T(8,128)(2,1)S(1)} collective-permute-done((bf16[64,1024]{1,0:T(8,128)(2,1)S(1)}, bf16[64,1024]{1,0:T(8,128)(2,1)S(1)}, u32[]{:S(2)}, u32[]{:S(2)}) %collective-permute-start.12) | collective-permute-done | bytes 131104 | tf_op jit(solution)/shard_map/ppermute | solution.py:21
  36.0 1.8 %shard_map.61 = (bf16[64,1024]{1,0:T(8,128)(2,1)S(1)}, f32[64,1024]{1,0:T(8,128)S(1)}) custom-call(bf16[64,1024]{1,0:T(8,128)(2,1)S(1)} %collective-permute-done.10.user, bf16[1024,4096]{1,0:T(8,128)(2,1)S(1)} %get-tuple-element.40.refs_5_.labels, bf16[64,1024]{1,0:T(8,128)(2,1)S(1)} %get-tuple-element.56.item, ...), custom_call_target="tpu_custom_call" | custom-call | flops 3000000000 | bytes 1048576 | tf_op jit(solution)/shard_map/pallas_call | solution.py:35
  37.8 1.7 %shard_map.62 = (f32[64,1024]{1,0:T(8,128)S(1)}, f32[64,1024]{1,0:T(8,128)S(1)}) custom-call(bf16[64,1024]{1,0:T(8,128)(2,1)S(1)} %collective-permute-done.12.user, bf16[1024,4096]{1,0:T(8,128)(2,1)S(1)} %get-tuple-element.40.refs_5_.labels, bf16[64,1024]{1,0:T(8,128)(2,1)S(1)} %get-tuple-element.56.item, bf16[1024,64]{1,0:T(8,128)(2,1)S(1)} %get-tuple-element.57.item_t, ...), custom_call_target="tpu_custom_call" | custom-call | flops 3000000000 | bytes 1048576 | tf_op jit(solution)/shard_map/pallas_call | solution.py:35
  39.5 1.7 %shard_map.63 = (bf16[64,1024]{1,0:T(8,128)(2,1)S(1)}, f32[64,1024]{1,0:T(8,128)S(1)}) custom-call(bf16[64,1024]{1,0:T(8,128)(2,1)S(1)} %collective-permute-done.13.user, bf16[1024,4096]{1,0:T(8,128)(2,1)S(1)} %get-tuple-element.40.refs_5_.labels, bf16[64,1024]{1,0:T(8,128)(2,1)S(1)} %get-tuple-element.56.item, ...), custom_call_target="tpu_custom_call" | custom-call | flops 3000000000 | bytes 1048576 | tf_op jit(solution)/shard_map/pallas_call | solution.py:35
  41.3 0.6 collective-permute-start.14
  41.8 0.1 collective-permute-start.11
  41.9 0.9 %collective-permute-done.14.refs_1_ = bf16[64,1024]{1,0:T(8,128)(2,1)S(1)} collective-permute-done((bf16[64,1024]{1,0:T(8,128)(2,1)S(1)}, bf16[64,1024]{1,0:T(8,128)(2,1)S(1)}, u32[]{:S(2)}, u32[]{:S(2)}) %collective-permute-start.14) | collective-permute-done | bytes 131104 | tf_op jit(solution)/shard_map/ppermute | solution.py:21
  42.8 0.2 collective-permute-start.15
  43.0 0.1 collective-permute-done.11.refs_1_
  43.2 5.5 %collective-permute-done.15.refs_2_ = bf16[64,1024]{1,0:T(8,128)(2,1)S(1)} collective-permute-done((bf16[64,1024]{1,0:T(8,128)(2,1)S(1)}, bf16[64,1024]{1,0:T(8,128)(2,1)S(1)}, u32[]{:S(2)}, u32[]{:S(2)}) %collective-permute-start.15) | collective-permute-done | bytes 131104 | tf_op jit(solution)/shard_map/ppermute | solution.py:21
  48.7 1.7 %collective-permute-start.16 = (bf16[64,1024]{1,0:T(8,128)(2,1)S(1)}, bf16[64,1024]{1,0:T(8,128)(2,1)S(1)}, u32[]{:S(2)}, u32[]{:S(2)}) collective-permute-start(bf16[64,1024]{1,0:T(8,128)(2,1)S(1)} %shard_map.65.mine), channel_id=1, source_target_pairs={{0,4},{1,5},{2,6},{3,7},{4,0},{5,1},{6,2},{7,3},{8,12},{9,13},{10,... | collective-permute-start | bytes 393224 | tf_op jit(solution)/shard_map/ppermute | solution.py:21
  50.5 1.6 %collective-permute-start.17 = (bf16[64,256]{1,0:T(8,128)(2,1)S(1)}, bf16[64,256]{1,0:T(8,128)(2,1)S(1)}, u32[]{:S(2)}, u32[]{:S(2)}) collective-permute-start(bf16[64,256]{1,0:T(8,128)(2,1)S(1)} %get-tuple-element.66), channel_id=1, source_target_pairs={{0,8},{8,0},{16,24},{24,16},{1,9},{9,1},{17,25},{25,17},{2,10},{10... | collective-permute-start | bytes 98312 | tf_op jit(solution)/shard_map/ppermute | solution.py:21
  52.0 1.5 %collective-permute-start.18 = (bf16[64,256]{1,0:T(8,128)(2,1)S(1)}, bf16[64,256]{1,0:T(8,128)(2,1)S(1)}, u32[]{:S(2)}, u32[]{:S(2)}) collective-permute-start(bf16[64,256]{1,0:T(8,128)(2,1)S(1)} %get-tuple-element.67), channel_id=1, source_target_pairs={{0,16},{8,24},{16,0},{24,8},{1,17},{9,25},{17,1},{25,9},{2,18},{10... | collective-permute-start | bytes 98312 | tf_op jit(solution)/shard_map/ppermute | solution.py:21
  53.6 0.5 collective-permute-start.19
  54.0 0.4 collective-permute-done.17.refs_0_
  54.5 1.5 %collective-permute-done.18.refs_1_ = bf16[64,256]{1,0:T(8,128)(2,1)S(1)} collective-permute-done((bf16[64,256]{1,0:T(8,128)(2,1)S(1)}, bf16[64,256]{1,0:T(8,128)(2,1)S(1)}, u32[]{:S(2)}, u32[]{:S(2)}) %collective-permute-start.18) | collective-permute-done | bytes 32800 | tf_op jit(solution)/shard_map/ppermute | solution.py:21
  56.0 2.4 %collective-permute-done.19.refs_2_ = bf16[64,256]{1,0:T(8,128)(2,1)S(1)} collective-permute-done((bf16[64,256]{1,0:T(8,128)(2,1)S(1)}, bf16[64,256]{1,0:T(8,128)(2,1)S(1)}, u32[]{:S(2)}, u32[]{:S(2)}) %collective-permute-start.19) | collective-permute-done | bytes 32800 | tf_op jit(solution)/shard_map/ppermute | solution.py:21
  58.4 0.1 shard_map.67.refs_0_
  58.4 1.8 %collective-permute-start.21 = (bf16[64,1024]{1,0:T(8,128)(2,1)S(1)}, bf16[64,1024]{1,0:T(8,128)(2,1)S(1)}, u32[]{:S(2)}, u32[]{:S(2)}) collective-permute-start(bf16[64,1024]{1,0:T(8,128)(2,1)S(1)} %shard_map.67.refs_0_), channel_id=1, source_target_pairs={{0,2},{1,3},{2,0},{3,1},{4,6},{5,7},{6,4},{7,5},{8,10},{9,11},{10,... | collective-permute-start | bytes 393224 | tf_op jit(solution)/shard_map/ppermute | solution.py:21
  60.3 3.2 %collective-permute-done.21.refs_2_ = bf16[64,1024]{1,0:T(8,128)(2,1)S(1)} collective-permute-done((bf16[64,1024]{1,0:T(8,128)(2,1)S(1)}, bf16[64,1024]{1,0:T(8,128)(2,1)S(1)}, u32[]{:S(2)}, u32[]{:S(2)}) %collective-permute-start.21) | collective-permute-done | bytes 131104 | tf_op jit(solution)/shard_map/ppermute | solution.py:21
  63.5 0.7 shard_map.69
  64.1 0.7 %collective-permute-done.22.refs_3_ = bf16[64,1024]{1,0:T(8,128)(2,1)S(1)} collective-permute-done((bf16[64,1024]{1,0:T(8,128)(2,1)S(1)}, bf16[64,1024]{1,0:T(8,128)(2,1)S(1)}, u32[]{:S(2)}, u32[]{:S(2)}) %collective-permute-start.22) | collective-permute-done | bytes 131104 | tf_op jit(solution)/shard_map/ppermute | solution.py:21
  64.8 1.1 %shard_map.68 = f32[64,4096]{1,0:T(8,128)} custom-call(f32[64,4096]{1,0:T(8,128)S(1)} %get-tuple-element.39.refs_4_.users, bf16[64,1024]{1,0:T(8,128)(2,1)S(1)} %shard_map.67.refs_0_, bf16[64,1024]{1,0:T(8,128)(2,1)S(1)} %collective-permute-done.20.refs_1_, bf16[64,1024]{1,0:T(8,128)(2,1)S(1)} %collective-permute-done.21.refs_2_, ...), custom_call_target="tpu_custom_call" | custom-call | bytes 1048576 | tf_op jit(solution)/shard_map/pallas_call | solution.py:35
  (22 shorter events, 0.3 us)
Async XLA Ops:
  0.6 10.4 %collective-permute-start = (f32[64,256]{1,0:T(8,128)}, f32[64,256]{1,0:T(8,128)S(1)}, u32[]{:S(2)}, u32[]{:S(2)}) collective-permute-start(f32[64,256]{1,0:T(8,128)} %items_hbm.1), channel_id=1, source_target_pairs={{0,8},{8,0},{16,24},{24,16},{1,9},{9,1},{17,25},{25,17},{2,10},{10... | collective-permute-start | bytes 196616 | tf_op jit(solution)/shard_map/ppermute | solution.py:21
  3.6 7.4 %collective-permute-start.2 = (f32[64,256]{1,0:T(8,128)}, f32[64,256]{1,0:T(8,128)S(1)}, u32[]{:S(2)}, u32[]{:S(2)}) collective-permute-start(f32[64,256]{1,0:T(8,128)} %items_hbm.1), channel_id=1, source_target_pairs={{0,24},{8,16},{16,8},{24,0},{1,25},{9,17},{17,9},{25,1},{2,26},{10... | collective-permute-start | bytes 196616 | tf_op jit(solution)/shard_map/ppermute | solution.py:21
  5.1 5.9 %collective-permute-start.1 = (f32[64,256]{1,0:T(8,128)}, f32[64,256]{1,0:T(8,128)S(1)}, u32[]{:S(2)}, u32[]{:S(2)}) collective-permute-start(f32[64,256]{1,0:T(8,128)} %items_hbm.1), channel_id=1, source_target_pairs={{0,16},{8,24},{16,0},{24,8},{1,17},{9,25},{17,1},{25,9},{2,18},{10... | collective-permute-start | bytes 196616 | tf_op jit(solution)/shard_map/ppermute | solution.py:21
  5.2 1.2 %copy-start = (f32[64,4096]{1,0:T(8,128)S(1)}, f32[64,4096]{1,0:T(8,128)}, u32[]{:S(2)}) copy-start(f32[64,4096]{1,0:T(8,128)} %users_hbm.1) | copy-start | bytes 3145732
  6.4 0.8 %copy-start.1 = (f32[64,256]{1,0:T(8,128)S(1)}, f32[64,256]{1,0:T(8,128)}, u32[]{:S(2)}) copy-start(f32[64,256]{1,0:T(8,128)} %items_hbm.1) | copy-start | bytes 196612
  12.5 3.3 %collective-permute-start.4 = (bf16[64,1024]{1,0:T(8,128)(2,1)S(1)}, bf16[64,1024]{1,0:T(8,128)(2,1)S(1)}, u32[]{:S(2)}, u32[]{:S(2)}) collective-permute-start(bf16[64,1024]{1,0:T(8,128)(2,1)S(1)} %get-tuple-element.52), channel_id=1, source_target_pairs={{0,1},{1,0},{2,3},{3,2},{4,5},{5,4},{6,7},{7,6},{8,9},{9,8},{10,11... | collective-permute-start | bytes 393224 | tf_op jit(solution)/shard_map/ppermute | solution.py:21
  15.2 7.6 %collective-permute-start.3 = (bf16[64,1024]{1,0:T(8,128)(2,1)S(1)}, bf16[64,1024]{1,0:T(8,128)(2,1)S(1)}, u32[]{:S(2)}, u32[]{:S(2)}) collective-permute-start(bf16[64,1024]{1,0:T(8,128)(2,1)S(1)} %get-tuple-element.50), channel_id=1, source_target_pairs={{0,1},{1,0},{2,3},{3,2},{4,5},{5,4},{6,7},{7,6},{8,9},{9,8},{10,11... | collective-permute-start | bytes 393224 | tf_op jit(solution)/shard_map/ppermute | solution.py:21
  15.8 7.0 %collective-permute-start.5 = (bf16[64,1024]{1,0:T(8,128)(2,1)S(1)}, bf16[64,1024]{1,0:T(8,128)(2,1)S(1)}, u32[]{:S(2)}, u32[]{:S(2)}) collective-permute-start(bf16[64,1024]{1,0:T(8,128)(2,1)S(1)} %shard_map.55), channel_id=1, source_target_pairs={{0,2},{1,3},{2,0},{3,1},{4,6},{5,7},{6,4},{7,5},{8,10},{9,11},{10,... | collective-permute-start | bytes 393224 | tf_op jit(solution)/shard_map/ppermute | solution.py:21
  19.2 6.5 %collective-permute-start.9 = (bf16[64,1024]{1,0:T(8,128)(2,1)S(1)}, bf16[64,1024]{1,0:T(8,128)(2,1)S(1)}, u32[]{:S(2)}, u32[]{:S(2)}) collective-permute-start(bf16[64,1024]{1,0:T(8,128)(2,1)S(1)} %shard_map.58.refs_0_), channel_id=1, source_target_pairs={{0,24},{8,16},{16,8},{24,0},{1,25},{9,17},{17,9},{25,1},{2,26},{10... | collective-permute-start | bytes 393224 | tf_op jit(solution)/shard_map/ppermute | solution.py:21
  21.7 6.4 %collective-permute-start.8 = (bf16[64,1024]{1,0:T(8,128)(2,1)S(1)}, bf16[64,1024]{1,0:T(8,128)(2,1)S(1)}, u32[]{:S(2)}, u32[]{:S(2)}) collective-permute-start(bf16[64,1024]{1,0:T(8,128)(2,1)S(1)} %shard_map.58.refs_0_), channel_id=1, source_target_pairs={{0,16},{8,24},{16,0},{24,8},{1,17},{9,25},{17,1},{25,9},{2,18},{10... | collective-permute-start | bytes 393224 | tf_op jit(solution)/shard_map/ppermute | solution.py:21
  22.2 6.0 %collective-permute-start.7 = (bf16[64,1024]{1,0:T(8,128)(2,1)S(1)}, bf16[64,1024]{1,0:T(8,128)(2,1)S(1)}, u32[]{:S(2)}, u32[]{:S(2)}) collective-permute-start(bf16[64,1024]{1,0:T(8,128)(2,1)S(1)} %shard_map.58.refs_0_), channel_id=1, source_target_pairs={{0,8},{8,0},{16,24},{24,16},{1,9},{9,1},{17,25},{25,17},{2,10},{10... | collective-permute-start | bytes 393224 | tf_op jit(solution)/shard_map/ppermute | solution.py:21
  22.8 8.1 %collective-permute-start.6 = (bf16[64,1024]{1,0:T(8,128)(2,1)S(1)}, bf16[64,1024]{1,0:T(8,128)(2,1)S(1)}, u32[]{:S(2)}, u32[]{:S(2)}) collective-permute-start(bf16[64,1024]{1,0:T(8,128)(2,1)S(1)} %shard_map.56.mine), channel_id=1, source_target_pairs={{0,4},{1,5},{2,6},{3,7},{4,0},{5,1},{6,2},{7,3},{8,12},{9,13},{10,... | collective-permute-start | bytes 393224 | tf_op jit(solution)/shard_map/ppermute | solution.py:21
  31.0 5.0 %collective-permute-start.12 = (bf16[64,1024]{1,0:T(8,128)(2,1)S(1)}, bf16[64,1024]{1,0:T(8,128)(2,1)S(1)}, u32[]{:S(2)}, u32[]{:S(2)}) collective-permute-start(bf16[64,1024]{1,0:T(8,128)(2,1)S(1)} %get-tuple-element.53.user), channel_id=1, source_target_pairs={{0,2},{1,3},{2,0},{3,1},{4,6},{5,7},{6,4},{7,5},{8,10},{9,11},{10,... | collective-permute-start | bytes 393224 | tf_op jit(solution)/shard_map/ppermute | solution.py:21
  31.1 4.9 %collective-permute-start.10 = (bf16[64,1024]{1,0:T(8,128)(2,1)S(1)}, bf16[64,1024]{1,0:T(8,128)(2,1)S(1)}, u32[]{:S(2)}, u32[]{:S(2)}) collective-permute-start(bf16[64,1024]{1,0:T(8,128)(2,1)S(1)} %get-tuple-element.53.user), channel_id=1, source_target_pairs={{0,1},{1,0},{2,3},{3,2},{4,5},{5,4},{6,7},{7,6},{8,9},{9,8},{10,11... | collective-permute-start | bytes 393224 | tf_op jit(solution)/shard_map/ppermute | solution.py:21
  36.0 3.5 %collective-permute-start.13 = (bf16[64,1024]{1,0:T(8,128)(2,1)S(1)}, bf16[64,1024]{1,0:T(8,128)(2,1)S(1)}, u32[]{:S(2)}, u32[]{:S(2)}) collective-permute-start(bf16[64,1024]{1,0:T(8,128)(2,1)S(1)} %collective-permute-done.12.user), channel_id=1, source_target_pairs={{0,1},{1,0},{2,3},{3,2},{4,5},{5,4},{6,7},{7,6},{8,9},{9,8},{10,11... | collective-permute-start | bytes 393224 | tf_op jit(solution)/shard_map/ppermute | solution.py:21
  41.3 1.6 %collective-permute-start.14 = (bf16[64,1024]{1,0:T(8,128)(2,1)S(1)}, bf16[64,1024]{1,0:T(8,128)(2,1)S(1)}, u32[]{:S(2)}, u32[]{:S(2)}) collective-permute-start(bf16[64,1024]{1,0:T(8,128)(2,1)S(1)} %get-tuple-element.64), channel_id=1, source_target_pairs={{0,1},{1,0},{2,3},{3,2},{4,5},{5,4},{6,7},{7,6},{8,9},{9,8},{10,11... | collective-permute-start | bytes 393224 | tf_op jit(solution)/shard_map/ppermute | solution.py:21
  41.8 1.3 %collective-permute-start.11 = (bf16[64,1024]{1,0:T(8,128)(2,1)S(1)}, bf16[64,1024]{1,0:T(8,128)(2,1)S(1)}, u32[]{:S(2)}, u32[]{:S(2)}) collective-permute-start(bf16[64,1024]{1,0:T(8,128)(2,1)S(1)} %get-tuple-element.60), channel_id=1, source_target_pairs={{0,1},{1,0},{2,3},{3,2},{4,5},{5,4},{6,7},{7,6},{8,9},{9,8},{10,11... | collective-permute-start | bytes 393224 | tf_op jit(solution)/shard_map/ppermute | solution.py:21
  42.8 5.8 %collective-permute-start.15 = (bf16[64,1024]{1,0:T(8,128)(2,1)S(1)}, bf16[64,1024]{1,0:T(8,128)(2,1)S(1)}, u32[]{:S(2)}, u32[]{:S(2)}) collective-permute-start(bf16[64,1024]{1,0:T(8,128)(2,1)S(1)} %shard_map.64), channel_id=1, source_target_pairs={{0,2},{1,3},{2,0},{3,1},{4,6},{5,7},{6,4},{7,5},{8,10},{9,11},{10,... | collective-permute-start | bytes 393224 | tf_op jit(solution)/shard_map/ppermute | solution.py:21
  48.7 9.7 %collective-permute-start.16 = (bf16[64,1024]{1,0:T(8,128)(2,1)S(1)}, bf16[64,1024]{1,0:T(8,128)(2,1)S(1)}, u32[]{:S(2)}, u32[]{:S(2)}) collective-permute-start(bf16[64,1024]{1,0:T(8,128)(2,1)S(1)} %shard_map.65.mine), channel_id=1, source_target_pairs={{0,4},{1,5},{2,6},{3,7},{4,0},{5,1},{6,2},{7,3},{8,12},{9,13},{10,... | collective-permute-start | bytes 393224 | tf_op jit(solution)/shard_map/ppermute | solution.py:21
  50.5 4.0 %collective-permute-start.17 = (bf16[64,256]{1,0:T(8,128)(2,1)S(1)}, bf16[64,256]{1,0:T(8,128)(2,1)S(1)}, u32[]{:S(2)}, u32[]{:S(2)}) collective-permute-start(bf16[64,256]{1,0:T(8,128)(2,1)S(1)} %get-tuple-element.66), channel_id=1, source_target_pairs={{0,8},{8,0},{16,24},{24,16},{1,9},{9,1},{17,25},{25,17},{2,10},{10... | collective-permute-start | bytes 98312 | tf_op jit(solution)/shard_map/ppermute | solution.py:21
  52.0 3.9 %collective-permute-start.18 = (bf16[64,256]{1,0:T(8,128)(2,1)S(1)}, bf16[64,256]{1,0:T(8,128)(2,1)S(1)}, u32[]{:S(2)}, u32[]{:S(2)}) collective-permute-start(bf16[64,256]{1,0:T(8,128)(2,1)S(1)} %get-tuple-element.67), channel_id=1, source_target_pairs={{0,16},{8,24},{16,0},{24,8},{1,17},{9,25},{17,1},{25,9},{2,18},{10... | collective-permute-start | bytes 98312 | tf_op jit(solution)/shard_map/ppermute | solution.py:21
  53.6 4.8 %collective-permute-start.19 = (bf16[64,256]{1,0:T(8,128)(2,1)S(1)}, bf16[64,256]{1,0:T(8,128)(2,1)S(1)}, u32[]{:S(2)}, u32[]{:S(2)}) collective-permute-start(bf16[64,256]{1,0:T(8,128)(2,1)S(1)} %get-tuple-element.68), channel_id=1, source_target_pairs={{0,24},{8,16},{16,8},{24,0},{1,25},{9,17},{17,9},{25,1},{2,26},{10... | collective-permute-start | bytes 98312 | tf_op jit(solution)/shard_map/ppermute | solution.py:21
  58.4 5.0 %collective-permute-start.21 = (bf16[64,1024]{1,0:T(8,128)(2,1)S(1)}, bf16[64,1024]{1,0:T(8,128)(2,1)S(1)}, u32[]{:S(2)}, u32[]{:S(2)}) collective-permute-start(bf16[64,1024]{1,0:T(8,128)(2,1)S(1)} %shard_map.67.refs_0_), channel_id=1, source_target_pairs={{0,2},{1,3},{2,0},{3,1},{4,6},{5,7},{6,4},{7,5},{8,10},{9,11},{10,... | collective-permute-start | bytes 393224 | tf_op jit(solution)/shard_map/ppermute | solution.py:21
  60.2 3.9 %collective-permute-start.20 = (bf16[64,1024]{1,0:T(8,128)(2,1)S(1)}, bf16[64,1024]{1,0:T(8,128)(2,1)S(1)}, u32[]{:S(2)}, u32[]{:S(2)}) collective-permute-start(bf16[64,1024]{1,0:T(8,128)(2,1)S(1)} %shard_map.67.refs_0_), channel_id=1, source_target_pairs={{0,1},{1,0},{2,3},{3,2},{4,5},{5,4},{6,7},{7,6},{8,9},{9,8},{10,11... | collective-permute-start | bytes 393224 | tf_op jit(solution)/shard_map/ppermute | solution.py:21
  63.5 1.3 %collective-permute-start.22 = (bf16[64,1024]{1,0:T(8,128)(2,1)S(1)}, bf16[64,1024]{1,0:T(8,128)(2,1)S(1)}, u32[]{:S(2)}, u32[]{:S(2)}) collective-permute-start(bf16[64,1024]{1,0:T(8,128)(2,1)S(1)} %collective-permute-done.21.refs_2_), channel_id=1, source_target_pairs={{0,1},{1,0},{2,3},{3,2},{4,5},{5,4},{6,7},{7,6},{8,9},{9,8},{10,11... | collective-permute-start | bytes 393224 | tf_op jit(solution)/shard_map/ppermute | solution.py:21

commit v5 on v4

--- a/solution.py
+++ b/solution.py
@@ -105,25 +105,14 @@
     item_t[...] = (rounded * jnp.asarray(0.5, bf16)).T
 
 
-def load_and_own_rows(rows_count, labels_hbm, users_hbm, items_hbm, labels, users, items, grad_user, grad_item, item, item_t, sems):
-    row, block = lax.axis_index("row"), items.shape[1]
-
-    def rows_of(o):
-        at = span(row ^ o, block)
-        return pltpu.make_async_copy(labels_hbm.at[at, :], labels.at[at, :], sems.at[2 + o])
-
-    copies = [
-        pltpu.make_async_copy(items_hbm, items, sems.at[0]),
-        pltpu.make_async_copy(users_hbm, users, sems.at[1]),
-    ] + [rows_of(o) for o in range(rows_count)]
-    for copy in copies:
-        copy.start()
-    copies[0].wait()
-    own = span(row, block)
+def hand_on(items, out):
+    out[...] = items[...]
+
+
+def own_rows(labels, users, items, grad_user, grad_item, item, item_t):
+    own = span(lax.axis_index("row"), items.shape[1])
     put_items(items[...], item, item_t)
     grad_item[...] = jnp.zeros_like(grad_item)
-    copies[1].wait()
-    copies[2].wait()
     width = users.shape[1]
     tile = min(TILE_USERS, width)
     for at in range(0, width, tile):
@@ -134,8 +123,6 @@
         residual = (jnp.abs(weights) * jnp.tanh(half_scores) - weights).astype(bf16)
         grad_user[:, here] = jnp.dot(item[...], residual, preferred_element_type=f32)
         grad_item[:, own] += lax.dot_general(user, residual, (((1,), (1,)), ((), ())), preferred_element_type=f32)
-    for copy in copies[3:]:
-        copy.wait()
 
 
 def first_open(rows_count, half, *refs):
@@ -258,7 +245,7 @@
     work = 3 * 10**9
     wide = ((rank, items_dev), f32)
     item_pair = [((rank, items_dev), bf16), ((items_dev, rank), bf16)]
-    sent, kept = ((rank, quarter), bf16), ((rank, quarter), f32)
+    sent_b, sent, kept = ((rank, quarter), bf16), ((rank, quarter), f32), ((rank, quarter), f32)
     others = list(range(1, rows_count))
 
     def along_z(block, level):
@@ -277,20 +264,20 @@
             (block,) = call(functools.partial(join, level), outs, block, along_z(block, level))
         return block
 
-    def meet(mine, *terms):
+    def meet(mine, *terms, behind):
         if levels > 2:
             (mine,) = call(combine, [kept], mine, *terms)
             mine, terms = narrow(mine), ()
         (mine,) = call(combine, [(mine.shape, bf16)], mine, *terms)
-        return mine, along_z(mine, levels - 1)
-
+        mine, behind = lax.optimization_barrier((mine, behind))
+        return mine, along_z(mine, levels - 1), behind
+
+    (items_v,) = call(hand_on, [(items.shape, f32)], items, flops=10 * work)
     item_blocks = [swap(items, "row", o) for o in others]
-    labels, users_v, items_v, grad_user, grad = call(
-        functools.partial(load_and_own_rows, rows_count),
-        [(preference.shape, bf16), (users.shape, f32), (items.shape, f32), (users.shape, f32), wide],
-        preference, users, items,
-        scratch=[VMEM((rank, block), bf16), VMEM((block, rank), bf16), pltpu.SemaphoreType.DMA((rows_count + 2,))],
-        space=HBM, flops=work, grant=42,
+    labels, users_v = preference, users
+    grad_user, grad = call(
+        own_rows, [(users.shape, f32), wide], labels, users_v, items_v,
+        scratch=[VMEM((rank, block), bf16), VMEM((block, rank), bf16)], flops=work,
     )
     send, grad, item_all, item, item_t = call(
         functools.partial(first_open, rows_count, half), [sent, wide, wide] + item_pair,
@@ -305,23 +292,20 @@
 
     recv = swap(send, "col", 1)
     mine, grad = first(True, False, grad)
-    (piece,) = call(combine, [sent], mine, recv)
+    (piece,) = call(combine, [sent_b], mine, recv)
     near = along_z(piece, 0)
+    piece, grad = lax.optimization_barrier((piece, grad))
     send, grad = first(False, True, grad)
     recv = swap(send, "col", 1)
     mine, grad = first(True, True, grad)
     (grad_b,) = call(round_items, [(wide[0], bf16)], grad)
+    mine, got, grad_b = meet(mine, recv, near, behind=grad_b)
     grads = [grad_b] + [swap(grad_b, "row", o) for o in others]
-    mine, got = meet(mine, recv, near)
     updated = [(mine.shape, f32), (mine.shape, bf16)]
     new, new_b = call(functools.partial(update_users, user_rate, half), updated, mine, got, users_v)
 
-    def gather(block):
-        own_keep = widen(block)
-        own_send = along_z(own_keep, 0)
-        return own_keep, swap(own_keep, "col", 1), own_send, swap(own_send, "col", 1)
-
-    own_keep, peer_keep, own_send, peer_send = gather(new_b)
+    own_keep = widen(new_b)
+    own_send, peer_keep = along_z(own_keep, 0), swap(own_keep, "col", 1)
     item_own, item, item_t = call(
         functools.partial(second_start, item_rate, rows_count), [(items.shape, f32)] + item_pair, item_all, *grads
     )
@@ -337,22 +321,27 @@
     )
     send, grad = second(False, True, peer_keep, grad)
     recv = swap(send, "col", 1)
+    own_send, grad = lax.optimization_barrier((own_send, grad))
+    peer_send = swap(own_send, "col", 1)
     mine_send, grad = second(True, False, own_send, grad)
     send, grad = second(False, False, peer_send, grad)
     recv_send = swap(send, "col", 1)
-    (piece,) = call(combine, [sent], mine_send, recv_send)
+    (piece,) = call(combine, [sent_b], mine_send, recv_send)
     near = along_z(piece, 0)
     item_pieces = call(cut_items, [(items.shape, f32)] + [(items.shape, bf16)] * len(others), grad)
+    mine, got, item_pieces = meet(mine, recv, near, behind=item_pieces)
     item_got = [swap(p, "row", o) for p, o in zip(item_pieces[1:], others)]
-    mine, got = meet(mine, recv, near)
-    got, *item_got = lax.optimization_barrier((got, *item_got))
+    (new_items,) = call(
+        functools.partial(finish_items, item_rate), [(items.shape, f32)], item_own, item_pieces[0], *item_got
+    )
+    got, new_items = lax.optimization_barrier((got, new_items))
     (delta,) = call(
         functools.partial(update_last, user_rate, half), [(mine.shape, bf16)], mine, got, users_v, new
     )
-    (new_items,) = call(
-        functools.partial(finish_items, item_rate), [(items.shape, f32)], item_own, item_pieces[0], *item_got
-    )
-    (new_users,) = call(functools.partial(finish_users, half), [(users.shape, f32)], users_v, *gather(delta))
+    own_keep = widen(delta)
+    own_send = along_z(own_keep, 0)
+    pieces = own_keep, swap(own_keep, "col", 1), own_send, swap(own_send, "col", 1)
+    (new_users,) = call(functools.partial(finish_users, half), [(users.shape, f32)], users_v, *pieces)
     return new_users, new_items
 
 

time: 66.1 us -> 61.9 us (0.936)
  waiting for transfers between devices: 23.2 us -> 20.7 us
  Pallas kernels: 18.3 us -> 16.5 us
  local copies, waits for them, and re-layouts: 2.06 us -> 0.91 us
  starting transfers between devices: 21.6 us -> 22.7 us
    ppermute x23, waiting for transfers between devices: 23.2 us -> 20.7 us  [swap(): lax.ppermute(block, axis, [(i, i ^ distance) for i in range(lax.axis_size...]
    pallas_call x20 -> x21, Pallas kernels: 18.3 us -> 16.5 us  [call(): pl.pallas_call(kernel, in_specs=[pl.BlockSpec(memory_space=space)] * len(...]
    unnamed x4 -> x6, local copies, waits for them, and re-layouts: 2.06 us -> 0.91 us
    ppermute x23, starting transfers between devices: 21.6 us -> 22.7 us  [swap(): lax.ppermute(block, axis, [(i, i ^ distance) for i in range(lax.axis_size...]
  transfers between devices with their start and end apart: 23 -> 23, of which waited for: 13 -> 14; matrix products, arithmetic and copies ran while one was open for 0% -> 0% of each run, Pallas kernels for 21% -> 20%
where the time goes in v5:
time: 61.9 us; the launch traced here: 61.7 us
  starting transfers between devices  22.7 us (37%)
  waiting for transfers between devices  20.7 us (33%)
  Pallas kernels  16.5 us (27%)
  local copies, waits for them, and re-layouts  0.91 us (1%)
  between operations  0.83 us (1%)
    ppermute x23, starting transfers between devices, swap(): lax.ppermute(block, axis, [(i, i ^ distance) for i in range(lax.axis_size...  22.7 us
    ppermute x23, waiting for transfers between devices, swap(): lax.ppermute(block, axis, [(i, i ^ distance) for i in range(lax.axis_size...  20.7 us
    pallas_call x21, Pallas kernels, call(): pl.pallas_call(kernel, in_specs=[pl.BlockSpec(memory_space=space)] * len(...  16.5 us
  transfers between devices with their start and end apart: 23, of which 14 were waited for; matrix products, arithmetic and copies ran while one was open for 0% of the time, Pallas kernels for 20%

profile of v5, /device:TPU:0, one launch (start us, length us, event | category | flops | bytes accessed | tf_op | source)
XLA Modules:
  0.0 61.7 jit_solution(17439502762568279618)
XLA Ops:
  0.6 3.0 %collective-permute-start = (f32[64,256]{1,0:T(8,128)}, f32[64,256]{1,0:T(8,128)S(1)}, u32[]{:S(2)}, u32[]{:S(2)}) collective-permute-start(f32[64,256]{1,0:T(8,128)} %items.1), channel_id=1, source_target_pairs={{0,8},{8,0},{16,24},{24,16},{1,9},{9,1},{17,25},{25,17},{2,10},{10... | collective-permute-start | bytes 196616 | tf_op jit(solution)/shard_map/ppermute | solution.py:21
  3.7 1.5 %collective-permute-start.2 = (f32[64,256]{1,0:T(8,128)}, f32[64,256]{1,0:T(8,128)S(1)}, u32[]{:S(2)}, u32[]{:S(2)}) collective-permute-start(f32[64,256]{1,0:T(8,128)} %items.1), channel_id=1, source_target_pairs={{0,24},{8,16},{16,8},{24,0},{1,25},{9,17},{17,9},{25,1},{2,26},{10... | collective-permute-start | bytes 196616 | tf_op jit(solution)/shard_map/ppermute | solution.py:21
  5.2 0.9 %copy-done.2 = f32[64,256]{1,0:T(8,128)S(1)} copy-done((f32[64,256]{1,0:T(8,128)S(1)}, f32[64,256]{1,0:T(8,128)}, u32[]{:S(2)}) %copy-start.2) | copy-done | bytes 65560
  6.1 2.0 %shard_map.51 = (f32[64,4096]{1,0:T(8,128)S(1)}, f32[64,1024]{1,0:T(8,128)S(1)}) custom-call(bf16[1024,4096]{1,0:T(8,128)(2,1)S(1)} %copy-done, f32[64,4096]{1,0:T(8,128)S(1)} %copy-done.1, f32[64,256]{1,0:T(8,128)S(1)} %shard_map.50.items.refs_0_), custom_call_target="tpu_custom_call" | custom-call | flops 3000000000 | bytes 1048576 | tf_op jit(solution)/shard_map/pallas_call | solution.py:35
  8.2 0.9 %collective-permute-done.2.refs_3_ = f32[64,256]{1,0:T(8,128)S(1)} collective-permute-done((f32[64,256]{1,0:T(8,128)}, f32[64,256]{1,0:T(8,128)S(1)}, u32[]{:S(2)}, u32[]{:S(2)}) %collective-permute-start.2) | collective-permute-done | bytes 65568 | tf_op jit(solution)/shard_map/ppermute | solution.py:21
  9.1 0.8 %collective-permute-done.1.refs_2_ = f32[64,256]{1,0:T(8,128)S(1)} collective-permute-done((f32[64,256]{1,0:T(8,128)}, f32[64,256]{1,0:T(8,128)S(1)}, u32[]{:S(2)}, u32[]{:S(2)}) %collective-permute-start.1) | collective-permute-done | bytes 65568 | tf_op jit(solution)/shard_map/ppermute | solution.py:21
  9.9 1.4 %shard_map.52 = (f32[64,1024]{1,0:T(8,128)S(1)}, f32[64,1024]{1,0:T(8,128)S(1)}, f32[64,1024]{1,0:T(8,128)S(1)}, bf16[64,1024]{1,0:T(8,128)(2,1)S(1)}, bf16[1024,64]{1,0:T(8,128)(2,1)S(1)}) custom-call(f32[64,256]{1,0:T(8,128)S(1)} %shard_map.50.items.refs_0_, f32[64,256]{1,0:T(8,128)S(1)} %collective-permute-done.refs_1_, ...), custom_call_target="tpu_custom_call" | custom-call | flops 3000000000 | bytes 1048576 | tf_op jit(solution)/shard_map/pallas_call | solution.py:35
  11.3 0.1 collective-permute-start.3
  11.4 1.3 %shard_map.53 = (f32[64,1024]{1,0:T(8,128)S(1)}, f32[64,1024]{1,0:T(8,128)S(1)}) custom-call(f32[64,4096]{1,0:T(8,128)S(1)} %copy-done.1, bf16[1024,4096]{1,0:T(8,128)(2,1)S(1)} %copy-done, f32[64,4096]{1,0:T(8,128)S(1)} %get-tuple-element.44.refs_6_.grad_user, bf16[64,1024]{1,0:T(8,128)(2,1)S(1)} %get-tuple-element.46.item, ...), custom_call_target="tpu_custom_call" | custom-call | flops 3000000000 | bytes 1048576 | tf_op jit(solution)/shard_map/pallas_call | solution.py:35
  12.7 0.2 collective-permute-done.3.refs_1_
  12.9 1.6 %collective-permute-start.5 = (bf16[64,1024]{1,0:T(8,128)(2,1)S(1)}, bf16[64,1024]{1,0:T(8,128)(2,1)S(1)}, u32[]{:S(2)}, u32[]{:S(2)}) collective-permute-start(bf16[64,1024]{1,0:T(8,128)(2,1)S(1)} %shard_map.54), channel_id=1, source_target_pairs={{0,2},{1,3},{2,0},{3,1},{4,6},{5,7},{6,4},{7,5},{8,10},{9,11},{10,... | collective-permute-start | bytes 393224 | tf_op jit(solution)/shard_map/ppermute | solution.py:21
  14.6 1.3 %shard_map.55 = (f32[64,1024]{1,0:T(8,128)S(1)}, f32[64,1024]{1,0:T(8,128)S(1)}) custom-call(f32[64,4096]{1,0:T(8,128)S(1)} %copy-done.1, bf16[1024,4096]{1,0:T(8,128)(2,1)S(1)} %copy-done, f32[64,4096]{1,0:T(8,128)S(1)} %get-tuple-element.44.refs_6_.grad_user, bf16[64,1024]{1,0:T(8,128)(2,1)S(1)} %get-tuple-element.46.item, ...), custom_call_target="tpu_custom_call" | custom-call | flops 3000000000 | bytes 1048576 | tf_op jit(solution)/shard_map/pallas_call | solution.py:35
  15.9 0.1 collective-permute-start.4
  16.0 1.3 %shard_map.56 = (f32[64,1024]{1,0:T(8,128)S(1)}, f32[64,1024]{1,0:T(8,128)S(1)}) custom-call(f32[64,4096]{1,0:T(8,128)S(1)} %copy-done.1, bf16[1024,4096]{1,0:T(8,128)(2,1)S(1)} %copy-done, f32[64,4096]{1,0:T(8,128)S(1)} %get-tuple-element.44.refs_6_.grad_user, bf16[64,1024]{1,0:T(8,128)(2,1)S(1)} %get-tuple-element.46.item, ...), custom_call_target="tpu_custom_call" | custom-call | flops 3000000000 | bytes 1048576 | tf_op jit(solution)/shard_map/pallas_call | solution.py:35
  17.3 1.4 %collective-permute-done.5.refs_2_ = bf16[64,1024]{1,0:T(8,128)(2,1)S(1)} collective-permute-done((bf16[64,1024]{1,0:T(8,128)(2,1)S(1)}, bf16[64,1024]{1,0:T(8,128)(2,1)S(1)}, u32[]{:S(2)}, u32[]{:S(2)}) %collective-permute-start.5) | collective-permute-done | bytes 131104 | tf_op jit(solution)/shard_map/ppermute | solution.py:21
  18.7 2.6 %collective-permute-start.6 = (bf16[64,1024]{1,0:T(8,128)(2,1)S(1)}, bf16[64,1024]{1,0:T(8,128)(2,1)S(1)}, u32[]{:S(2)}, u32[]{:S(2)}) collective-permute-start(bf16[64,1024]{1,0:T(8,128)(2,1)S(1)} %shard_map.57.mine), channel_id=1, source_target_pairs={{0,4},{1,5},{2,6},{3,7},{4,0},{5,1},{6,2},{7,3},{8,12},{9,13},{10,... | collective-permute-start | bytes 393224 | tf_op jit(solution)/shard_map/ppermute | solution.py:21
  21.4 1.5 %collective-permute-start.9 = (bf16[64,1024]{1,0:T(8,128)(2,1)S(1)}, bf16[64,1024]{1,0:T(8,128)(2,1)S(1)}, u32[]{:S(2)}, u32[]{:S(2)}) collective-permute-start(bf16[64,1024]{1,0:T(8,128)(2,1)S(1)} %shard_map.58.refs_0_), channel_id=1, source_target_pairs={{0,24},{8,16},{16,8},{24,0},{1,25},{9,17},{17,9},{25,1},{2,26},{10... | collective-permute-start | bytes 393224 | tf_op jit(solution)/shard_map/ppermute | solution.py:21
  22.9 1.2 %collective-permute-start.8 = (bf16[64,1024]{1,0:T(8,128)(2,1)S(1)}, bf16[64,1024]{1,0:T(8,128)(2,1)S(1)}, u32[]{:S(2)}, u32[]{:S(2)}) collective-permute-start(bf16[64,1024]{1,0:T(8,128)(2,1)S(1)} %shard_map.58.refs_0_), channel_id=1, source_target_pairs={{0,16},{8,24},{16,0},{24,8},{1,17},{9,25},{17,1},{25,9},{2,18},{10... | collective-permute-start | bytes 393224 | tf_op jit(solution)/shard_map/ppermute | solution.py:21
  24.1 0.8 %collective-permute-start.7 = (bf16[64,1024]{1,0:T(8,128)(2,1)S(1)}, bf16[64,1024]{1,0:T(8,128)(2,1)S(1)}, u32[]{:S(2)}, u32[]{:S(2)}) collective-permute-start(bf16[64,1024]{1,0:T(8,128)(2,1)S(1)} %shard_map.58.refs_0_), channel_id=1, source_target_pairs={{0,8},{8,0},{16,24},{24,16},{1,9},{9,1},{17,25},{25,17},{2,10},{10... | collective-permute-start | bytes 393224 | tf_op jit(solution)/shard_map/ppermute | solution.py:21
  24.9 2.5 %collective-permute-done.6.got = bf16[64,1024]{1,0:T(8,128)(2,1)S(1)} collective-permute-done((bf16[64,1024]{1,0:T(8,128)(2,1)S(1)}, bf16[64,1024]{1,0:T(8,128)(2,1)S(1)}, u32[]{:S(2)}, u32[]{:S(2)}) %collective-permute-start.6) | collective-permute-done | bytes 131104 | tf_op jit(solution)/shard_map/ppermute | solution.py:21
  27.4 0.1 shard_map.59
  27.5 0.7 %collective-permute-start.12 = (bf16[64,1024]{1,0:T(8,128)(2,1)S(1)}, bf16[64,1024]{1,0:T(8,128)(2,1)S(1)}, u32[]{:S(2)}, u32[]{:S(2)}) collective-permute-start(bf16[64,1024]{1,0:T(8,128)(2,1)S(1)} %get-tuple-element.58.user), channel_id=1, source_target_pairs={{0,2},{1,3},{2,0},{3,1},{4,6},{5,7},{6,4},{7,5},{8,10},{9,11},{10,... | collective-permute-start | bytes 393224 | tf_op jit(solution)/shard_map/ppermute | solution.py:21
  28.2 0.2 collective-permute-done.9.refs_3_
  28.4 1.3 %collective-permute-done.8.refs_2_ = bf16[64,1024]{1,0:T(8,128)(2,1)S(1)} collective-permute-done((bf16[64,1024]{1,0:T(8,128)(2,1)S(1)}, bf16[64,1024]{1,0:T(8,128)(2,1)S(1)}, u32[]{:S(2)}, u32[]{:S(2)}) %collective-permute-start.8) | collective-permute-done | bytes 131104 | tf_op jit(solution)/shard_map/ppermute | solution.py:21
  29.7 0.2 shard_map.60
  29.9 1.8 %shard_map.61 = (f32[64,1024]{1,0:T(8,128)S(1)}, f32[64,1024]{1,0:T(8,128)S(1)}) custom-call(bf16[64,1024]{1,0:T(8,128)(2,1)S(1)} %get-tuple-element.58.user, bf16[1024,4096]{1,0:T(8,128)(2,1)S(1)} %copy-done, bf16[64,1024]{1,0:T(8,128)(2,1)S(1)} %get-tuple-element.61.item, bf16[1024,64]{1,0:T(8,128)(2,1)S(1)} %get-tuple-element.62.item_t), custom_call_target="tpu_custom_call" | custom-call | flops 3000000000 | bytes 1048576 | tf_op jit(solution)/shard_map/pallas_call | solution.py:35
  31.6 1.7 %shard_map.62 = (f32[64,1024]{1,0:T(8,128)S(1)}, f32[64,1024]{1,0:T(8,128)S(1)}) custom-call(bf16[64,1024]{1,0:T(8,128)(2,1)S(1)} %collective-permute-done.10.user, bf16[1024,4096]{1,0:T(8,128)(2,1)S(1)} %copy-done, bf16[64,1024]{1,0:T(8,128)(2,1)S(1)} %get-tuple-element.61.item, bf16[1024,64]{1,0:T(8,128)(2,1)S(1)} %get-tuple-element.62.item_t, ...), custom_call_target="tpu_custom_call" | custom-call | flops 3000000000 | bytes 1048576 | tf_op jit(solution)/shard_map/pallas_call | solution.py:35
  33.4 0.1 collective-permute-start.13
  33.5 1.8 %shard_map.63 = (f32[64,1024]{1,0:T(8,128)S(1)}, f32[64,1024]{1,0:T(8,128)S(1)}) custom-call(bf16[64,1024]{1,0:T(8,128)(2,1)S(1)} %collective-permute-done.12.user, bf16[1024,4096]{1,0:T(8,128)(2,1)S(1)} %copy-done, bf16[64,1024]{1,0:T(8,128)(2,1)S(1)} %get-tuple-element.61.item, bf16[1024,64]{1,0:T(8,128)(2,1)S(1)} %get-tuple-element.62.item_t, ...), custom_call_target="tpu_custom_call" | custom-call | flops 3000000000 | bytes 1048576 | tf_op jit(solution)/shard_map/pallas_call | solution.py:35
  35.2 1.7 %shard_map.64 = (f32[64,1024]{1,0:T(8,128)S(1)}, f32[64,1024]{1,0:T(8,128)S(1)}) custom-call(bf16[64,1024]{1,0:T(8,128)(2,1)S(1)} %collective-permute-done.13.user, bf16[1024,4096]{1,0:T(8,128)(2,1)S(1)} %copy-done, bf16[64,1024]{1,0:T(8,128)(2,1)S(1)} %get-tuple-element.61.item, bf16[1024,64]{1,0:T(8,128)(2,1)S(1)} %get-tuple-element.62.item_t, ...), custom_call_target="tpu_custom_call" | custom-call | flops 3000000000 | bytes 1048576 | tf_op jit(solution)/shard_map/pallas_call | solution.py:35
  37.0 0.6 collective-permute-start.14
  37.5 0.1 collective-permute-start.11
  37.6 1.1 %collective-permute-done.14.refs_1_ = f32[64,1024]{1,0:T(8,128)S(1)} collective-permute-done((f32[64,1024]{1,0:T(8,128)S(1)}, f32[64,1024]{1,0:T(8,128)S(1)}, u32[]{:S(2)}, u32[]{:S(2)}) %collective-permute-start.14) | collective-permute-done | bytes 262176 | tf_op jit(solution)/shard_map/ppermute | solution.py:21
  38.7 1.7 %collective-permute-start.15 = (bf16[64,1024]{1,0:T(8,128)(2,1)S(1)}, bf16[64,1024]{1,0:T(8,128)(2,1)S(1)}, u32[]{:S(2)}, u32[]{:S(2)}) collective-permute-start(bf16[64,1024]{1,0:T(8,128)(2,1)S(1)} %shard_map.65), channel_id=1, source_target_pairs={{0,2},{1,3},{2,0},{3,1},{4,6},{5,7},{6,4},{7,5},{8,10},{9,11},{10,... | collective-permute-start | bytes 393224 | tf_op jit(solution)/shard_map/ppermute | solution.py:21
  40.4 4.1 %collective-permute-done.15.refs_2_ = bf16[64,1024]{1,0:T(8,128)(2,1)S(1)} collective-permute-done((bf16[64,1024]{1,0:T(8,128)(2,1)S(1)}, bf16[64,1024]{1,0:T(8,128)(2,1)S(1)}, u32[]{:S(2)}, u32[]{:S(2)}) %collective-permute-start.15) | collective-permute-done | bytes 131104 | tf_op jit(solution)/shard_map/ppermute | solution.py:21
  44.6 2.1 %collective-permute-start.16 = (bf16[64,1024]{1,0:T(8,128)(2,1)S(1)}, bf16[64,1024]{1,0:T(8,128)(2,1)S(1)}, u32[]{:S(2)}, u32[]{:S(2)}) collective-permute-start(bf16[64,1024]{1,0:T(8,128)(2,1)S(1)} %shard_map.66.mine), channel_id=1, source_target_pairs={{0,4},{1,5},{2,6},{3,7},{4,0},{5,1},{6,2},{7,3},{8,12},{9,13},{10,... | collective-permute-start | bytes 393224 | tf_op jit(solution)/shard_map/ppermute | solution.py:21
  46.7 1.2 %collective-permute-start.17 = (bf16[64,256]{1,0:T(8,128)(2,1)S(1)}, bf16[64,256]{1,0:T(8,128)(2,1)S(1)}, u32[]{:S(2)}, u32[]{:S(2)}) collective-permute-start(bf16[64,256]{1,0:T(8,128)(2,1)S(1)} %get-tuple-element.80), channel_id=1, source_target_pairs={{0,8},{8,0},{16,24},{24,16},{1,9},{9,1},{17,25},{25,17},{2,10},{10... | collective-permute-start | bytes 98312 | tf_op jit(solution)/shard_map/ppermute | solution.py:21
  47.9 0.8 %collective-permute-start.18 = (bf16[64,256]{1,0:T(8,128)(2,1)S(1)}, bf16[64,256]{1,0:T(8,128)(2,1)S(1)}, u32[]{:S(2)}, u32[]{:S(2)}) collective-permute-start(bf16[64,256]{1,0:T(8,128)(2,1)S(1)} %get-tuple-element.81), channel_id=1, source_target_pairs={{0,16},{8,24},{16,0},{24,8},{1,17},{9,25},{17,1},{25,9},{2,18},{10... | collective-permute-start | bytes 98312 | tf_op jit(solution)/shard_map/ppermute | solution.py:21
  48.7 1.5 %collective-permute-start.19 = (bf16[64,256]{1,0:T(8,128)(2,1)S(1)}, bf16[64,256]{1,0:T(8,128)(2,1)S(1)}, u32[]{:S(2)}, u32[]{:S(2)}) collective-permute-start(bf16[64,256]{1,0:T(8,128)(2,1)S(1)} %get-tuple-element.82), channel_id=1, source_target_pairs={{0,24},{8,16},{16,8},{24,0},{1,25},{9,17},{17,9},{25,1},{2,26},{10... | collective-permute-start | bytes 98312 | tf_op jit(solution)/shard_map/ppermute | solution.py:21
  50.2 0.6 collective-permute-done.17.refs_0_
  50.8 1.1 %collective-permute-done.18.refs_1_ = bf16[64,256]{1,0:T(8,128)(2,1)S(1)} collective-permute-done((bf16[64,256]{1,0:T(8,128)(2,1)S(1)}, bf16[64,256]{1,0:T(8,128)(2,1)S(1)}, u32[]{:S(2)}, u32[]{:S(2)}) %collective-permute-start.18) | collective-permute-done | bytes 32800 | tf_op jit(solution)/shard_map/ppermute | solution.py:21
  51.8 1.7 %collective-permute-done.19.refs_2_ = bf16[64,256]{1,0:T(8,128)(2,1)S(1)} collective-permute-done((bf16[64,256]{1,0:T(8,128)(2,1)S(1)}, bf16[64,256]{1,0:T(8,128)(2,1)S(1)}, u32[]{:S(2)}, u32[]{:S(2)}) %collective-permute-start.19) | collective-permute-done | bytes 32800 | tf_op jit(solution)/shard_map/ppermute | solution.py:21
  53.5 0.7 %shard_map.68 = f32[64,256]{1,0:T(8,128)} custom-call(f32[64,256]{1,0:T(8,128)S(1)} %get-tuple-element.78.item, f32[64,256]{1,0:T(8,128)S(1)} %get-tuple-element.79.own, bf16[64,256]{1,0:T(8,128)(2,1)S(1)} %collective-permute-done.17.refs_0_, bf16[64,256]{1,0:T(8,128)(2,1)S(1)} %collective-permute-done.18.refs_1_, ...), custom_call_target="tpu_custom_call" | custom-call | bytes 1048576 | tf_op jit(solution)/shard_map/pallas_call | solution.py:35
  54.2 0.1 shard_map.69.refs_0_
  54.3 1.6 %collective-permute-start.21 = (bf16[64,1024]{1,0:T(8,128)(2,1)S(1)}, bf16[64,1024]{1,0:T(8,128)(2,1)S(1)}, u32[]{:S(2)}, u32[]{:S(2)}) collective-permute-start(bf16[64,1024]{1,0:T(8,128)(2,1)S(1)} %shard_map.69.refs_0_), channel_id=1, source_target_pairs={{0,2},{1,3},{2,0},{3,1},{4,6},{5,7},{6,4},{7,5},{8,10},{9,11},{10,... | collective-permute-start | bytes 393224 | tf_op jit(solution)/shard_map/ppermute | solution.py:21
  55.8 3.5 %collective-permute-done.21.refs_2_ = bf16[64,1024]{1,0:T(8,128)(2,1)S(1)} collective-permute-done((bf16[64,1024]{1,0:T(8,128)(2,1)S(1)}, bf16[64,1024]{1,0:T(8,128)(2,1)S(1)}, u32[]{:S(2)}, u32[]{:S(2)}) %collective-permute-start.21) | collective-permute-done | bytes 131104 | tf_op jit(solution)/shard_map/ppermute | solution.py:21
  59.3 1.3 %collective-permute-done.22.refs_3_ = bf16[64,1024]{1,0:T(8,128)(2,1)S(1)} collective-permute-done((bf16[64,1024]{1,0:T(8,128)(2,1)S(1)}, bf16[64,1024]{1,0:T(8,128)(2,1)S(1)}, u32[]{:S(2)}, u32[]{:S(2)}) %collective-permute-start.22) | collective-permute-done | bytes 131104 | tf_op jit(solution)/shard_map/ppermute | solution.py:21
  60.6 1.1 %shard_map.70 = f32[64,4096]{1,0:T(8,128)} custom-call(f32[64,4096]{1,0:T(8,128)S(1)} %copy-done.1, bf16[64,1024]{1,0:T(8,128)(2,1)S(1)} %shard_map.69.refs_0_, bf16[64,1024]{1,0:T(8,128)(2,1)S(1)} %collective-permute-done.20.refs_1_, bf16[64,1024]{1,0:T(8,128)(2,1)S(1)} %collective-permute-done.21.refs_2_, bf16[64,1024]{1,0:T(8,128)(2,1)S(1)} %collective-permute-done.22.refs_3_), custom_call_target="tpu_custom_call" | custom-call | bytes 1048576 | tf_op jit(solution)/shard_map/pallas_call | solution.py:35
  (25 shorter events, 0.3 us)
Async XLA Ops:
  0.6 5.5 %copy-start = (bf16[1024,4096]{1,0:T(8,128)(2,1)S(1)}, bf16[1024,4096]{1,0:T(8,128)(2,1)}, u32[]{:S(2)}) copy-start(bf16[1024,4096]{1,0:T(8,128)(2,1)} %labels.15) | copy-start | bytes 25165828
  0.6 5.5 %copy-start.1 = (f32[64,4096]{1,0:T(8,128)S(1)}, f32[64,4096]{1,0:T(8,128)}, u32[]{:S(2)}) copy-start(f32[64,4096]{1,0:T(8,128)} %users.13) | copy-start | bytes 3145732
  0.6 7.5 %collective-permute-start = (f32[64,256]{1,0:T(8,128)}, f32[64,256]{1,0:T(8,128)S(1)}, u32[]{:S(2)}, u32[]{:S(2)}) collective-permute-start(f32[64,256]{1,0:T(8,128)} %items.1), channel_id=1, source_target_pairs={{0,8},{8,0},{16,24},{24,16},{1,9},{9,1},{17,25},{25,17},{2,10},{10... | collective-permute-start | bytes 196616 | tf_op jit(solution)/shard_map/ppermute | solution.py:21
  3.7 5.4 %collective-permute-start.2 = (f32[64,256]{1,0:T(8,128)}, f32[64,256]{1,0:T(8,128)S(1)}, u32[]{:S(2)}, u32[]{:S(2)}) collective-permute-start(f32[64,256]{1,0:T(8,128)} %items.1), channel_id=1, source_target_pairs={{0,24},{8,16},{16,8},{24,0},{1,25},{9,17},{17,9},{25,1},{2,26},{10... | collective-permute-start | bytes 196616 | tf_op jit(solution)/shard_map/ppermute | solution.py:21
  5.1 4.7 %collective-permute-start.1 = (f32[64,256]{1,0:T(8,128)}, f32[64,256]{1,0:T(8,128)S(1)}, u32[]{:S(2)}, u32[]{:S(2)}) collective-permute-start(f32[64,256]{1,0:T(8,128)} %items.1), channel_id=1, source_target_pairs={{0,16},{8,24},{16,0},{24,8},{1,17},{9,25},{17,1},{25,9},{2,18},{10... | collective-permute-start | bytes 196616 | tf_op jit(solution)/shard_map/ppermute | solution.py:21
  5.2 0.9 %copy-start.2 = (f32[64,256]{1,0:T(8,128)S(1)}, f32[64,256]{1,0:T(8,128)}, u32[]{:S(2)}) copy-start(f32[64,256]{1,0:T(8,128)} %items.1) | copy-start | bytes 196612
  11.3 1.6 %collective-permute-start.3 = (f32[64,1024]{1,0:T(8,128)S(1)}, f32[64,1024]{1,0:T(8,128)S(1)}, u32[]{:S(2)}, u32[]{:S(2)}) collective-permute-start(f32[64,1024]{1,0:T(8,128)S(1)} %get-tuple-element.50), channel_id=1, source_target_pairs={{0,1},{1,0},{2,3},{3,2},{4,5},{5,4},{6,7},{7,6},{8,9},{9,8},{10,11... | collective-permute-start | bytes 786440 | tf_op jit(solution)/shard_map/ppermute | solution.py:21
  12.9 5.8 %collective-permute-start.5 = (bf16[64,1024]{1,0:T(8,128)(2,1)S(1)}, bf16[64,1024]{1,0:T(8,128)(2,1)S(1)}, u32[]{:S(2)}, u32[]{:S(2)}) collective-permute-start(bf16[64,1024]{1,0:T(8,128)(2,1)S(1)} %shard_map.54), channel_id=1, source_target_pairs={{0,2},{1,3},{2,0},{3,1},{4,6},{5,7},{6,4},{7,5},{8,10},{9,11},{10,... | collective-permute-start | bytes 393224 | tf_op jit(solution)/shard_map/ppermute | solution.py:21
  15.9 2.8 %collective-permute-start.4 = (f32[64,1024]{1,0:T(8,128)S(1)}, f32[64,1024]{1,0:T(8,128)S(1)}, u32[]{:S(2)}, u32[]{:S(2)}) collective-permute-start(f32[64,1024]{1,0:T(8,128)S(1)} %get-tuple-element.55), channel_id=1, source_target_pairs={{0,1},{1,0},{2,3},{3,2},{4,5},{5,4},{6,7},{7,6},{8,9},{9,8},{10,11... | collective-permute-start | bytes 786440 | tf_op jit(solution)/shard_map/ppermute | solution.py:21
  18.7 8.7 %collective-permute-start.6 = (bf16[64,1024]{1,0:T(8,128)(2,1)S(1)}, bf16[64,1024]{1,0:T(8,128)(2,1)S(1)}, u32[]{:S(2)}, u32[]{:S(2)}) collective-permute-start(bf16[64,1024]{1,0:T(8,128)(2,1)S(1)} %shard_map.57.mine), channel_id=1, source_target_pairs={{0,4},{1,5},{2,6},{3,7},{4,0},{5,1},{6,2},{7,3},{8,12},{9,13},{10,... | collective-permute-start | bytes 393224 | tf_op jit(solution)/shard_map/ppermute | solution.py:21
  21.4 7.0 %collective-permute-start.9 = (bf16[64,1024]{1,0:T(8,128)(2,1)S(1)}, bf16[64,1024]{1,0:T(8,128)(2,1)S(1)}, u32[]{:S(2)}, u32[]{:S(2)}) collective-permute-start(bf16[64,1024]{1,0:T(8,128)(2,1)S(1)} %shard_map.58.refs_0_), channel_id=1, source_target_pairs={{0,24},{8,16},{16,8},{24,0},{1,25},{9,17},{17,9},{25,1},{2,26},{10... | collective-permute-start | bytes 393224 | tf_op jit(solution)/shard_map/ppermute | solution.py:21
  22.9 6.8 %collective-permute-start.8 = (bf16[64,1024]{1,0:T(8,128)(2,1)S(1)}, bf16[64,1024]{1,0:T(8,128)(2,1)S(1)}, u32[]{:S(2)}, u32[]{:S(2)}) collective-permute-start(bf16[64,1024]{1,0:T(8,128)(2,1)S(1)} %shard_map.58.refs_0_), channel_id=1, source_target_pairs={{0,16},{8,24},{16,0},{24,8},{1,17},{9,25},{17,1},{25,9},{2,18},{10... | collective-permute-start | bytes 393224 | tf_op jit(solution)/shard_map/ppermute | solution.py:21
  24.1 5.6 %collective-permute-start.7 = (bf16[64,1024]{1,0:T(8,128)(2,1)S(1)}, bf16[64,1024]{1,0:T(8,128)(2,1)S(1)}, u32[]{:S(2)}, u32[]{:S(2)}) collective-permute-start(bf16[64,1024]{1,0:T(8,128)(2,1)S(1)} %shard_map.58.refs_0_), channel_id=1, source_target_pairs={{0,8},{8,0},{16,24},{24,16},{1,9},{9,1},{17,25},{25,17},{2,10},{10... | collective-permute-start | bytes 393224 | tf_op jit(solution)/shard_map/ppermute | solution.py:21
  27.5 5.9 %collective-permute-start.12 = (bf16[64,1024]{1,0:T(8,128)(2,1)S(1)}, bf16[64,1024]{1,0:T(8,128)(2,1)S(1)}, u32[]{:S(2)}, u32[]{:S(2)}) collective-permute-start(bf16[64,1024]{1,0:T(8,128)(2,1)S(1)} %get-tuple-element.58.user), channel_id=1, source_target_pairs={{0,2},{1,3},{2,0},{3,1},{4,6},{5,7},{6,4},{7,5},{8,10},{9,11},{10,... | collective-permute-start | bytes 393224 | tf_op jit(solution)/shard_map/ppermute | solution.py:21
  28.2 3.4 %collective-permute-start.10 = (bf16[64,1024]{1,0:T(8,128)(2,1)S(1)}, bf16[64,1024]{1,0:T(8,128)(2,1)S(1)}, u32[]{:S(2)}, u32[]{:S(2)}) collective-permute-start(bf16[64,1024]{1,0:T(8,128)(2,1)S(1)} %get-tuple-element.58.user), channel_id=1, source_target_pairs={{0,1},{1,0},{2,3},{3,2},{4,5},{5,4},{6,7},{7,6},{8,9},{9,8},{10,11... | collective-permute-start | bytes 393224 | tf_op jit(solution)/shard_map/ppermute | solution.py:21
  33.4 1.8 %collective-permute-start.13 = (bf16[64,1024]{1,0:T(8,128)(2,1)S(1)}, bf16[64,1024]{1,0:T(8,128)(2,1)S(1)}, u32[]{:S(2)}, u32[]{:S(2)}) collective-permute-start(bf16[64,1024]{1,0:T(8,128)(2,1)S(1)} %collective-permute-done.12.user), channel_id=1, source_target_pairs={{0,1},{1,0},{2,3},{3,2},{4,5},{5,4},{6,7},{7,6},{8,9},{9,8},{10,11... | collective-permute-start | bytes 393224 | tf_op jit(solution)/shard_map/ppermute | solution.py:21
  37.0 1.7 %collective-permute-start.14 = (f32[64,1024]{1,0:T(8,128)S(1)}, f32[64,1024]{1,0:T(8,128)S(1)}, u32[]{:S(2)}, u32[]{:S(2)}) collective-permute-start(f32[64,1024]{1,0:T(8,128)S(1)} %get-tuple-element.71), channel_id=1, source_target_pairs={{0,1},{1,0},{2,3},{3,2},{4,5},{5,4},{6,7},{7,6},{8,9},{9,8},{10,11... | collective-permute-start | bytes 786440 | tf_op jit(solution)/shard_map/ppermute | solution.py:21
  37.5 2.9 %collective-permute-start.11 = (f32[64,1024]{1,0:T(8,128)S(1)}, f32[64,1024]{1,0:T(8,128)S(1)}, u32[]{:S(2)}, u32[]{:S(2)}) collective-permute-start(f32[64,1024]{1,0:T(8,128)S(1)} %get-tuple-element.65), channel_id=1, source_target_pairs={{0,1},{1,0},{2,3},{3,2},{4,5},{5,4},{6,7},{7,6},{8,9},{9,8},{10,11... | collective-permute-start | bytes 786440 | tf_op jit(solution)/shard_map/ppermute | solution.py:21
  38.7 5.8 %collective-permute-start.15 = (bf16[64,1024]{1,0:T(8,128)(2,1)S(1)}, bf16[64,1024]{1,0:T(8,128)(2,1)S(1)}, u32[]{:S(2)}, u32[]{:S(2)}) collective-permute-start(bf16[64,1024]{1,0:T(8,128)(2,1)S(1)} %shard_map.65), channel_id=1, source_target_pairs={{0,2},{1,3},{2,0},{3,1},{4,6},{5,7},{6,4},{7,5},{8,10},{9,11},{10,... | collective-permute-start | bytes 393224 | tf_op jit(solution)/shard_map/ppermute | solution.py:21
  44.6 9.6 %collective-permute-start.16 = (bf16[64,1024]{1,0:T(8,128)(2,1)S(1)}, bf16[64,1024]{1,0:T(8,128)(2,1)S(1)}, u32[]{:S(2)}, u32[]{:S(2)}) collective-permute-start(bf16[64,1024]{1,0:T(8,128)(2,1)S(1)} %shard_map.66.mine), channel_id=1, source_target_pairs={{0,4},{1,5},{2,6},{3,7},{4,0},{5,1},{6,2},{7,3},{8,12},{9,13},{10,... | collective-permute-start | bytes 393224 | tf_op jit(solution)/shard_map/ppermute | solution.py:21
  46.7 4.1 %collective-permute-start.17 = (bf16[64,256]{1,0:T(8,128)(2,1)S(1)}, bf16[64,256]{1,0:T(8,128)(2,1)S(1)}, u32[]{:S(2)}, u32[]{:S(2)}) collective-permute-start(bf16[64,256]{1,0:T(8,128)(2,1)S(1)} %get-tuple-element.80), channel_id=1, source_target_pairs={{0,8},{8,0},{16,24},{24,16},{1,9},{9,1},{17,25},{25,17},{2,10},{10... | collective-permute-start | bytes 98312 | tf_op jit(solution)/shard_map/ppermute | solution.py:21
  47.9 3.9 %collective-permute-start.18 = (bf16[64,256]{1,0:T(8,128)(2,1)S(1)}, bf16[64,256]{1,0:T(8,128)(2,1)S(1)}, u32[]{:S(2)}, u32[]{:S(2)}) collective-permute-start(bf16[64,256]{1,0:T(8,128)(2,1)S(1)} %get-tuple-element.81), channel_id=1, source_target_pairs={{0,16},{8,24},{16,0},{24,8},{1,17},{9,25},{17,1},{25,9},{2,18},{10... | collective-permute-start | bytes 98312 | tf_op jit(solution)/shard_map/ppermute | solution.py:21
  48.7 4.8 %collective-permute-start.19 = (bf16[64,256]{1,0:T(8,128)(2,1)S(1)}, bf16[64,256]{1,0:T(8,128)(2,1)S(1)}, u32[]{:S(2)}, u32[]{:S(2)}) collective-permute-start(bf16[64,256]{1,0:T(8,128)(2,1)S(1)} %get-tuple-element.82), channel_id=1, source_target_pairs={{0,24},{8,16},{16,8},{24,0},{1,25},{9,17},{17,9},{25,1},{2,26},{10... | collective-permute-start | bytes 98312 | tf_op jit(solution)/shard_map/ppermute | solution.py:21
  54.3 5.0 %collective-permute-start.21 = (bf16[64,1024]{1,0:T(8,128)(2,1)S(1)}, bf16[64,1024]{1,0:T(8,128)(2,1)S(1)}, u32[]{:S(2)}, u32[]{:S(2)}) collective-permute-start(bf16[64,1024]{1,0:T(8,128)(2,1)S(1)} %shard_map.69.refs_0_), channel_id=1, source_target_pairs={{0,2},{1,3},{2,0},{3,1},{4,6},{5,7},{6,4},{7,5},{8,10},{9,11},{10,... | collective-permute-start | bytes 393224 | tf_op jit(solution)/shard_map/ppermute | solution.py:21
  55.8 3.5 %collective-permute-start.20 = (bf16[64,1024]{1,0:T(8,128)(2,1)S(1)}, bf16[64,1024]{1,0:T(8,128)(2,1)S(1)}, u32[]{:S(2)}, u32[]{:S(2)}) collective-permute-start(bf16[64,1024]{1,0:T(8,128)(2,1)S(1)} %shard_map.69.refs_0_), channel_id=1, source_target_pairs={{0,1},{1,0},{2,3},{3,2},{4,5},{5,4},{6,7},{7,6},{8,9},{9,8},{10,11... | collective-permute-start | bytes 393224 | tf_op jit(solution)/shard_map/ppermute | solution.py:21
  59.3 1.3 %collective-permute-start.22 = (bf16[64,1024]{1,0:T(8,128)(2,1)S(1)}, bf16[64,1024]{1,0:T(8,128)(2,1)S(1)}, u32[]{:S(2)}, u32[]{:S(2)}) collective-permute-start(bf16[64,1024]{1,0:T(8,128)(2,1)S(1)} %collective-permute-done.21.refs_2_), channel_id=1, source_target_pairs={{0,1},{1,0},{2,3},{3,2},{4,5},{5,4},{6,7},{7,6},{8,9},{9,8},{10,11... | collective-permute-start | bytes 393224 | tf_op jit(solution)/shard_map/ppermute | solution.py:21

commit v6 on v5

--- a/solution.py
+++ b/solution.py
@@ -11,7 +11,7 @@
 CORES = 2
 GROUPS = ((True, True), (False, True), (True, False), (False, False))
 TILE_USERS = 1024
-TILE_ITEMS = 512
+TILE_ITEMS = 1024
 
 f32, bf16 = jnp.float32, jnp.bfloat16
 VMEM, HBM = pltpu.VMEM, pltpu.HBM
@@ -331,15 +331,15 @@
     item_pieces = call(cut_items, [(items.shape, f32)] + [(items.shape, bf16)] * len(others), grad)
     mine, got, item_pieces = meet(mine, recv, near, behind=item_pieces)
     item_got = [swap(p, "row", o) for p, o in zip(item_pieces[1:], others)]
+    got, *item_got = lax.optimization_barrier((got, *item_got))
     (new_items,) = call(
         functools.partial(finish_items, item_rate), [(items.shape, f32)], item_own, item_pieces[0], *item_got
     )
-    got, new_items = lax.optimization_barrier((got, new_items))
     (delta,) = call(
         functools.partial(update_last, user_rate, half), [(mine.shape, bf16)], mine, got, users_v, new
     )
     own_keep = widen(delta)
-    own_send = along_z(own_keep, 0)
+    own_send, new_items = lax.optimization_barrier((along_z(own_keep, 0), new_items))
     pieces = own_keep, swap(own_keep, "col", 1), own_send, swap(own_send, "col", 1)
     (new_users,) = call(functools.partial(finish_users, half), [(users.shape, f32)], users_v, *pieces)
     return new_users, new_items

time: 61.9 us -> 61.3 us (level)
    ppermute x23, waiting for transfers between devices: 20.7 us -> 20.1 us  [swap(): lax.ppermute(block, axis, [(i, i ^ distance) for i in range(lax.axis_size...]
where the time goes in v6:
time: 61.3 us; the launch traced here: 61.1 us
  starting transfers between devices  22.7 us (37%)
  waiting for transfers between devices  20.1 us (33%)
  Pallas kernels  16.6 us (27%)
  local copies, waits for them, and re-layouts  0.91 us (1%)
  between operations  0.83 us (1%)
    ppermute x23, starting transfers between devices, swap(): lax.ppermute(block, axis, [(i, i ^ distance) for i in range(lax.axis_size...  22.7 us
    ppermute x23, waiting for transfers between devices, swap(): lax.ppermute(block, axis, [(i, i ^ distance) for i in range(lax.axis_size...  20.1 us
    pallas_call x21, Pallas kernels, call(): pl.pallas_call(kernel, in_specs=[pl.BlockSpec(memory_space=space)] * len(...  16.6 us
  transfers between devices with their start and end apart: 23, of which 14 were waited for; matrix products, arithmetic and copies ran while one was open for 0% of the time, Pallas kernels for 20%

profile of v6, /device:TPU:0, one launch (start us, length us, event | category | flops | bytes accessed | tf_op | source)
XLA Modules:
  0.0 61.1 jit_solution(7579774361855409776)
XLA Ops:
  0.6 3.0 %collective-permute-start = (f32[64,256]{1,0:T(8,128)}, f32[64,256]{1,0:T(8,128)S(1)}, u32[]{:S(2)}, u32[]{:S(2)}) collective-permute-start(f32[64,256]{1,0:T(8,128)} %items.1), channel_id=1, source_target_pairs={{0,8},{8,0},{16,24},{24,16},{1,9},{9,1},{17,25},{25,17},{2,10},{10... | collective-permute-start | bytes 196616 | tf_op jit(solution)/shard_map/ppermute | solution.py:21
  3.7 1.5 %collective-permute-start.2 = (f32[64,256]{1,0:T(8,128)}, f32[64,256]{1,0:T(8,128)S(1)}, u32[]{:S(2)}, u32[]{:S(2)}) collective-permute-start(f32[64,256]{1,0:T(8,128)} %items.1), channel_id=1, source_target_pairs={{0,24},{8,16},{16,8},{24,0},{1,25},{9,17},{17,9},{25,1},{2,26},{10... | collective-permute-start | bytes 196616 | tf_op jit(solution)/shard_map/ppermute | solution.py:21
  5.2 0.9 %copy-done.2 = f32[64,256]{1,0:T(8,128)S(1)} copy-done((f32[64,256]{1,0:T(8,128)S(1)}, f32[64,256]{1,0:T(8,128)}, u32[]{:S(2)}) %copy-start.2) | copy-done | bytes 65560
  6.1 2.0 %shard_map.51 = (f32[64,4096]{1,0:T(8,128)S(1)}, f32[64,1024]{1,0:T(8,128)S(1)}) custom-call(bf16[1024,4096]{1,0:T(8,128)(2,1)S(1)} %copy-done, f32[64,4096]{1,0:T(8,128)S(1)} %copy-done.1, f32[64,256]{1,0:T(8,128)S(1)} %shard_map.50.items.refs_0_), custom_call_target="tpu_custom_call" | custom-call | flops 3000000000 | bytes 1048576 | tf_op jit(solution)/shard_map/pallas_call | solution.py:35
  8.2 0.9 %collective-permute-done.2.refs_3_ = f32[64,256]{1,0:T(8,128)S(1)} collective-permute-done((f32[64,256]{1,0:T(8,128)}, f32[64,256]{1,0:T(8,128)S(1)}, u32[]{:S(2)}, u32[]{:S(2)}) %collective-permute-start.2) | collective-permute-done | bytes 65568 | tf_op jit(solution)/shard_map/ppermute | solution.py:21
  9.1 0.8 %collective-permute-done.1.refs_2_ = f32[64,256]{1,0:T(8,128)S(1)} collective-permute-done((f32[64,256]{1,0:T(8,128)}, f32[64,256]{1,0:T(8,128)S(1)}, u32[]{:S(2)}, u32[]{:S(2)}) %collective-permute-start.1) | collective-permute-done | bytes 65568 | tf_op jit(solution)/shard_map/ppermute | solution.py:21
  9.9 1.4 %shard_map.52 = (f32[64,1024]{1,0:T(8,128)S(1)}, f32[64,1024]{1,0:T(8,128)S(1)}, f32[64,1024]{1,0:T(8,128)S(1)}, bf16[64,1024]{1,0:T(8,128)(2,1)S(1)}, bf16[1024,64]{1,0:T(8,128)(2,1)S(1)}) custom-call(f32[64,256]{1,0:T(8,128)S(1)} %shard_map.50.items.refs_0_, f32[64,256]{1,0:T(8,128)S(1)} %collective-permute-done.refs_1_, ...), custom_call_target="tpu_custom_call" | custom-call | flops 3000000000 | bytes 1048576 | tf_op jit(solution)/shard_map/pallas_call | solution.py:35
  11.3 0.1 collective-permute-start.3
  11.4 1.3 %shard_map.53 = (f32[64,1024]{1,0:T(8,128)S(1)}, f32[64,1024]{1,0:T(8,128)S(1)}) custom-call(f32[64,4096]{1,0:T(8,128)S(1)} %copy-done.1, bf16[1024,4096]{1,0:T(8,128)(2,1)S(1)} %copy-done, f32[64,4096]{1,0:T(8,128)S(1)} %get-tuple-element.48.refs_6_.grad_user, bf16[64,1024]{1,0:T(8,128)(2,1)S(1)} %get-tuple-element.50.item, ...), custom_call_target="tpu_custom_call" | custom-call | flops 3000000000 | bytes 1048576 | tf_op jit(solution)/shard_map/pallas_call | solution.py:35
  12.7 0.2 collective-permute-done.3.refs_1_
  12.9 1.6 %collective-permute-start.5 = (bf16[64,1024]{1,0:T(8,128)(2,1)S(1)}, bf16[64,1024]{1,0:T(8,128)(2,1)S(1)}, u32[]{:S(2)}, u32[]{:S(2)}) collective-permute-start(bf16[64,1024]{1,0:T(8,128)(2,1)S(1)} %shard_map.54), channel_id=1, source_target_pairs={{0,2},{1,3},{2,0},{3,1},{4,6},{5,7},{6,4},{7,5},{8,10},{9,11},{10,... | collective-permute-start | bytes 393224 | tf_op jit(solution)/shard_map/ppermute | solution.py:21
  14.6 1.3 %shard_map.55 = (f32[64,1024]{1,0:T(8,128)S(1)}, f32[64,1024]{1,0:T(8,128)S(1)}) custom-call(f32[64,4096]{1,0:T(8,128)S(1)} %copy-done.1, bf16[1024,4096]{1,0:T(8,128)(2,1)S(1)} %copy-done, f32[64,4096]{1,0:T(8,128)S(1)} %get-tuple-element.48.refs_6_.grad_user, bf16[64,1024]{1,0:T(8,128)(2,1)S(1)} %get-tuple-element.50.item, ...), custom_call_target="tpu_custom_call" | custom-call | flops 3000000000 | bytes 1048576 | tf_op jit(solution)/shard_map/pallas_call | solution.py:35
  15.9 0.1 collective-permute-start.4
  16.0 1.3 %shard_map.56 = (f32[64,1024]{1,0:T(8,128)S(1)}, f32[64,1024]{1,0:T(8,128)S(1)}) custom-call(f32[64,4096]{1,0:T(8,128)S(1)} %copy-done.1, bf16[1024,4096]{1,0:T(8,128)(2,1)S(1)} %copy-done, f32[64,4096]{1,0:T(8,128)S(1)} %get-tuple-element.48.refs_6_.grad_user, bf16[64,1024]{1,0:T(8,128)(2,1)S(1)} %get-tuple-element.50.item, ...), custom_call_target="tpu_custom_call" | custom-call | flops 3000000000 | bytes 1048576 | tf_op jit(solution)/shard_map/pallas_call | solution.py:35
  17.3 1.4 %collective-permute-done.5.refs_2_ = bf16[64,1024]{1,0:T(8,128)(2,1)S(1)} collective-permute-done((bf16[64,1024]{1,0:T(8,128)(2,1)S(1)}, bf16[64,1024]{1,0:T(8,128)(2,1)S(1)}, u32[]{:S(2)}, u32[]{:S(2)}) %collective-permute-start.5) | collective-permute-done | bytes 131104 | tf_op jit(solution)/shard_map/ppermute | solution.py:21
  18.7 2.6 %collective-permute-start.6 = (bf16[64,1024]{1,0:T(8,128)(2,1)S(1)}, bf16[64,1024]{1,0:T(8,128)(2,1)S(1)}, u32[]{:S(2)}, u32[]{:S(2)}) collective-permute-start(bf16[64,1024]{1,0:T(8,128)(2,1)S(1)} %shard_map.57.mine), channel_id=1, source_target_pairs={{0,4},{1,5},{2,6},{3,7},{4,0},{5,1},{6,2},{7,3},{8,12},{9,13},{10,... | collective-permute-start | bytes 393224 | tf_op jit(solution)/shard_map/ppermute | solution.py:21
  21.4 1.5 %collective-permute-start.9 = (bf16[64,1024]{1,0:T(8,128)(2,1)S(1)}, bf16[64,1024]{1,0:T(8,128)(2,1)S(1)}, u32[]{:S(2)}, u32[]{:S(2)}) collective-permute-start(bf16[64,1024]{1,0:T(8,128)(2,1)S(1)} %shard_map.58.refs_0_), channel_id=1, source_target_pairs={{0,24},{8,16},{16,8},{24,0},{1,25},{9,17},{17,9},{25,1},{2,26},{10... | collective-permute-start | bytes 393224 | tf_op jit(solution)/shard_map/ppermute | solution.py:21
  22.9 1.2 %collective-permute-start.8 = (bf16[64,1024]{1,0:T(8,128)(2,1)S(1)}, bf16[64,1024]{1,0:T(8,128)(2,1)S(1)}, u32[]{:S(2)}, u32[]{:S(2)}) collective-permute-start(bf16[64,1024]{1,0:T(8,128)(2,1)S(1)} %shard_map.58.refs_0_), channel_id=1, source_target_pairs={{0,16},{8,24},{16,0},{24,8},{1,17},{9,25},{17,1},{25,9},{2,18},{10... | collective-permute-start | bytes 393224 | tf_op jit(solution)/shard_map/ppermute | solution.py:21
  24.1 0.8 %collective-permute-start.7 = (bf16[64,1024]{1,0:T(8,128)(2,1)S(1)}, bf16[64,1024]{1,0:T(8,128)(2,1)S(1)}, u32[]{:S(2)}, u32[]{:S(2)}) collective-permute-start(bf16[64,1024]{1,0:T(8,128)(2,1)S(1)} %shard_map.58.refs_0_), channel_id=1, source_target_pairs={{0,8},{8,0},{16,24},{24,16},{1,9},{9,1},{17,25},{25,17},{2,10},{10... | collective-permute-start | bytes 393224 | tf_op jit(solution)/shard_map/ppermute | solution.py:21
  24.9 2.5 %collective-permute-done.6.got = bf16[64,1024]{1,0:T(8,128)(2,1)S(1)} collective-permute-done((bf16[64,1024]{1,0:T(8,128)(2,1)S(1)}, bf16[64,1024]{1,0:T(8,128)(2,1)S(1)}, u32[]{:S(2)}, u32[]{:S(2)}) %collective-permute-start.6) | collective-permute-done | bytes 131104 | tf_op jit(solution)/shard_map/ppermute | solution.py:21
  27.4 0.1 shard_map.59
  27.5 0.7 %collective-permute-start.12 = (bf16[64,1024]{1,0:T(8,128)(2,1)S(1)}, bf16[64,1024]{1,0:T(8,128)(2,1)S(1)}, u32[]{:S(2)}, u32[]{:S(2)}) collective-permute-start(bf16[64,1024]{1,0:T(8,128)(2,1)S(1)} %get-tuple-element.62.user), channel_id=1, source_target_pairs={{0,2},{1,3},{2,0},{3,1},{4,6},{5,7},{6,4},{7,5},{8,10},{9,11},{10,... | collective-permute-start | bytes 393224 | tf_op jit(solution)/shard_map/ppermute | solution.py:21
  28.2 0.2 collective-permute-done.9.refs_3_
  28.4 1.3 %collective-permute-done.8.refs_2_ = bf16[64,1024]{1,0:T(8,128)(2,1)S(1)} collective-permute-done((bf16[64,1024]{1,0:T(8,128)(2,1)S(1)}, bf16[64,1024]{1,0:T(8,128)(2,1)S(1)}, u32[]{:S(2)}, u32[]{:S(2)}) %collective-permute-start.8) | collective-permute-done | bytes 131104 | tf_op jit(solution)/shard_map/ppermute | solution.py:21
  29.7 0.2 shard_map.60
  29.9 1.8 %shard_map.61 = (f32[64,1024]{1,0:T(8,128)S(1)}, f32[64,1024]{1,0:T(8,128)S(1)}) custom-call(bf16[64,1024]{1,0:T(8,128)(2,1)S(1)} %get-tuple-element.62.user, bf16[1024,4096]{1,0:T(8,128)(2,1)S(1)} %copy-done, bf16[64,1024]{1,0:T(8,128)(2,1)S(1)} %get-tuple-element.65.item, bf16[1024,64]{1,0:T(8,128)(2,1)S(1)} %get-tuple-element.66.item_t), custom_call_target="tpu_custom_call" | custom-call | flops 3000000000 | bytes 1048576 | tf_op jit(solution)/shard_map/pallas_call | solution.py:35
  31.6 1.8 %shard_map.62 = (f32[64,1024]{1,0:T(8,128)S(1)}, f32[64,1024]{1,0:T(8,128)S(1)}) custom-call(bf16[64,1024]{1,0:T(8,128)(2,1)S(1)} %collective-permute-done.10.user, bf16[1024,4096]{1,0:T(8,128)(2,1)S(1)} %copy-done, bf16[64,1024]{1,0:T(8,128)(2,1)S(1)} %get-tuple-element.65.item, bf16[1024,64]{1,0:T(8,128)(2,1)S(1)} %get-tuple-element.66.item_t, ...), custom_call_target="tpu_custom_call" | custom-call | flops 3000000000 | bytes 1048576 | tf_op jit(solution)/shard_map/pallas_call | solution.py:35
  33.4 0.1 collective-permute-start.13
  33.5 1.8 %shard_map.63 = (f32[64,1024]{1,0:T(8,128)S(1)}, f32[64,1024]{1,0:T(8,128)S(1)}) custom-call(bf16[64,1024]{1,0:T(8,128)(2,1)S(1)} %collective-permute-done.12.user, bf16[1024,4096]{1,0:T(8,128)(2,1)S(1)} %copy-done, bf16[64,1024]{1,0:T(8,128)(2,1)S(1)} %get-tuple-element.65.item, bf16[1024,64]{1,0:T(8,128)(2,1)S(1)} %get-tuple-element.66.item_t, ...), custom_call_target="tpu_custom_call" | custom-call | flops 3000000000 | bytes 1048576 | tf_op jit(solution)/shard_map/pallas_call | solution.py:35
  35.3 1.8 %shard_map.64 = (f32[64,1024]{1,0:T(8,128)S(1)}, f32[64,1024]{1,0:T(8,128)S(1)}) custom-call(bf16[64,1024]{1,0:T(8,128)(2,1)S(1)} %collective-permute-done.13.user, bf16[1024,4096]{1,0:T(8,128)(2,1)S(1)} %copy-done, bf16[64,1024]{1,0:T(8,128)(2,1)S(1)} %get-tuple-element.65.item, bf16[1024,64]{1,0:T(8,128)(2,1)S(1)} %get-tuple-element.66.item_t, ...), custom_call_target="tpu_custom_call" | custom-call | flops 3000000000 | bytes 1048576 | tf_op jit(solution)/shard_map/pallas_call | solution.py:35
  37.0 0.6 collective-permute-start.14
  37.6 0.1 collective-permute-start.11
  37.7 1.1 %collective-permute-done.14.refs_1_ = f32[64,1024]{1,0:T(8,128)S(1)} collective-permute-done((f32[64,1024]{1,0:T(8,128)S(1)}, f32[64,1024]{1,0:T(8,128)S(1)}, u32[]{:S(2)}, u32[]{:S(2)}) %collective-permute-start.14) | collective-permute-done | bytes 262176 | tf_op jit(solution)/shard_map/ppermute | solution.py:21
  38.8 1.7 %collective-permute-start.15 = (bf16[64,1024]{1,0:T(8,128)(2,1)S(1)}, bf16[64,1024]{1,0:T(8,128)(2,1)S(1)}, u32[]{:S(2)}, u32[]{:S(2)}) collective-permute-start(bf16[64,1024]{1,0:T(8,128)(2,1)S(1)} %shard_map.65), channel_id=1, source_target_pairs={{0,2},{1,3},{2,0},{3,1},{4,6},{5,7},{6,4},{7,5},{8,10},{9,11},{10,... | collective-permute-start | bytes 393224 | tf_op jit(solution)/shard_map/ppermute | solution.py:21
  40.5 4.1 %collective-permute-done.15.refs_2_ = bf16[64,1024]{1,0:T(8,128)(2,1)S(1)} collective-permute-done((bf16[64,1024]{1,0:T(8,128)(2,1)S(1)}, bf16[64,1024]{1,0:T(8,128)(2,1)S(1)}, u32[]{:S(2)}, u32[]{:S(2)}) %collective-permute-start.15) | collective-permute-done | bytes 131104 | tf_op jit(solution)/shard_map/ppermute | solution.py:21
  44.6 2.1 %collective-permute-start.16 = (bf16[64,1024]{1,0:T(8,128)(2,1)S(1)}, bf16[64,1024]{1,0:T(8,128)(2,1)S(1)}, u32[]{:S(2)}, u32[]{:S(2)}) collective-permute-start(bf16[64,1024]{1,0:T(8,128)(2,1)S(1)} %shard_map.66.mine), channel_id=1, source_target_pairs={{0,4},{1,5},{2,6},{3,7},{4,0},{5,1},{6,2},{7,3},{8,12},{9,13},{10,... | collective-permute-start | bytes 393224 | tf_op jit(solution)/shard_map/ppermute | solution.py:21
  46.7 1.2 %collective-permute-start.17 = (bf16[64,256]{1,0:T(8,128)(2,1)S(1)}, bf16[64,256]{1,0:T(8,128)(2,1)S(1)}, u32[]{:S(2)}, u32[]{:S(2)}) collective-permute-start(bf16[64,256]{1,0:T(8,128)(2,1)S(1)} %get-tuple-element.82), channel_id=1, source_target_pairs={{0,8},{8,0},{16,24},{24,16},{1,9},{9,1},{17,25},{25,17},{2,10},{10... | collective-permute-start | bytes 98312 | tf_op jit(solution)/shard_map/ppermute | solution.py:21
  48.0 0.8 %collective-permute-start.18 = (bf16[64,256]{1,0:T(8,128)(2,1)S(1)}, bf16[64,256]{1,0:T(8,128)(2,1)S(1)}, u32[]{:S(2)}, u32[]{:S(2)}) collective-permute-start(bf16[64,256]{1,0:T(8,128)(2,1)S(1)} %get-tuple-element.83), channel_id=1, source_target_pairs={{0,16},{8,24},{16,0},{24,8},{1,17},{9,25},{17,1},{25,9},{2,18},{10... | collective-permute-start | bytes 98312 | tf_op jit(solution)/shard_map/ppermute | solution.py:21
  48.8 1.5 %collective-permute-start.19 = (bf16[64,256]{1,0:T(8,128)(2,1)S(1)}, bf16[64,256]{1,0:T(8,128)(2,1)S(1)}, u32[]{:S(2)}, u32[]{:S(2)}) collective-permute-start(bf16[64,256]{1,0:T(8,128)(2,1)S(1)} %get-tuple-element.84), channel_id=1, source_target_pairs={{0,24},{8,16},{16,8},{24,0},{1,25},{9,17},{17,9},{25,1},{2,26},{10... | collective-permute-start | bytes 98312 | tf_op jit(solution)/shard_map/ppermute | solution.py:21
  50.2 0.6 collective-permute-done.17.refs_0_
  50.8 1.1 %collective-permute-done.18.refs_1_ = bf16[64,256]{1,0:T(8,128)(2,1)S(1)} collective-permute-done((bf16[64,256]{1,0:T(8,128)(2,1)S(1)}, bf16[64,256]{1,0:T(8,128)(2,1)S(1)}, u32[]{:S(2)}, u32[]{:S(2)}) %collective-permute-start.18) | collective-permute-done | bytes 32800 | tf_op jit(solution)/shard_map/ppermute | solution.py:21
  51.9 1.7 %collective-permute-done.19.refs_2_ = bf16[64,256]{1,0:T(8,128)(2,1)S(1)} collective-permute-done((bf16[64,256]{1,0:T(8,128)(2,1)S(1)}, bf16[64,256]{1,0:T(8,128)(2,1)S(1)}, u32[]{:S(2)}, u32[]{:S(2)}) %collective-permute-start.19) | collective-permute-done | bytes 32800 | tf_op jit(solution)/shard_map/ppermute | solution.py:21
  53.6 0.1 shard_map.68.refs_0_
  53.6 1.6 %collective-permute-start.21 = (bf16[64,1024]{1,0:T(8,128)(2,1)S(1)}, bf16[64,1024]{1,0:T(8,128)(2,1)S(1)}, u32[]{:S(2)}, u32[]{:S(2)}) collective-permute-start(bf16[64,1024]{1,0:T(8,128)(2,1)S(1)} %shard_map.68.refs_0_), channel_id=1, source_target_pairs={{0,2},{1,3},{2,0},{3,1},{4,6},{5,7},{6,4},{7,5},{8,10},{9,11},{10,... | collective-permute-start | bytes 393224 | tf_op jit(solution)/shard_map/ppermute | solution.py:21
  55.2 0.7 %shard_map.69 = f32[64,256]{1,0:T(8,128)} custom-call(f32[64,256]{1,0:T(8,128)S(1)} %get-tuple-element.87.item, f32[64,256]{1,0:T(8,128)S(1)} %get-tuple-element.88.own, bf16[64,256]{1,0:T(8,128)(2,1)S(1)} %collective-permute-done.17.refs_0_, bf16[64,256]{1,0:T(8,128)(2,1)S(1)} %collective-permute-done.18.refs_1_, ...), custom_call_target="tpu_custom_call" | custom-call | bytes 1048576 | tf_op jit(solution)/shard_map/pallas_call | solution.py:35
  55.9 2.8 %collective-permute-done.21.refs_2_ = bf16[64,1024]{1,0:T(8,128)(2,1)S(1)} collective-permute-done((bf16[64,1024]{1,0:T(8,128)(2,1)S(1)}, bf16[64,1024]{1,0:T(8,128)(2,1)S(1)}, u32[]{:S(2)}, u32[]{:S(2)}) %collective-permute-start.21) | collective-permute-done | bytes 131104 | tf_op jit(solution)/shard_map/ppermute | solution.py:21
  58.7 1.3 %collective-permute-done.22.refs_3_ = bf16[64,1024]{1,0:T(8,128)(2,1)S(1)} collective-permute-done((bf16[64,1024]{1,0:T(8,128)(2,1)S(1)}, bf16[64,1024]{1,0:T(8,128)(2,1)S(1)}, u32[]{:S(2)}, u32[]{:S(2)}) %collective-permute-start.22) | collective-permute-done | bytes 131104 | tf_op jit(solution)/shard_map/ppermute | solution.py:21
  60.0 1.1 %shard_map.70 = f32[64,4096]{1,0:T(8,128)} custom-call(f32[64,4096]{1,0:T(8,128)S(1)} %copy-done.1, bf16[64,1024]{1,0:T(8,128)(2,1)S(1)} %shard_map.68.refs_0_, bf16[64,1024]{1,0:T(8,128)(2,1)S(1)} %collective-permute-done.20.refs_1_, bf16[64,1024]{1,0:T(8,128)(2,1)S(1)} %collective-permute-done.21.refs_2_, bf16[64,1024]{1,0:T(8,128)(2,1)S(1)} %collective-permute-done.22.refs_3_), custom_call_target="tpu_custom_call" | custom-call | bytes 1048576 | tf_op jit(solution)/shard_map/pallas_call | solution.py:35
  (25 shorter events, 0.3 us)
Async XLA Ops:
  0.6 5.5 %copy-start = (bf16[1024,4096]{1,0:T(8,128)(2,1)S(1)}, bf16[1024,4096]{1,0:T(8,128)(2,1)}, u32[]{:S(2)}) copy-start(bf16[1024,4096]{1,0:T(8,128)(2,1)} %labels.15) | copy-start | bytes 25165828
  0.6 5.5 %copy-start.1 = (f32[64,4096]{1,0:T(8,128)S(1)}, f32[64,4096]{1,0:T(8,128)}, u32[]{:S(2)}) copy-start(f32[64,4096]{1,0:T(8,128)} %users.13) | copy-start | bytes 3145732
  0.6 7.5 %collective-permute-start = (f32[64,256]{1,0:T(8,128)}, f32[64,256]{1,0:T(8,128)S(1)}, u32[]{:S(2)}, u32[]{:S(2)}) collective-permute-start(f32[64,256]{1,0:T(8,128)} %items.1), channel_id=1, source_target_pairs={{0,8},{8,0},{16,24},{24,16},{1,9},{9,1},{17,25},{25,17},{2,10},{10... | collective-permute-start | bytes 196616 | tf_op jit(solution)/shard_map/ppermute | solution.py:21
  3.7 5.4 %collective-permute-start.2 = (f32[64,256]{1,0:T(8,128)}, f32[64,256]{1,0:T(8,128)S(1)}, u32[]{:S(2)}, u32[]{:S(2)}) collective-permute-start(f32[64,256]{1,0:T(8,128)} %items.1), channel_id=1, source_target_pairs={{0,24},{8,16},{16,8},{24,0},{1,25},{9,17},{17,9},{25,1},{2,26},{10... | collective-permute-start | bytes 196616 | tf_op jit(solution)/shard_map/ppermute | solution.py:21
  5.1 4.7 %collective-permute-start.1 = (f32[64,256]{1,0:T(8,128)}, f32[64,256]{1,0:T(8,128)S(1)}, u32[]{:S(2)}, u32[]{:S(2)}) collective-permute-start(f32[64,256]{1,0:T(8,128)} %items.1), channel_id=1, source_target_pairs={{0,16},{8,24},{16,0},{24,8},{1,17},{9,25},{17,1},{25,9},{2,18},{10... | collective-permute-start | bytes 196616 | tf_op jit(solution)/shard_map/ppermute | solution.py:21
  5.2 0.9 %copy-start.2 = (f32[64,256]{1,0:T(8,128)S(1)}, f32[64,256]{1,0:T(8,128)}, u32[]{:S(2)}) copy-start(f32[64,256]{1,0:T(8,128)} %items.1) | copy-start | bytes 196612
  11.3 1.6 %collective-permute-start.3 = (f32[64,1024]{1,0:T(8,128)S(1)}, f32[64,1024]{1,0:T(8,128)S(1)}, u32[]{:S(2)}, u32[]{:S(2)}) collective-permute-start(f32[64,1024]{1,0:T(8,128)S(1)} %get-tuple-element.54), channel_id=1, source_target_pairs={{0,1},{1,0},{2,3},{3,2},{4,5},{5,4},{6,7},{7,6},{8,9},{9,8},{10,11... | collective-permute-start | bytes 786440 | tf_op jit(solution)/shard_map/ppermute | solution.py:21
  12.9 5.8 %collective-permute-start.5 = (bf16[64,1024]{1,0:T(8,128)(2,1)S(1)}, bf16[64,1024]{1,0:T(8,128)(2,1)S(1)}, u32[]{:S(2)}, u32[]{:S(2)}) collective-permute-start(bf16[64,1024]{1,0:T(8,128)(2,1)S(1)} %shard_map.54), channel_id=1, source_target_pairs={{0,2},{1,3},{2,0},{3,1},{4,6},{5,7},{6,4},{7,5},{8,10},{9,11},{10,... | collective-permute-start | bytes 393224 | tf_op jit(solution)/shard_map/ppermute | solution.py:21
  15.9 2.8 %collective-permute-start.4 = (f32[64,1024]{1,0:T(8,128)S(1)}, f32[64,1024]{1,0:T(8,128)S(1)}, u32[]{:S(2)}, u32[]{:S(2)}) collective-permute-start(f32[64,1024]{1,0:T(8,128)S(1)} %get-tuple-element.59), channel_id=1, source_target_pairs={{0,1},{1,0},{2,3},{3,2},{4,5},{5,4},{6,7},{7,6},{8,9},{9,8},{10,11... | collective-permute-start | bytes 786440 | tf_op jit(solution)/shard_map/ppermute | solution.py:21
  18.7 8.7 %collective-permute-start.6 = (bf16[64,1024]{1,0:T(8,128)(2,1)S(1)}, bf16[64,1024]{1,0:T(8,128)(2,1)S(1)}, u32[]{:S(2)}, u32[]{:S(2)}) collective-permute-start(bf16[64,1024]{1,0:T(8,128)(2,1)S(1)} %shard_map.57.mine), channel_id=1, source_target_pairs={{0,4},{1,5},{2,6},{3,7},{4,0},{5,1},{6,2},{7,3},{8,12},{9,13},{10,... | collective-permute-start | bytes 393224 | tf_op jit(solution)/shard_map/ppermute | solution.py:21
  21.4 7.0 %collective-permute-start.9 = (bf16[64,1024]{1,0:T(8,128)(2,1)S(1)}, bf16[64,1024]{1,0:T(8,128)(2,1)S(1)}, u32[]{:S(2)}, u32[]{:S(2)}) collective-permute-start(bf16[64,1024]{1,0:T(8,128)(2,1)S(1)} %shard_map.58.refs_0_), channel_id=1, source_target_pairs={{0,24},{8,16},{16,8},{24,0},{1,25},{9,17},{17,9},{25,1},{2,26},{10... | collective-permute-start | bytes 393224 | tf_op jit(solution)/shard_map/ppermute | solution.py:21
  22.9 6.8 %collective-permute-start.8 = (bf16[64,1024]{1,0:T(8,128)(2,1)S(1)}, bf16[64,1024]{1,0:T(8,128)(2,1)S(1)}, u32[]{:S(2)}, u32[]{:S(2)}) collective-permute-start(bf16[64,1024]{1,0:T(8,128)(2,1)S(1)} %shard_map.58.refs_0_), channel_id=1, source_target_pairs={{0,16},{8,24},{16,0},{24,8},{1,17},{9,25},{17,1},{25,9},{2,18},{10... | collective-permute-start | bytes 393224 | tf_op jit(solution)/shard_map/ppermute | solution.py:21
  24.1 5.6 %collective-permute-start.7 = (bf16[64,1024]{1,0:T(8,128)(2,1)S(1)}, bf16[64,1024]{1,0:T(8,128)(2,1)S(1)}, u32[]{:S(2)}, u32[]{:S(2)}) collective-permute-start(bf16[64,1024]{1,0:T(8,128)(2,1)S(1)} %shard_map.58.refs_0_), channel_id=1, source_target_pairs={{0,8},{8,0},{16,24},{24,16},{1,9},{9,1},{17,25},{25,17},{2,10},{10... | collective-permute-start | bytes 393224 | tf_op jit(solution)/shard_map/ppermute | solution.py:21
  27.5 5.9 %collective-permute-start.12 = (bf16[64,1024]{1,0:T(8,128)(2,1)S(1)}, bf16[64,1024]{1,0:T(8,128)(2,1)S(1)}, u32[]{:S(2)}, u32[]{:S(2)}) collective-permute-start(bf16[64,1024]{1,0:T(8,128)(2,1)S(1)} %get-tuple-element.62.user), channel_id=1, source_target_pairs={{0,2},{1,3},{2,0},{3,1},{4,6},{5,7},{6,4},{7,5},{8,10},{9,11},{10,... | collective-permute-start | bytes 393224 | tf_op jit(solution)/shard_map/ppermute | solution.py:21
  28.2 3.4 %collective-permute-start.10 = (bf16[64,1024]{1,0:T(8,128)(2,1)S(1)}, bf16[64,1024]{1,0:T(8,128)(2,1)S(1)}, u32[]{:S(2)}, u32[]{:S(2)}) collective-permute-start(bf16[64,1024]{1,0:T(8,128)(2,1)S(1)} %get-tuple-element.62.user), channel_id=1, source_target_pairs={{0,1},{1,0},{2,3},{3,2},{4,5},{5,4},{6,7},{7,6},{8,9},{9,8},{10,11... | collective-permute-start | bytes 393224 | tf_op jit(solution)/shard_map/ppermute | solution.py:21
  33.4 1.8 %collective-permute-start.13 = (bf16[64,1024]{1,0:T(8,128)(2,1)S(1)}, bf16[64,1024]{1,0:T(8,128)(2,1)S(1)}, u32[]{:S(2)}, u32[]{:S(2)}) collective-permute-start(bf16[64,1024]{1,0:T(8,128)(2,1)S(1)} %collective-permute-done.12.user), channel_id=1, source_target_pairs={{0,1},{1,0},{2,3},{3,2},{4,5},{5,4},{6,7},{7,6},{8,9},{9,8},{10,11... | collective-permute-start | bytes 393224 | tf_op jit(solution)/shard_map/ppermute | solution.py:21
  37.0 1.7 %collective-permute-start.14 = (f32[64,1024]{1,0:T(8,128)S(1)}, f32[64,1024]{1,0:T(8,128)S(1)}, u32[]{:S(2)}, u32[]{:S(2)}) collective-permute-start(f32[64,1024]{1,0:T(8,128)S(1)} %get-tuple-element.75), channel_id=1, source_target_pairs={{0,1},{1,0},{2,3},{3,2},{4,5},{5,4},{6,7},{7,6},{8,9},{9,8},{10,11... | collective-permute-start | bytes 786440 | tf_op jit(solution)/shard_map/ppermute | solution.py:21
  37.6 2.9 %collective-permute-start.11 = (f32[64,1024]{1,0:T(8,128)S(1)}, f32[64,1024]{1,0:T(8,128)S(1)}, u32[]{:S(2)}, u32[]{:S(2)}) collective-permute-start(f32[64,1024]{1,0:T(8,128)S(1)} %get-tuple-element.69), channel_id=1, source_target_pairs={{0,1},{1,0},{2,3},{3,2},{4,5},{5,4},{6,7},{7,6},{8,9},{9,8},{10,11... | collective-permute-start | bytes 786440 | tf_op jit(solution)/shard_map/ppermute | solution.py:21
  38.8 5.8 %collective-permute-start.15 = (bf16[64,1024]{1,0:T(8,128)(2,1)S(1)}, bf16[64,1024]{1,0:T(8,128)(2,1)S(1)}, u32[]{:S(2)}, u32[]{:S(2)}) collective-permute-start(bf16[64,1024]{1,0:T(8,128)(2,1)S(1)} %shard_map.65), channel_id=1, source_target_pairs={{0,2},{1,3},{2,0},{3,1},{4,6},{5,7},{6,4},{7,5},{8,10},{9,11},{10,... | collective-permute-start | bytes 393224 | tf_op jit(solution)/shard_map/ppermute | solution.py:21
  44.6 8.9 %collective-permute-start.16 = (bf16[64,1024]{1,0:T(8,128)(2,1)S(1)}, bf16[64,1024]{1,0:T(8,128)(2,1)S(1)}, u32[]{:S(2)}, u32[]{:S(2)}) collective-permute-start(bf16[64,1024]{1,0:T(8,128)(2,1)S(1)} %shard_map.66.mine), channel_id=1, source_target_pairs={{0,4},{1,5},{2,6},{3,7},{4,0},{5,1},{6,2},{7,3},{8,12},{9,13},{10,... | collective-permute-start | bytes 393224 | tf_op jit(solution)/shard_map/ppermute | solution.py:21
  46.7 4.1 %collective-permute-start.17 = (bf16[64,256]{1,0:T(8,128)(2,1)S(1)}, bf16[64,256]{1,0:T(8,128)(2,1)S(1)}, u32[]{:S(2)}, u32[]{:S(2)}) collective-permute-start(bf16[64,256]{1,0:T(8,128)(2,1)S(1)} %get-tuple-element.82), channel_id=1, source_target_pairs={{0,8},{8,0},{16,24},{24,16},{1,9},{9,1},{17,25},{25,17},{2,10},{10... | collective-permute-start | bytes 98312 | tf_op jit(solution)/shard_map/ppermute | solution.py:21
  48.0 3.9 %collective-permute-start.18 = (bf16[64,256]{1,0:T(8,128)(2,1)S(1)}, bf16[64,256]{1,0:T(8,128)(2,1)S(1)}, u32[]{:S(2)}, u32[]{:S(2)}) collective-permute-start(bf16[64,256]{1,0:T(8,128)(2,1)S(1)} %get-tuple-element.83), channel_id=1, source_target_pairs={{0,16},{8,24},{16,0},{24,8},{1,17},{9,25},{17,1},{25,9},{2,18},{10... | collective-permute-start | bytes 98312 | tf_op jit(solution)/shard_map/ppermute | solution.py:21
  48.8 4.8 %collective-permute-start.19 = (bf16[64,256]{1,0:T(8,128)(2,1)S(1)}, bf16[64,256]{1,0:T(8,128)(2,1)S(1)}, u32[]{:S(2)}, u32[]{:S(2)}) collective-permute-start(bf16[64,256]{1,0:T(8,128)(2,1)S(1)} %get-tuple-element.84), channel_id=1, source_target_pairs={{0,24},{8,16},{16,8},{24,0},{1,25},{9,17},{17,9},{25,1},{2,26},{10... | collective-permute-start | bytes 98312 | tf_op jit(solution)/shard_map/ppermute | solution.py:21
  53.6 5.0 %collective-permute-start.21 = (bf16[64,1024]{1,0:T(8,128)(2,1)S(1)}, bf16[64,1024]{1,0:T(8,128)(2,1)S(1)}, u32[]{:S(2)}, u32[]{:S(2)}) collective-permute-start(bf16[64,1024]{1,0:T(8,128)(2,1)S(1)} %shard_map.68.refs_0_), channel_id=1, source_target_pairs={{0,2},{1,3},{2,0},{3,1},{4,6},{5,7},{6,4},{7,5},{8,10},{9,11},{10,... | collective-permute-start | bytes 393224 | tf_op jit(solution)/shard_map/ppermute | solution.py:21
  55.2 3.5 %collective-permute-start.20 = (bf16[64,1024]{1,0:T(8,128)(2,1)S(1)}, bf16[64,1024]{1,0:T(8,128)(2,1)S(1)}, u32[]{:S(2)}, u32[]{:S(2)}) collective-permute-start(bf16[64,1024]{1,0:T(8,128)(2,1)S(1)} %shard_map.68.refs_0_), channel_id=1, source_target_pairs={{0,1},{1,0},{2,3},{3,2},{4,5},{5,4},{6,7},{7,6},{8,9},{9,8},{10,11... | collective-permute-start | bytes 393224 | tf_op jit(solution)/shard_map/ppermute | solution.py:21
  58.7 1.3 %collective-permute-start.22 = (bf16[64,1024]{1,0:T(8,128)(2,1)S(1)}, bf16[64,1024]{1,0:T(8,128)(2,1)S(1)}, u32[]{:S(2)}, u32[]{:S(2)}) collective-permute-start(bf16[64,1024]{1,0:T(8,128)(2,1)S(1)} %collective-permute-done.21.refs_2_), channel_id=1, source_target_pairs={{0,1},{1,0},{2,3},{3,2},{4,5},{5,4},{6,7},{7,6},{8,9},{9,8},{10,11... | collective-permute-start | bytes 393224 | tf_op jit(solution)/shard_map/ppermute | solution.py:21
